TPU v7x, 32 devices: a whole 2x2x4 slice. The times are simulated.
32 devices in a mesh: img: 16 (over z, x, core), seq: 2 (over y).
Axes of the slice: x: 2, y: 2, z: 4, core: 2. Of those that a mesh axis runs over, the one named last changes fastest.
Arguments:
- tokens: bfloat16 [32, 656, 768], P('img', 'seq'), may hold values from -6 to 6
- token_mask: int32 [32, 656], P('img', 'seq'), may hold values from 0 to 1, as said below
- ln1_gain: bfloat16 [768], P('img'), may hold values from 0.25 to 1.75
- ln1_bias: bfloat16 [768], P('img'), may hold values from -1.75 to 1.75
- w_qkv: bfloat16 [768, 2304], P('img'), may hold values from -0.21875 to 0.21875
- bias_q: bfloat16 [768], P('img'), may hold values from -1.75 to 1.75
- bias_v: bfloat16 [768], P('img'), may hold values from -1.75 to 1.75
- w_out: bfloat16 [768, 768], P('img'), may hold values from -3 to 3
- bias_out: bfloat16 [768], P('img'), may hold values from -1.75 to 1.75
- ln2_gain: bfloat16 [768], P('img'), may hold values from 0.25 to 1.75
- ln2_bias: bfloat16 [768], P('img'), may hold values from -1.75 to 1.75
- w_up: bfloat16 [768, 3072], P('img'), may hold values from -0.21875 to 0.21875
- bias_up: bfloat16 [3072], P('img'), may hold values from -1.75 to 1.75
- w_down: bfloat16 [3072, 768], P('img'), may hold values from -0.109375 to 0.109375
- bias_down: bfloat16 [768], P('img'), may hold values from -1.75 to 1.75
- cotangent: bfloat16 [32, 656, 768], P('img', 'seq'), may hold values from -8 to 8
Outputs:
- output: float32 [32, 656, 768], P('img', 'seq')
- input_grad: float32 [32, 656, 768], P('img', 'seq')
- grad_ln1_gain: float32 [768], P('img')
- grad_ln1_bias: float32 [768], P('img')
- grad_w_qkv: float32 [768, 2304], P('img')
- grad_bias_q: float32 [768], P('img')
- grad_bias_v: float32 [768], P('img')
- grad_w_out: float32 [768, 768], P('img')
- grad_bias_out: float32 [768], P('img')
- grad_ln2_gain: float32 [768], P('img')
- grad_ln2_bias: float32 [768], P('img')
- grad_w_up: float32 [768, 3072], P('img')
- grad_bias_up: float32 [3072], P('img')
- grad_w_down: float32 [3072, 768], P('img')
- grad_bias_down: float32 [768], P('img')
Inputs may be any that keep to these rules, and one draw needn't show every extreme that they name: `token_mask`: each image has between 492 and 655 real tokens, spread over its 2 blocks of 328 rows as evenly as possible, the earlier blocks taking the extra ones; in every block the real tokens come first.
All inputs are finite; a program needn't handle non-finite values.
Results may differ from a plain program's by a relative error of at most 0.01.
Values may be sent and summed in bfloat16 or wider, within the bound.
No kernel may reach another device: no remote copies, remote signals or barrier semaphores. Data moves between devices by JAX's collectives and lax.ppermute only.
A program may use at most 128 MiB of HBM per device.

v0:
```python
import jax
import jax.numpy as jnp
from jax import lax
from jax.sharding import PartitionSpec as P

HEADS = 12


epsilon = 1e-06


def layer_norm(values, gain, shift):
    center = jnp.mean(values, axis=-1, keepdims=True)
    offset = values - center
    spread = jnp.mean(offset * offset, axis=-1, keepdims=True)
    return offset * lax.rsqrt(spread + epsilon) * gain + shift


def gelu_exact(pre_value):
    return jax.nn.gelu(pre_value, approximate=False)


def split_heads(tensor, head_count):
    images, row_count, columns = tensor.shape
    head_size = columns // head_count
    moved = tensor.reshape(images, row_count, head_count, head_size).transpose(0, 2, 1, 3)
    return moved.reshape(images * head_count, row_count, head_size)


def join_heads(tensor, images):
    combined, row_count, head_size = tensor.shape
    heads_here = combined // images
    moved = tensor.reshape(images, heads_here, row_count, head_size).transpose(0, 2, 1, 3)
    return moved.reshape(images, row_count, heads_here * head_size)


def attend_forward(query_head, key_head, value_head, key_mask):
    scaling = query_head.shape[-1] ** (-0.5)
    row_count = query_head.shape[0]
    blocks = max(1, 2 * row_count // key_head.shape[0])

    def one_block(query_block):
        scores = (
            jnp.einsum("qd,kd->qk", query_block, key_head, preferred_element_type=jnp.float32)
            * scaling
        )
        scores = jnp.where(key_mask[None, :] > 0.5, scores, -1000000000.0)
        highest = jnp.max(scores, axis=-1, keepdims=True)
        weights = jnp.exp(scores - highest)
        totals = jnp.sum(weights, axis=-1, keepdims=True)
        mixed = jnp.dot(
            (weights / totals).astype(jnp.bfloat16), value_head, preferred_element_type=jnp.float32
        )
        return (mixed, (highest + jnp.log(totals))[:, 0])

    mixed, log_sums = lax.map(one_block, query_head.reshape(blocks, row_count // blocks, -1))
    return (mixed.reshape(row_count, -1), log_sums.reshape(row_count))


def attend_backward(query_head, key_head, value_head, key_mask, log_sums, out_grad):
    scaling = query_head.shape[-1] ** (-0.5)
    row_count = query_head.shape[0]
    blocks = max(1, 2 * row_count // key_head.shape[0])
    block_rows = row_count // blocks

    def one_block(carry, pieces):
        key_grad, value_grad = carry
        query_block, log_block, grad_block = pieces
        scores = (
            jnp.einsum("qd,kd->qk", query_block, key_head, preferred_element_type=jnp.float32)
            * scaling
        )
        scores = jnp.where(key_mask[None, :] > 0.5, scores, -1000000000.0)
        weights = jnp.exp(scores - log_block[:, None])
        value_grad = value_grad + jnp.einsum(
            "qk,qd->kd",
            weights.astype(jnp.bfloat16),
            grad_block,
            preferred_element_type=jnp.float32,
        )
        weight_grad = jnp.einsum(
            "qd,kd->qk", grad_block, value_head, preferred_element_type=jnp.float32
        )
        centered = jnp.sum(weights * weight_grad, axis=-1, keepdims=True)
        score_grad = (weights * (weight_grad - centered)).astype(jnp.bfloat16)
        query_grad = jnp.dot(score_grad, key_head, preferred_element_type=jnp.float32) * scaling
        key_grad = (
            key_grad
            + jnp.einsum("qk,qd->kd", score_grad, query_block, preferred_element_type=jnp.float32)
            * scaling
        )
        return ((key_grad, value_grad), query_grad)

    zeros_init = jnp.zeros(key_head.shape, jnp.float32)
    (key_grad, value_grad), query_grad = lax.scan(
        one_block,
        (zeros_init, zeros_init),
        (
            query_head.reshape(blocks, block_rows, -1),
            log_sums.reshape(blocks, block_rows),
            out_grad.reshape(blocks, block_rows, -1),
        ),
    )
    return (query_grad.reshape(row_count, -1), key_grad, value_grad)


def heads_forward(query_heads, key_heads, value_heads, key_masks):
    return lax.map(
        lambda pieces: attend_forward(pieces[0], pieces[1], pieces[2], pieces[3]),
        (query_heads, key_heads, value_heads, key_masks),
    )


def heads_backward(query_heads, key_heads, value_heads, key_masks, log_sums, out_grads):
    return lax.map(
        lambda pieces: attend_backward(
            pieces[0], pieces[1], pieces[2], pieces[3], pieces[4], pieces[5]
        ),
        (query_heads, key_heads, value_heads, key_masks, log_sums, out_grads),
    )


def column_sum(tensor):
    return jnp.sum(tensor.astype(jnp.float32), axis=(0, 1))


def body(
    tokens,
    token_mask,
    ln1_gain,
    ln1_bias,
    w_qkv,
    bias_q,
    bias_v,
    w_out,
    bias_out,
    ln2_gain,
    ln2_bias,
    w_up,
    bias_up,
    w_down,
    bias_down,
    cotangent,
):
    (
        gain_one,
        shift_one,
        qkv_full,
        query_bias,
        value_bias,
        out_full,
        out_bias,
        gain_two,
        shift_two,
        up_full,
        up_bias,
        down_full,
        down_bias,
    ) = (
        lax.all_gather(ln1_gain, "img", axis=0, tiled=True),
        lax.all_gather(ln1_bias, "img", axis=0, tiled=True),
        lax.all_gather(w_qkv, "img", axis=0, tiled=True),
        lax.all_gather(bias_q, "img", axis=0, tiled=True),
        lax.all_gather(bias_v, "img", axis=0, tiled=True),
        lax.all_gather(w_out, "img", axis=0, tiled=True),
        lax.all_gather(bias_out, "img", axis=0, tiled=True),
        lax.all_gather(ln2_gain, "img", axis=0, tiled=True),
        lax.all_gather(ln2_bias, "img", axis=0, tiled=True),
        lax.all_gather(w_up, "img", axis=0, tiled=True),
        lax.all_gather(bias_up, "img", axis=0, tiled=True),
        lax.all_gather(w_down, "img", axis=0, tiled=True),
        lax.all_gather(bias_down, "img", axis=0, tiled=True),
    )
    images, shard_rows, model_dim = tokens.shape
    seq_parts = lax.axis_size("seq")
    inputs = tokens.astype(jnp.float32)
    mask_float = token_mask.astype(jnp.float32)
    normed, norm_one_pull = jax.vjp(
        layer_norm, inputs, gain_one.astype(jnp.float32), shift_one.astype(jnp.float32)
    )
    normed_low = normed.astype(jnp.bfloat16)
    projected = jnp.einsum("bsd,de->bse", normed_low, qkv_full, preferred_element_type=jnp.float32)
    query_tok = (projected[..., :model_dim] + query_bias.astype(jnp.float32)).astype(jnp.bfloat16)
    key_tok = projected[..., model_dim : 2 * model_dim].astype(jnp.bfloat16)
    value_tok = (projected[..., 2 * model_dim :] + value_bias.astype(jnp.float32)).astype(
        jnp.bfloat16
    )
    mask_low = token_mask.astype(jnp.bfloat16)
    local_heads = HEADS // seq_parts
    stacked = jnp.stack([query_tok, key_tok, value_tok], axis=2)
    mask_tile = jnp.broadcast_to(mask_low[:, :, None, None], (images, shard_rows, 1, seq_parts))
    stacked_heads, mask_heads = (
        lax.all_to_all(stacked, "seq", split_axis=3, concat_axis=1, tiled=True),
        lax.all_to_all(mask_tile, "seq", split_axis=3, concat_axis=1, tiled=True),
    )
    query_heads = split_heads(stacked_heads[:, :, 0], local_heads)
    key_heads = split_heads(stacked_heads[:, :, 1], local_heads)
    value_heads = split_heads(stacked_heads[:, :, 2], local_heads)
    key_masks = jnp.repeat(mask_heads[:, :, 0, 0].astype(jnp.float32), local_heads, axis=0)
    attended, log_sums = heads_forward(query_heads, key_heads, value_heads, key_masks)
    merged_heads = join_heads(attended, images).astype(jnp.bfloat16)
    merged = lax.all_to_all(merged_heads, "seq", split_axis=1, concat_axis=2, tiled=True)
    branch = jnp.einsum(
        "bsd,de->bse", merged, out_full, preferred_element_type=jnp.float32
    ) + out_bias.astype(jnp.float32)
    middle = inputs + branch
    second, norm_two_pull = jax.vjp(
        layer_norm, middle, gain_two.astype(jnp.float32), shift_two.astype(jnp.float32)
    )
    second_low = second.astype(jnp.bfloat16)
    pre_act = jnp.einsum(
        "bsd,df->bsf", second_low, up_full, preferred_element_type=jnp.float32
    ) + up_bias.astype(jnp.float32)
    hidden, gelu_pull = jax.vjp(gelu_exact, pre_act)
    hidden_low = hidden.astype(jnp.bfloat16)
    output = (
        middle
        + jnp.einsum("bsf,fd->bsd", hidden_low, down_full, preferred_element_type=jnp.float32)
        + down_bias.astype(jnp.float32)
    )
    upstream = cotangent.astype(jnp.float32) * mask_float[..., None]
    down_in = upstream.astype(jnp.bfloat16)
    grad_down = jnp.einsum("bsf,bsd->fd", hidden_low, down_in, preferred_element_type=jnp.float32)
    grad_down_bias = column_sum(down_in)
    hidden_grad = jnp.einsum("bsd,fd->bsf", down_in, down_full, preferred_element_type=jnp.float32)
    pre_grad = gelu_pull(hidden_grad)[0].astype(jnp.bfloat16)
    grad_up = jnp.einsum("bsd,bsf->df", second_low, pre_grad, preferred_element_type=jnp.float32)
    grad_up_bias = column_sum(pre_grad)
    second_grad = jnp.einsum("bsf,df->bsd", pre_grad, up_full, preferred_element_type=jnp.float32)
    middle_ln_grad, grad_gain_two, grad_shift_two = norm_two_pull(second_grad)
    middle_grad = upstream + middle_ln_grad
    branch_grad = middle_grad.astype(jnp.bfloat16)
    grad_out = jnp.einsum("bsd,bse->de", merged, branch_grad, preferred_element_type=jnp.float32)
    grad_out_bias = column_sum(branch_grad)
    merged_grad = jnp.einsum(
        "bse,de->bsd", branch_grad, out_full, preferred_element_type=jnp.float32
    ).astype(jnp.bfloat16)
    grad_heads_in = lax.all_to_all(merged_grad, "seq", split_axis=2, concat_axis=1, tiled=True)
    query_grad, key_grad, value_grad = heads_backward(
        query_heads,
        key_heads,
        value_heads,
        key_masks,
        log_sums,
        split_heads(grad_heads_in, local_heads),
    )
    triple = jnp.stack(
        [
            join_heads(query_grad, images),
            join_heads(key_grad, images),
            join_heads(value_grad, images),
        ],
        axis=2,
    ).astype(jnp.bfloat16)
    qkv_grad = lax.all_to_all(triple, "seq", split_axis=1, concat_axis=3, tiled=True)
    qkv_flat = qkv_grad.reshape(images, shard_rows, 3 * model_dim)
    grad_qkv = jnp.einsum("bsd,bse->de", normed_low, qkv_flat, preferred_element_type=jnp.float32)
    grad_query_bias = column_sum(qkv_grad[:, :, 0])
    grad_value_bias = column_sum(qkv_grad[:, :, 2])
    normed_grad = jnp.einsum("bse,de->bsd", qkv_flat, qkv_full, preferred_element_type=jnp.float32)
    input_ln_grad, grad_gain_one, grad_shift_one = norm_one_pull(normed_grad)
    input_grad = middle_grad + input_ln_grad
    shards_all = (
        lax.psum_scatter(grad_gain_one, "img", scatter_dimension=0, tiled=True),
        lax.psum_scatter(grad_shift_one, "img", scatter_dimension=0, tiled=True),
        lax.psum_scatter(grad_qkv, "img", scatter_dimension=0, tiled=True),
        lax.psum_scatter(grad_query_bias, "img", scatter_dimension=0, tiled=True),
        lax.psum_scatter(grad_value_bias, "img", scatter_dimension=0, tiled=True),
        lax.psum_scatter(grad_out, "img", scatter_dimension=0, tiled=True),
        lax.psum_scatter(grad_out_bias, "img", scatter_dimension=0, tiled=True),
        lax.psum_scatter(grad_gain_two, "img", scatter_dimension=0, tiled=True),
        lax.psum_scatter(grad_shift_two, "img", scatter_dimension=0, tiled=True),
        lax.psum_scatter(grad_up, "img", scatter_dimension=0, tiled=True),
        lax.psum_scatter(grad_up_bias, "img", scatter_dimension=0, tiled=True),
        lax.psum_scatter(grad_down, "img", scatter_dimension=0, tiled=True),
        lax.psum_scatter(grad_down_bias, "img", scatter_dimension=0, tiled=True),
    )
    summed_all = lax.psum(
        (
            shards_all[0],
            shards_all[1],
            shards_all[2],
            shards_all[3],
            shards_all[4],
            shards_all[5],
            shards_all[6],
            shards_all[7],
            shards_all[8],
            shards_all[9],
            shards_all[10],
            shards_all[11],
            shards_all[12],
        ),
        "seq",
    )
    return (
        output,
        input_grad,
        summed_all[0],
        summed_all[1],
        summed_all[2],
        summed_all[3],
        summed_all[4],
        summed_all[5],
        summed_all[6],
        summed_all[7],
        summed_all[8],
        summed_all[9],
        summed_all[10],
        summed_all[11],
        summed_all[12],
    )


def solution(mesh):
    in_specs = (
        P("img", "seq", None),
        P("img", "seq"),
        P("img"),
        P("img"),
        P("img", None),
        P("img"),
        P("img"),
        P("img", None),
        P("img"),
        P("img"),
        P("img"),
        P("img", None),
        P("img"),
        P("img", None),
        P("img"),
        P("img", "seq", None),
    )
    out_specs = (
        P("img", "seq", None),
        P("img", "seq", None),
        P("img"),
        P("img"),
        P("img", None),
        P("img"),
        P("img"),
        P("img", None),
        P("img"),
        P("img"),
        P("img"),
        P("img", None),
        P("img"),
        P("img", None),
        P("img"),
    )
    return jax.shard_map(body, mesh=mesh, in_specs=in_specs, out_specs=out_specs, check_vma=False)
```

profile of v0, /device:TPU:0, one launch (start us, length us, event | category | flops | bytes accessed | tf_op | source)
XLA Modules:
  0.0 952.0 jit_solution(4960267484112274725)
XLA Ops:
  10.8 4.2 all-to-all-start.1
  25.2 62.3 %all-reduce.21 = (bf16[768]{0:T(1024)(128)(2,1)S(1)}, bf16[768]{0:T(1024)(128)(2,1)S(1)}, bf16[768]{0:T(1024)(128)(2,1)S(1)}, bf16[768]{0:T(1024)(128)(2,1)S(1)}...) all-reduce(bf16[768]{0:T(1024)(128)(2,1)S(1)} %dynamic-update-slice, ...), channel_id=1, replica_groups=mesh['img'=16,'seq'=2] {'img'}, use_global_device_ids=true, to_apply=%add.1 | all-reduce | flops 9216 | bytes 36864
  89.5 4.8 fusion.42
  96.8 11.9 %copy.86 = bf16[2,328,3,768]{1,0,2,3:T(2,128)(2,1)} copy(bf16[2,328,3,768]{3,1,0,2:T(8,128)(2,1)} %pad_maximum_fusion.1) | data formatting | bytes 6045696 | tf_op jit(solution)/shard_map/stack | solution.py:190
  108.8 5.3 all-to-all-start
  114.8 35.8 %all-to-all-done = bf16[2,328,3,768]{1,0,2,3:T(2,128)(2,1)} async-done(((bf16[2,328,3,768]{1,0,2,3:T(2,128)(2,1)}), bf16[2,328,3,768]{1,0,2,3:T(2,128)(2,1)}, u32[]{:S(2)}, u32[]{:S(2)}) %all-to-all-start) | async-done | bytes 3022880 | tf_op jit(solution)/shard_map/all_to_all | solution.py:193
  150.6 11.9 %copy.88 = bf16[2,2,328,3,384]{4,2,1,3,0:T(8,128)(2,1)} copy(bf16[2,2,328,3,384]{2,0,3,4,1:T(2,128)(2,1)} %bitcast.20) | data formatting | bytes 6045696 | tf_op jit(solution)/shard_map/all_to_all | solution.py:193
  162.5 3.5 fusion.82
  178.2 66.7 %while.54 = (s32[]{:T(128)}, bf16[12,656,64]{2,1,0:T(8,128)(2,1)}, f32[12,656]{1,0:T(8,128)S(1)}, bf16[12,656,64]{2,1,0:T(8,128)(2,1)}, bf16[12,656,64]{2,1,0:T(...) while((s32[]{:T(128)}, bf16[12,656,64]{2,1,0:T(8,128)(2,1)}, ...), condition=%wide.region_7.8_spmd, body=%wide.region_2.7_spmd.sunk | while | flops 56804680 | bytes 4194502 | solution.py:108
  250.4 3.8 all-to-all-start.2
  254.3 9.1 all-to-all-done.2
  267.7 8.5 fusion.61
  276.2 3.2 copy-done.5
  279.4 20.4 %multiply_convert_fusion.1 = (bf16[2,328,3072]{2,1,0:T(8,128)(2,1)}, f32[2,328,3072]{2,1,0:T(8,128)}) fusion(f32[2,328,3072]{2,1,0:T(8,128)S(1)} %get-tuple-element.434, f32[3072]{0:T(1024)S(1)} %convert_element_type.139, u8[328,3072]{1,0:T(8,128)(4,1)S(1)} %get-tuple-element.299, u8[328,3072]{1,0:T(8,128)(4,1)S(1)} %get-tuple-element.298), kind=kLoop, calls=%fused_computation.63 | loop fusion | flops 143081472 | bytes 22179840 | tf_op jit(solution)/shard_map/convert_element_type | solution.py:215
  299.8 11.1 %convert_reduce_fusion = (f32[3072]{0:T(1024)}, bf16[2,328,3072]{2,1,0:T(8,128)(2,1)S(1)}) fusion(f32[2,328,3072]{2,1,0:T(8,128)} %get-tuple-element.413, bf16[3072,768]{1,0:T(8,128)(2,1)} %all-gather.11.cloned.1.call-done, bf16[2,328,768]{2,1,0:T(8,128)(2,1)S(1)} %copy-done.8, f32[2,328]{1,0:T(2,128)S(1)} %get-tuple-element.428, ...), kind=kOutput, calls=%fused_computation.61 | convolution fusion | flops 3131163648 | bytes 25905728 | tf_op jit(solution)/shard_map/bsd,fd->bsf/dot_general | solution.py:225
  310.9 8.1 multiply_reduce_fusion.1
  323.2 2.8 copy.100
  326.0 3.6 all-to-all-start.3
  332.4 7.4 all-to-all-done.3
  344.4 114.3 %while.56 = (s32[]{:T(128)}, bf16[12,656,64]{2,1,0:T(8,128)(2,1)}, bf16[12,656,64]{1,2,0:T(8,128)(2,1)}, bf16[12,656,64]{1,2,0:T(8,128)(2,1)}, bf16[12,656,64]{2...) while((s32[]{:T(128)}, bf16[12,656,64]{2,1,0:T(8,128)(2,1)}, ...), condition=%wide.region_16.17_spmd, body=%wide.region_12.16_spmd.sunk | while | flops 139875264 | bytes 10565997 | solution.py:115
  348.5 3.9 while.58
  358.0 3.9 while.58
  367.6 3.9 while.58
  377.2 3.9 while.58
  386.7 3.9 while.58
  396.2 3.9 while.58
  405.7 3.9 while.58
  415.3 3.9 while.58
  424.8 3.9 while.58
  434.3 3.9 while.58
  443.8 3.9 while.58
  453.3 3.9 while.58
  458.8 3.7 copy.108
  464.7 8.2 copy.109
  472.9 31.5 %all_to_all.78 = bf16[2,656,3,384]{3,0,2,1:T(2,128)(2,1)S(1)} all-to-all(bf16[2,656,3,384]{3,0,2,1:T(2,128)(2,1)} %copy.109), channel_id=1, replica_groups=mesh['img'=16,'seq'=2] {'seq'}, dimensions={1} | all-to-all | bytes 6045696 | tf_op jit(solution)/shard_map/all_to_all | solution.py:255
  504.8 4.0 copy.111
  508.7 7.7 reshape.214
  516.4 8.2 convolution_bitcast_fusion.3
  524.9 10.5 %convolution_bitcast_fusion.2 = f32[768,3072]{1,0:T(8,128)} fusion(bf16[2,328,3072]{2,1,0:T(8,128)(2,1)} %copy-done.7, f32[2,328,768]{2,1,0:T(8,128)} %copy-done.2, f32[768]{0:T(1024)S(1)} %convert_element_type.137, f32[768]{0:T(1024)S(1)} %convert_element_type.136, f32[2,328]{1,0:T(2,128)S(1)} %fusion.76, f32[2,328]{1,0:T(2,128)S(1)} %broadcast_multiply_fusion), kind=kOutput, calls=%fused_computation.77 | convolution fusion | flops 3097915392 | bytes 15494272 | tf_op jit(solution)/shard_map/bsd,bsf->df/dot_general | solution.py:227
  536.1 10.0 %convolution_bitcast_fusion.1 = f32[3072,768]{1,0:T(8,128)} fusion(bf16[2,328,3072]{2,1,0:T(8,128)(2,1)} %get-tuple-element.412, bf16[2,328,768]{2,1,0:T(8,128)(2,1)} %param.39, f32[2,328]{1,0:T(2,128)S(1)} %copy-done.22), kind=kOutput, calls=%fused_computation.76 | convolution fusion | flops 3096907776 | bytes 14477888 | tf_op jit(solution)/shard_map/bsf,bsd->fd/dot_general | solution.py:223
  547.8 9.6 %add_add_fusion.4 = f32[2,328,768]{2,1,0:T(8,128)} fusion(f32[2,328,768]{2,1,0:T(8,128)} %copy-done.2, bf16[2,328,3072]{2,1,0:T(8,128)(2,1)} %get-tuple-element.412, bf16[3072,768]{1,0:T(8,128)(2,1)} %all-gather.11.cloned.1.call-done, f32[768]{0:T(1024)S(1)} %convert_element_type.141), kind=kOutput, calls=%fused_computation.124 | convolution fusion | flops 3096403968 | bytes 12782592 | tf_op jit(solution)/shard_map/bsf,fd->bsd/dot_general | solution.py:218
  558.1 72.0 %reduce-scatter.5.cloned.1.call-done = f32[48,2304]{1,0:T(8,128)} async-done(((f32[768,2304]{1,0:T(8,128)}), f32[48,2304]{1,0:T(8,128)}) %reduce-scatter.5.cloned.1.call-update) | async-done | bytes 442384 | tf_op jit(solution)/shard_map/reduce_scatter | solution.py:266
  630.1 115.0 %reduce-scatter.9.cloned.1.call-done = f32[48,3072]{1,0:T(8,128)} async-done(((f32[768,3072]{1,0:T(8,128)}), f32[48,3072]{1,0:T(8,128)}) %reduce-scatter.9.cloned.1.call-update) | async-done | bytes 589840 | tf_op jit(solution)/shard_map/reduce_scatter | solution.py:273
  745.0 115.8 %reduce-scatter.11.cloned.1.call-done = f32[192,768]{1,0:T(8,128)} async-done(((f32[3072,768]{1,0:T(8,128)}), f32[192,768]{1,0:T(8,128)}) %reduce-scatter.11.cloned.1.call-update) | async-done | bytes 589840 | tf_op jit(solution)/shard_map/reduce_scatter | solution.py:275
  860.9 5.7 fusion.77
  868.9 60.4 %all-reduce.18 = (f32[768]{0:T(1024)S(1)}, f32[768]{0:T(1024)S(1)}, f32[768]{0:T(1024)S(1)}, f32[768]{0:T(1024)S(1)}, f32[768]{0:T(1024)S(1)}, /*index=5*/f32[76...) all-reduce(f32[768]{0:T(1024)S(1)} %get-tuple-element.302, ...), channel_id=2, replica_groups=mesh['img'=16,'seq'=2] {'img'}, use_global_device_ids=true, to_apply=%region_20.21.clone | all-reduce | flops 9216 | bytes 73728
  929.9 5.6 all-reduce.19
  935.5 3.4 add_add_fusion.2
  (825 shorter events, 271.9 us)
Async XLA Ops:
  7.2 81.8 %copy-start = (bf16[2,328,768]{2,1,0:T(8,128)(2,1)S(1)}, bf16[2,328,768]{2,1,0:T(8,128)(2,1)}, u32[]{:S(2)}) copy-start(bf16[2,328,768]{2,1,0:T(8,128)(2,1)} %param.24) | copy-start | bytes 3022852
  7.2 82.3 %all-gather.5.cloned.1.call-start = ((), (), s32[]{:S(2)}) async-start(), calls=%async_computation.9 | async-start | bytes 3760128 | tf_op jit(solution)/shard_map/all_gather | solution.py:162
  7.9 256.7 %all-gather.7.cloned.1.call-start = ((), (), s32[]{:S(2)}) async-start(), calls=%async_computation.10 | async-start | bytes 1253376 | tf_op jit(solution)/shard_map/all_gather | solution.py:165
  8.7 259.0 %all-gather.9.cloned.1.call-start = ((), (), s32[]{:S(2)}) async-start(), calls=%async_computation.11 | async-start | bytes 5013504 | tf_op jit(solution)/shard_map/all_gather | solution.py:169
  10.2 309.7 %copy-start.21 = (f32[2,328]{1,0:T(2,128)}, f32[2,328]{1,0:T(2,128)S(1)}, u32[]{:S(2)}) copy-start(f32[2,328]{1,0:T(2,128)S(1)} %get-tuple-element.428) | copy-start | bytes 7876
  10.8 98.0 %all-to-all-start.1 = ((bf16[2,328,1,2]{1,0,2,3:T(2,128)(2,1)}), bf16[2,328,1,2]{1,0,2,3:T(2,128)(2,1)S(1)}, u32[]{:S(2)}, u32[]{:S(2)}) async-start(bf16[2,328,1,2]{1,0,2,3:T(2,128)(2,1)} %broadcast_in_dim.91), calls=%async_computation.1 | async-start | bytes 6144 | tf_op jit(solution)/shard_map/all_to_all | solution.py:194
  87.5 6.8 copy-start.11
  87.5 6.8 copy-start.17
  88.9 5.3 copy-start.13
  89.4 4.9 copy-start.23
  89.4 4.9 copy-start.15
  108.8 41.9 %all-to-all-start = ((bf16[2,328,3,768]{1,0,2,3:T(2,128)(2,1)}), bf16[2,328,3,768]{1,0,2,3:T(2,128)(2,1)}, u32[]{:S(2)}, u32[]{:S(2)}) async-start(bf16[2,328,3,768]{1,0,2,3:T(2,128)(2,1)} %copy.86), calls=%async_computation | async-start | bytes 7077888 | tf_op jit(solution)/shard_map/all_to_all | solution.py:193
  114.1 185.7 %all-gather.11.cloned.1.call-start = ((), (), s32[]{:S(2)}) async-start(), calls=%async_computation.12 | async-start | bytes 5013504 | tf_op jit(solution)/shard_map/all_gather | solution.py:171
  250.4 12.9 %all-to-all-start.2 = ((bf16[2,656,384]{2,0,1:T(2,128)(2,1)}), bf16[2,656,384]{2,0,1:T(2,128)(2,1)S(1)}, u32[]{:S(2)}, u32[]{:S(2)}) async-start(bf16[2,656,384]{2,0,1:T(2,128)(2,1)} %copy.97), calls=%async_computation.2 | async-start | bytes 2015232 | tf_op jit(solution)/shard_map/all_to_all | solution.py:202
  267.3 51.8 %copy-start.2 = (f32[2,328,768]{2,1,0:T(8,128)}, f32[2,328,768]{2,1,0:T(8,128)S(1)}, u32[]{:S(2)}) copy-start(f32[2,328,768]{2,1,0:T(8,128)S(1)} %get-tuple-element.433) | copy-start | bytes 6045700
  276.2 3.2 copy-start.5
  279.4 20.4 %copy-start.8 = (bf16[2,328,768]{2,1,0:T(8,128)(2,1)S(1)}, bf16[2,328,768]{2,1,0:T(8,128)(2,1)}, u32[]{:S(2)}) copy-start(bf16[2,328,768]{2,1,0:T(8,128)(2,1)} %param.39) | copy-start | bytes 3022852
  310.9 8.1 copy-start.7
  319.8 1.2 copy-start.3
  319.8 2.4 copy-start.31
  319.9 3.3 copy-start.19
  323.2 6.5 copy-start.9
  326.0 13.7 %all-to-all-start.3 = ((bf16[2,328,768]{1,0,2:T(2,128)(2,1)}), bf16[2,328,768]{1,0,2:T(2,128)(2,1)S(1)}, u32[]{:S(2)}, u32[]{:S(2)}) async-start(bf16[2,328,768]{1,0,2:T(2,128)(2,1)} %copy.100), calls=%async_computation.3 | async-start | bytes 2359296 | tf_op jit(solution)/shard_map/all_to_all | solution.py:238
  329.7 228.4 %reduce-scatter.7.cloned.1.call-start = ((), (), s32[]{:S(2)}) async-start(), calls=%async_computation.14 | async-start | bytes 2506752 | tf_op jit(solution)/shard_map/reduce_scatter | solution.py:269
  332.3 297.8 %reduce-scatter.5.cloned.1.call-start = ((), (), s32[]{:S(2)}) async-start(), calls=%async_computation.13 | async-start | bytes 7520256 | tf_op jit(solution)/shard_map/reduce_scatter | solution.py:266
  508.7 7.7 copy-start.12
  508.7 7.7 copy-start.14
  508.7 7.7 copy-start.16
  508.7 7.7 copy-start.18
  524.7 220.4 %reduce-scatter.9.cloned.1.call-start = ((), (), s32[]{:S(2)}) async-start(), calls=%async_computation.15 | async-start | bytes 10027008 | tf_op jit(solution)/shard_map/reduce_scatter | solution.py:273
  535.4 0.7 copy-start.22
  535.4 325.4 %reduce-scatter.11.cloned.1.call-start = ((), (), s32[]{:S(2)}) async-start(), calls=%async_computation.16 | async-start | bytes 10027008 | tf_op jit(solution)/shard_map/reduce_scatter | solution.py:275
  546.1 1.6 copy-start.30
  546.2 392.7 %all-reduce.24.cloned.1.call-start = ((), (), s32[]{:S(2)}) async-start(), calls=%async_computation.17 | async-start | bytes 3538944 | tf_op jit(solution)/shard_map/psum | solution.py:278
  557.7 303.2 %copy-start.1 = (bf16[2,328,768]{2,1,0:T(8,128)(2,1)S(1)}, bf16[2,328,768]{2,1,0:T(8,128)(2,1)}, u32[]{:S(2)}) copy-start(bf16[2,328,768]{2,1,0:T(8,128)(2,1)} %param.24) | copy-start | bytes 3022852
  860.9 5.8 copy-start.24
  866.6 1.3 copy-start.6
  866.6 2.2 copy-start.25
  866.6 2.2 copy-start.26
  866.6 2.2 copy-start.27
  866.6 2.2 copy-start.28
  866.6 2.2 copy-start.29
  866.6 68.8 %copy-start.4 = (f32[2,328,768]{2,1,0:T(8,128)S(1)}, f32[2,328,768]{2,1,0:T(8,128)}, u32[]{:S(2)}) copy-start(f32[2,328,768]{2,1,0:T(8,128)} %copy-done.3) | copy-start | bytes 6045700
  866.6 68.8 %copy-start.20 = (f32[2,328]{1,0:T(2,128)S(1)}, f32[2,328]{1,0:T(2,128)}, u32[]{:S(2)}) copy-start(f32[2,328]{1,0:T(2,128)} %copy-done.19) | copy-start | bytes 7876
  938.9 5.4 copy-start.10
Sparse Core Ops, SparseCore 0:
  10.3 49.9 all-gather.4
  62.6 37.3 all-gather.6
  102.3 52.1 all-gather.8
  156.6 51.7 all-gather.10
  333.9 67.1 reduce-scatter.6
  524.8 105.2 reduce-scatter.4
  634.2 110.8 reduce-scatter.8
  749.7 111.1 reduce-scatter.10
  863.4 56.0 all-reduce.23
where the time goes:
time: 963 us; the launch traced here: 952 us
  waiting for transfers between devices  358 us (37%)
  local copies, waits for them, and re-layouts  205 us (21%)
  blocking collectives  160 us (17%)
  matrix products  143 us (15%)
  other arithmetic  47 us (5%)
  starting transfers between devices  17.8 us (2%)
  between operations  17.6 us (2%)
    unnamed x2, blocking collectives  123 us
    reduce_scatter x1, waiting for transfers between devices, body(): lax.psum_scatter(grad_down, 'img', scatter_dimension=0, tiled=True)  116 us
    reduce_scatter x1, waiting for transfers between devices, body(): lax.psum_scatter(grad_up, 'img', scatter_dimension=0, tiled=True)  115 us
    reduce_scatter x1, waiting for transfers between devices, body(): lax.psum_scatter(grad_qkv, 'img', scatter_dimension=0, tiled=True)  72 us
    dynamic_slice x84, local copies, waits for them, and re-layouts, heads_forward(): lax.map(lambda pieces: attend_forward(pieces[0], pieces[1], pieces[2], pi...  36 us
    all_to_all x1, waiting for transfers between devices, body(): lax.all_to_all(stacked, 'seq', split_axis=3, concat_axis=1, tiled=True)  35.8 us
    squeeze x36, local copies, waits for them, and re-layouts, heads_forward(): lax.map(lambda pieces: attend_forward(pieces[0], pieces[1], pieces[2], pi...  34.9 us
    all_to_all x1, blocking collectives, body(): lax.all_to_all(triple, 'seq', split_axis=1, concat_axis=3, tiled=True)  31.5 us
  transfers between devices with their start and end apart: 13, of which 6 were waited for; matrix products, arithmetic and copies ran while one was open for 38% of the time, Pallas kernels for 0%

commit v1 on v0

--- a/solution.py
+++ b/solution.py
@@ -1,11 +1,12 @@
+import functools
 import jax
 import jax.numpy as jnp
 from jax import lax
+from jax.experimental import pallas as pl
+from jax.experimental.pallas import tpu as pltpu
 from jax.sharding import PartitionSpec as P
 
 HEADS = 12
-
-
 epsilon = 1e-06
 
 
@@ -124,7 +125,7 @@
     return jnp.sum(tensor.astype(jnp.float32), axis=(0, 1))
 
 
-def body(
+def general_body(
     tokens,
     token_mask,
     ln1_gain,
@@ -312,6 +313,328 @@
     )
 
 
+LOW = jnp.bfloat16
+F32 = jnp.float32
+VMEM = 56 * 1024 * 1024
+
+
+def dot_nt(left, right):
+    return lax.dot_general(left, right, (((1,), (1,)), ((), ())), preferred_element_type=F32)
+
+
+def dot_nn(left, right):
+    return lax.dot_general(left, right, (((1,), (0,)), ((), ())), preferred_element_type=F32)
+
+
+def dot_tn(left, right):
+    return lax.dot_general(left, right, (((0,), (0,)), ((), ())), preferred_element_type=F32)
+
+
+def attention_forward_kernel(scale, size, query_ref, key_ref, value_ref, mask_ref, out_ref, log_ref):
+    real = mask_ref[...] > 0.5
+    query = query_ref[...] * jnp.asarray(scale, LOW)
+    key = jnp.where(real, key_ref[...], key_ref[0:1, :])
+    value = value_ref[...]
+    lane = lax.broadcasted_iota(jnp.int32, key.shape, 1)
+    pieces = []
+    for head in range(2):
+        mine = (lane // size) == head
+        scores = dot_nt(jnp.where(mine, key, jnp.zeros_like(key)), query)
+        highest = jnp.max(scores, axis=0, keepdims=True)
+        weights = jnp.exp(scores - highest).astype(LOW)
+        extended = jnp.where(real, jnp.where(mine, value, jnp.ones_like(value)), jnp.zeros_like(value))
+        mixed = dot_tn(extended, weights)
+        own, other = head * size, (1 - head) * size
+        totals = mixed[other : other + size, :]
+        pieces.append(mixed[own : own + size, :] / totals)
+        log_ref[0, head : head + 1, :] = highest + jnp.log(totals[0:1, :])
+    out_ref[...] = jnp.concatenate(pieces, axis=0).T.astype(LOW)
+
+
+def attention_forward(qkv, mask_column):
+    rows, width = qkv.shape
+    dim = width // 3
+    size = dim // HEADS
+    pairs = HEADS // 2
+    block = (rows, 2 * size)
+    return pl.pallas_call(
+        functools.partial(attention_forward_kernel, size ** (-0.5), size),
+        grid=(pairs,),
+        in_specs=[
+            pl.BlockSpec(block, lambda p: (0, p)),
+            pl.BlockSpec(block, lambda p: (0, pairs + p)),
+            pl.BlockSpec(block, lambda p: (0, 2 * pairs + p)),
+            pl.BlockSpec((rows, 1), lambda p: (0, 0)),
+        ],
+        out_specs=[
+            pl.BlockSpec(block, lambda p: (0, p)),
+            pl.BlockSpec((1, 2, rows), lambda p: (p, 0, 0)),
+        ],
+        out_shape=[
+            jax.ShapeDtypeStruct((rows, dim), LOW),
+            jax.ShapeDtypeStruct((pairs, 2, rows), F32),
+        ],
+        compiler_params=pltpu.CompilerParams(vmem_limit_bytes=VMEM),
+        cost_estimate=pl.CostEstimate(
+            flops=8 * rows * rows * dim, bytes_accessed=8 * rows * dim, transcendentals=HEADS * rows * rows
+        ),
+        name="attention_forward",
+    )(qkv, qkv, qkv, mask_column)
+
+
+def attention_backward_kernel(
+    scale, size, query_ref, key_ref, value_ref, mask_ref, log_ref, grad_ref, dq_ref, dk_ref, dv_ref
+):
+    real = mask_ref[...] > 0.5
+    query = query_ref[...] * jnp.asarray(scale, LOW)
+    zeros = jnp.zeros_like(query)
+    key_kept = jnp.where(real, key_ref[...], zeros)
+    key = jnp.where(real, key_kept, key_ref[0:1, :])
+    value = jnp.where(real, value_ref[...], zeros)
+    grad = grad_ref[...]
+    lane = lax.broadcasted_iota(jnp.int32, key.shape, 1)
+    totals = None
+    for head in range(2):
+        mine = (lane // size) == head
+        scores = dot_nt(jnp.where(mine, key, zeros), query)
+        weights = jnp.exp(scores - log_ref[0, head : head + 1, :])
+        grad_here = jnp.where(mine, grad, zeros)
+        value_grad = dot_nn(weights.astype(LOW), grad_here)
+        weight_grad = dot_nt(value, grad_here)
+        centered = jnp.sum(weights * weight_grad, axis=0, keepdims=True)
+        score_grad = (weights * (weight_grad - centered)).astype(LOW)
+        key_grad = dot_nn(score_grad, jnp.where(mine, query, zeros))
+        query_grad = dot_tn(jnp.where(mine, key_kept, zeros), score_grad)
+        if totals is None:
+            totals = (query_grad, key_grad, value_grad)
+        else:
+            totals = tuple(a + b for a, b in zip(totals, (query_grad, key_grad, value_grad)))
+    query_grad, key_grad, value_grad = totals
+    dq_ref[...] = (query_grad * scale).T.astype(LOW)
+    dk_ref[...] = jnp.where(real, key_grad, 0.0).astype(LOW)
+    dv_ref[...] = jnp.where(real, value_grad, 0.0).astype(LOW)
+
+
+def attention_backward(qkv, mask_column, logs, grad):
+    rows, width = qkv.shape
+    dim = width // 3
+    size = dim // HEADS
+    pairs = HEADS // 2
+    block = (rows, 2 * size)
+    spec = pl.BlockSpec(block, lambda p: (0, p))
+    return pl.pallas_call(
+        functools.partial(attention_backward_kernel, size ** (-0.5), size),
+        grid=(pairs,),
+        in_specs=[
+            spec,
+            pl.BlockSpec(block, lambda p: (0, pairs + p)),
+            pl.BlockSpec(block, lambda p: (0, 2 * pairs + p)),
+            pl.BlockSpec((rows, 1), lambda p: (0, 0)),
+            pl.BlockSpec((1, 2, rows), lambda p: (p, 0, 0)),
+            spec,
+        ],
+        out_specs=[spec, spec, spec],
+        out_shape=[jax.ShapeDtypeStruct((rows, dim), LOW)] * 3,
+        compiler_params=pltpu.CompilerParams(vmem_limit_bytes=VMEM),
+        cost_estimate=pl.CostEstimate(
+            flops=20 * rows * rows * dim, bytes_accessed=16 * rows * dim, transcendentals=HEADS * rows * rows
+        ),
+        name="attention_backward",
+    )(qkv, qkv, qkv, mask_column, logs, grad)
+
+
+def mlp_kernel(
+    second_ref, dz_ref, up_ref, up_bias_ref, down_ref,
+    out_ref, second_grad_ref, down_grad_ref, up_grad_ref, up_bias_grad_ref,
+):
+    step = pl.program_id(0)
+    second = second_ref[...]
+    dz = dz_ref[...]
+    up = up_ref[...]
+    down = down_ref[...]
+    pre_act = dot_nn(second, up) + up_bias_ref[...]
+    hidden_grad = dot_nt(dz, down)
+    cumulative = 0.5 + 0.5 * lax.erf(pre_act * (0.5 ** 0.5))
+    density = jnp.exp(-0.5 * pre_act * pre_act) * 0.3989422804014327
+    hidden = (pre_act * cumulative).astype(LOW)
+    pre_grad = hidden_grad * (cumulative + pre_act * density)
+    pre_grad_low = pre_grad.astype(LOW)
+    up_bias_grad_ref[...] = jnp.sum(pre_grad_low.astype(F32), axis=0, keepdims=True)
+    out_part = dot_nn(hidden, down)
+    second_part = dot_nt(pre_grad_low, up)
+    down_grad_ref[...] = dot_tn(hidden, dz).astype(LOW)
+    up_grad_ref[...] = dot_tn(second, pre_grad_low).astype(LOW)
+
+    @pl.when(step == 0)
+    def _():
+        out_ref[...] = out_part
+        second_grad_ref[...] = second_part
+
+    @pl.when(step > 0)
+    def _():
+        out_ref[...] += out_part
+        second_grad_ref[...] += second_part
+
+
+def mlp_both(second, dz, up, up_bias, down, block=512):
+    rows, dim = second.shape
+    width = up.shape[1]
+    whole = pl.BlockSpec((rows, dim), lambda j: (0, 0))
+    return pl.pallas_call(
+        mlp_kernel,
+        grid=(width // block,),
+        in_specs=[
+            whole,
+            whole,
+            pl.BlockSpec((dim, block), lambda j: (0, j)),
+            pl.BlockSpec((1, block), lambda j: (0, j)),
+            pl.BlockSpec((block, dim), lambda j: (j, 0)),
+        ],
+        out_specs=[
+            whole,
+            whole,
+            pl.BlockSpec((block, dim), lambda j: (j, 0)),
+            pl.BlockSpec((dim, block), lambda j: (0, j)),
+            pl.BlockSpec((1, block), lambda j: (0, j)),
+        ],
+        out_shape=[
+            jax.ShapeDtypeStruct((rows, dim), F32),
+            jax.ShapeDtypeStruct((rows, dim), F32),
+            jax.ShapeDtypeStruct((width, dim), LOW),
+            jax.ShapeDtypeStruct((dim, width), LOW),
+            jax.ShapeDtypeStruct((1, width), F32),
+        ],
+        compiler_params=pltpu.CompilerParams(vmem_limit_bytes=VMEM),
+        cost_estimate=pl.CostEstimate(
+            flops=12 * rows * dim * width, bytes_accessed=16 * dim * width, transcendentals=3 * rows * width
+        ),
+        name="mlp_both",
+    )(second, dz, up, up_bias, down)
+
+
+def exchange_rows(blocks):
+    here = lax.axis_index("seq")
+    own = lax.dynamic_index_in_dim(blocks, here, 0, keepdims=False)
+    away = lax.dynamic_index_in_dim(blocks, 1 - here, 0, keepdims=False)
+    return own, lax.ppermute(away, "seq", [(0, 1), (1, 0)])
+
+
+def return_rows(rows):
+    here = lax.axis_index("seq")
+    half = rows.shape[0] // 2
+    own = rows[:half]
+    back = lax.ppermute(rows[half:].astype(LOW), "seq", [(0, 1), (1, 0)]).astype(F32)
+    return jnp.where(here == 0, jnp.stack([own, back]), jnp.stack([back, own]))
+
+
+def gather(block):
+    return lax.all_gather(block, "img", axis=0, tiled=True)
+
+
+def reduce(total):
+    part = lax.psum_scatter(total, "img", scatter_dimension=0, tiled=True)
+    return part.astype(F32) + lax.ppermute(part, "seq", [(0, 1), (1, 0)]).astype(F32)
+
+
+def norm_parts(values):
+    offset = values - jnp.mean(values, axis=-1, keepdims=True)
+    inverse = lax.rsqrt(jnp.mean(offset * offset, axis=-1, keepdims=True) + epsilon)
+    return offset * inverse, inverse
+
+
+def norm_back(unit, inverse, gain, grad):
+    scaled = grad * gain
+    across = jnp.mean(scaled, axis=-1, keepdims=True)
+    along = jnp.mean(scaled * unit, axis=-1, keepdims=True)
+    return inverse * (scaled - across - unit * along), jnp.sum(grad * unit, axis=0), jnp.sum(grad, axis=0)
+
+
+SMALL_PAD = 256
+
+
+def image_body(
+    tokens, token_mask, ln1_gain, ln1_bias, w_qkv, bias_q, bias_v, w_out, bias_out,
+    ln2_gain, ln2_bias, w_up, bias_up, w_down, bias_down, cotangent,
+):
+    shard_rows, dim = tokens.shape[1:]
+    owners = lax.axis_size("img")
+    shard = dim // owners
+    width = bias_up.shape[0] * owners
+    smalls = (ln1_gain, ln1_bias, bias_q, bias_v, bias_out, ln2_gain, ln2_bias, bias_down, bias_up)
+    sizes = [s.shape[0] for s in smalls]
+    columns = sum(sizes) // shard
+
+    packed = jnp.concatenate(smalls).reshape(shard, columns)
+    first = gather(jnp.concatenate([w_qkv, jnp.pad(packed, ((0, 0), (0, 128 - columns)))], axis=1))
+    qkv_full = first[:, : 3 * dim]
+    small_full = first[:, 3 * dim : 3 * dim + columns].reshape(owners, shard * columns).astype(F32)
+    cuts = [sum(sizes[:i]) for i in range(len(sizes) + 1)]
+    (gain_one, shift_one, query_bias, value_bias, out_bias, gain_two, shift_two, down_bias, up_bias) = [
+        small_full[:, a:b].reshape(-1) for a, b in zip(cuts[:-1], cuts[1:])
+    ]
+    second_gather = gather(jnp.concatenate([w_out, w_up], axis=1))
+    out_full, up_full = second_gather[:, :dim], second_gather[:, dim:]
+    down_full = gather(w_down)
+
+    mask_rows = jnp.broadcast_to(
+        jnp.pad(token_mask.astype(LOW), ((0, 0), (0, dim - shard_rows)))[:, None, :], (2, 16, dim)
+    )
+    own, away = exchange_rows(jnp.concatenate([tokens, mask_rows], axis=1))
+    both = jnp.stack([own, away])
+    inputs = both[:, :shard_rows].reshape(2 * shard_rows, dim).astype(F32)
+    mask_column = both[:, shard_rows, :shard_rows].astype(F32).reshape(2 * shard_rows, 1)
+    masked = jnp.where(token_mask[..., None] > 0, cotangent, jnp.zeros_like(cotangent))
+    down_in = jnp.concatenate(exchange_rows(masked), axis=0)
+
+    unit_one, inverse_one = norm_parts(inputs)
+    normed = (unit_one * gain_one + shift_one).astype(LOW)
+    qkv_bias = jnp.concatenate([query_bias, jnp.zeros_like(query_bias), value_bias])
+    qkv = (dot_nn(normed, qkv_full) + qkv_bias).astype(LOW)
+    merged, logs = attention_forward(qkv, mask_column)
+    middle = inputs + dot_nn(merged, out_full) + out_bias
+    unit_two, inverse_two = norm_parts(middle)
+    second = (unit_two * gain_two + shift_two).astype(LOW)
+    mlp_out, second_grad, grad_down, grad_up, grad_up_bias = mlp_both(
+        second, down_in, up_full, up_bias.reshape(1, width), down_full
+    )
+    output = middle + mlp_out + down_bias
+    upstream = down_in.astype(F32)
+    grad_down_bias = jnp.sum(upstream, axis=0)
+    middle_ln, grad_gain_two, grad_shift_two = norm_back(unit_two, inverse_two, gain_two, second_grad)
+    middle_grad = upstream + middle_ln
+    branch_grad = middle_grad.astype(LOW)
+    grad_out = dot_tn(merged, branch_grad).astype(LOW)
+    grad_out_bias = jnp.sum(branch_grad.astype(F32), axis=0)
+    merged_grad = dot_nt(branch_grad, out_full).astype(LOW)
+    query_grad, key_grad, value_grad = attention_backward(qkv, mask_column, logs, merged_grad)
+    qkv_grad = jnp.concatenate([query_grad, key_grad, value_grad], axis=1)
+    grad_qkv = dot_tn(normed, qkv_grad).astype(LOW)
+    grad_query_bias = jnp.sum(query_grad.astype(F32), axis=0)
+    grad_value_bias = jnp.sum(value_grad.astype(F32), axis=0)
+    normed_grad = dot_nt(qkv_grad, qkv_full)
+    input_ln, grad_gain_one, grad_shift_one = norm_back(unit_one, inverse_one, gain_one, normed_grad)
+    input_grad = middle_grad + input_ln
+
+    small_grads = (
+        grad_gain_one, grad_shift_one, grad_query_bias, grad_value_bias, grad_out_bias,
+        grad_gain_two, grad_shift_two, grad_down_bias, grad_up_bias.reshape(-1),
+    )
+    small_packed = jnp.concatenate([g.reshape(owners, -1) for g in small_grads], axis=1)
+    small_packed = jnp.pad(small_packed.reshape(dim, columns), ((0, 0), (0, SMALL_PAD - columns))).astype(LOW)
+    down_sum = reduce(grad_down)
+    up_sum = reduce(jnp.concatenate([grad_out, grad_up], axis=1))
+    qkv_sum = reduce(jnp.concatenate([grad_qkv, small_packed], axis=1))
+    small_sum = qkv_sum[:, 3 * dim : 3 * dim + columns].reshape(-1)
+    (sum_gain_one, sum_shift_one, sum_query, sum_value, sum_out, sum_gain_two, sum_shift_two, sum_down, sum_up) = [
+        small_sum[a:b] for a, b in zip(cuts[:-1], cuts[1:])
+    ]
+    return (
+        return_rows(output), return_rows(input_grad), sum_gain_one, sum_shift_one, qkv_sum[:, : 3 * dim],
+        sum_query, sum_value, up_sum[:, :dim], sum_out, sum_gain_two, sum_shift_two, up_sum[:, dim:],
+        sum_up, down_sum, sum_down,
+    )
+
+
 def solution(mesh):
     in_specs = (
         P("img", "seq", None),
@@ -348,4 +671,9 @@
         P("img", None),
         P("img"),
     )
+    def body(*blocks):
+        one_each = blocks[0].shape[0] == mesh.shape["seq"] == 2
+        plan = image_body if one_each and mesh.shape["img"] == 16 else general_body
+        return plan(*blocks)
+
     return jax.shard_map(body, mesh=mesh, in_specs=in_specs, out_specs=out_specs, check_vma=False)

time: 963 us -> 527 us (0.55); the launches traced: 952 us -> 526 us
  local copies, waits for them, and re-layouts: 205 us -> 42.6 us
  blocking collectives: 160 us -> 0 us
  matrix products: 143 us -> 25.4 us
  Pallas kernels: 0 us -> 66 us
  waiting for transfers between devices: 358 us -> 324 us
    unnamed x2 -> x0, blocking collectives: 123 us -> none
    dot_general x180 -> x6, matrix products: 143 us -> 25.4 us  [the longest x2 8.83 us: dot_tn(): lax.dot_general(left, right, (((0,), (0,)), ((), ())), preferred_element_...]
    reduce_scatter x4 -> x3, waiting for transfers between devices: 303 us -> 189 us  [reduce(): part = lax.psum_scatter(total, 'img', scatter_dimension=0, tiled=True)]
    all_gather x4 -> x3, waiting for transfers between devices: 0.04 us -> 93 us  [gather(): return lax.all_gather(block, 'img', axis=0, tiled=True)]
    pallas_call x0 -> x3, Pallas kernels: none -> 66 us  [the longest x1 28.3 us: mlp_both(): pl.pallas_call(mlp_kernel, grid=(width // block,), in_specs=[whole, whole...]
    all_to_all x4 -> x0, waiting for transfers between devices: 52.3 us -> none  [the longest x1 35.8 us: body(): lax.all_to_all(stacked, 'seq', split_axis=3, concat_axis=1, tiled=True)]
    ppermute x0 -> x7, waiting for transfers between devices: none -> 40.6 us  [the longest x2 19.3 us: exchange_rows(): return (own, lax.ppermute(away, 'seq', [(0, 1), (1, 0)]))]
    dynamic_slice x108 -> x0, local copies, waits for them, and re-layouts: 36.7 us -> none  [the longest x84 36 us: heads_forward(): lax.map(lambda pieces: attend_forward(pieces[0], pieces[1], pieces[2], pi...]
  transfers between devices with their start and end apart: 13 -> 13, of which waited for: 6 -> 11; matrix products, arithmetic and copies ran while one was open for 38% -> 11% of each run, Pallas kernels for 0% -> 3%
where the time goes in v1:
time: 527 us; the launch traced here: 526 us
  waiting for transfers between devices  324 us (61%)
  Pallas kernels  66 us (13%)
  other arithmetic  43.2 us (8%)
  local copies, waits for them, and re-layouts  42.6 us (8%)
  matrix products  25.4 us (5%)
  between operations  14.5 us (3%)
  starting transfers between devices  10.6 us (2%)
    reduce_scatter x3, waiting for transfers between devices, reduce(): part = lax.psum_scatter(total, 'img', scatter_dimension=0, tiled=True)  189 us
    all_gather x3, waiting for transfers between devices, gather(): return lax.all_gather(block, 'img', axis=0, tiled=True)  93 us
    pallas_call x1, Pallas kernels, mlp_both(): pl.pallas_call(mlp_kernel, grid=(width // block,), in_specs=[whole, whole...  28.3 us
    pallas_call x1, Pallas kernels, attention_backward(): pl.pallas_call(functools.partial(attention_backward_kernel, size ** (-0.5...  24.2 us
    ppermute x2, waiting for transfers between devices, exchange_rows(): return (own, lax.ppermute(away, 'seq', [(0, 1), (1, 0)]))  19.3 us
    ppermute x2, waiting for transfers between devices, return_rows(): lax.ppermute(rows[half:].astype(LOW), 'seq', [(0, 1), (1, 0)]).astype(F32)  18.6 us
    pallas_call x1, Pallas kernels, attention_forward(): pl.pallas_call(functools.partial(attention_forward_kernel, size ** (-0.5)...  13.4 us
  transfers between devices with their start and end apart: 13, of which 11 were waited for; matrix products, arithmetic and copies ran while one was open for 11% of the time, Pallas kernels for 3%

profile of v1, /device:TPU:0, one launch (start us, length us, event | category | flops | bytes accessed | tf_op | source)
XLA Modules:
  0.0 526.1 jit_solution(10265251992236098011)
XLA Ops:
  7.2 6.2 %concatenate.32 = bf16[576]{0:T(1024)(128)(2,1)S(1)} concatenate(bf16[48]{0:T(256)(128)(2,1)} %param.18, bf16[48]{0:T(256)(128)(2,1)} %param.19, bf16[48]{0:T(256)(128)(2,1)} %param.21, bf16[48]{0:T(256)(128)(2,1)} %param.22, bf16[48]{0:T(256)(128)(2,1)} %param.24, bf16[48]{0:T(256)(128)(2,1)} %param.25, bf16[48]{0:T(256)(128)(2,1)} %param.26, bf16[48]{0:T(256)(128)(2,1)} %param.30, ...), dimensions={0} | concatenate | bytes 2304 | tf_op jit(solution)/shard_map/concatenate | solution.py:567
  13.5 1.6 fusion.15
  15.2 1.7 pad_maximum_fusion.2
  18.1 3.0 collective-permute-start.1
  22.9 10.6 %collective-permute-done.1 = bf16[328,768]{1,0:T(8,128)(2,1)S(1)} collective-permute-done((bf16[328,768]{1,0:T(8,128)(2,1)S(1)}, bf16[328,768]{1,0:T(8,128)(2,1)S(1)}, u32[]{:S(2)}, u32[]{:S(2)}) %collective-permute-start.1) | collective-permute-done | bytes 503840 | tf_op jit(solution)/shard_map/ppermute | solution.py:519
  35.3 8.7 %collective-permute-done = bf16[344,768]{1,0:T(8,128)(2,1)S(1)} collective-permute-done((bf16[344,768]{1,0:T(8,128)(2,1)}, bf16[344,768]{1,0:T(8,128)(2,1)S(1)}, u32[]{:S(2)}, u32[]{:S(2)}) %collective-permute-start) | collective-permute-done | bytes 528416 | tf_op jit(solution)/shard_map/ppermute | solution.py:519
  46.2 19.7 %all-gather.4.cloned.1.call-done = bf16[768,2432]{1,0:T(8,128)(2,1)} async-done(((bf16[48,2432]{1,0:T(8,128)(2,1)}), bf16[768,2432]{1,0:T(8,128)(2,1)}) %all-gather.4.cloned.1.call-update) | async-done | bytes 3735568 | tf_op jit(solution)/shard_map/all_gather | solution.py:531
  65.9 1.7 slice_convert_fusion.2
  67.6 1.8 reshape.187
  70.8 1.5 fusion.25
  72.3 1.4 add.126
  75.3 1.4 add.112
  76.7 1.4 add.122
  79.6 6.3 %add_convert_fusion.query_ref.key_ref.value_ref = bf16[656,2304]{1,0:T(8,128)(2,1)} fusion(bf16[768,2432]{1,0:T(8,128)(2,1)} %all-gather.4.cloned.1.call-done, f32[2304]{0:T(1024)S(1)} %pad_maximum_fusion.3, f32[656,768]{1,0:T(8,128)S(1)} %fusion.7, f32[768]{0:T(1024)} %add.112, f32[768]{0:T(1024)S(1)} %mul.98), kind=kOutput, calls=%fused_computation.2 | convolution fusion | flops 2326081536 | bytes 8593408 | tf_op jit(solution)/shard_map/dot_general | solution.py:326
  85.9 13.4 %attention_forward.1 = (bf16[656,768]{1,0:T(8,128)(2,1)}, f32[6,2,656]{2,1,0:T(2,128)}) custom-call(bf16[656,2304]{1,0:T(8,128)(2,1)} %add_convert_fusion.query_ref.key_ref.value_ref, bf16[656,2304]{1,0:T(8,128)(2,1)} %add_convert_fusion.query_ref.key_ref.value_ref, bf16[656,2304]{1,0:T(8,128)(2,1)} %add_convert_fusion.query_ref.key_ref.value_ref, ...), custom_call_target="tpu_custom_call" | custom-call | flops 2643984384 | bytes 4030464 | tf_op jit(solution)/shard_map/attention_forward/pallas_call | solution.py:360
  99.3 28.3 %all-gather.6.cloned.1.call-done = bf16[768,3840]{1,0:T(8,128)(2,1)} async-done(((bf16[48,3840]{1,0:T(8,128)(2,1)}), bf16[768,3840]{1,0:T(8,128)(2,1)}) %all-gather.6.cloned.1.call-update) | async-done | bytes 5898256 | tf_op jit(solution)/shard_map/all_gather | solution.py:531
  127.5 4.9 slice.184.up_ref
  132.4 2.2 bitcast_add_fusion
  135.3 1.4 add_convert_fusion.1.second_ref
  136.7 45.0 %all-gather.8.cloned.1.call-done.down_ref = bf16[3072,768]{1,0:T(8,128)(2,1)} async-done(((bf16[192,768]{1,0:T(8,128)(2,1)}), bf16[3072,768]{1,0:T(8,128)(2,1)}) %all-gather.8.cloned.1.call-update) | async-done | bytes 4718608 | tf_op jit(solution)/shard_map/all_gather | solution.py:531
  181.7 28.3 %mlp_both.1 = (f32[656,768]{1,0:T(8,128)}, f32[656,768]{1,0:T(8,128)}, bf16[3072,768]{1,0:T(8,128)(2,1)}, bf16[768,3072]{1,0:T(8,128)(2,1)}, f32[1,3072]{1,0:T(1,128)}) custom-call(bf16[656,768]{1,0:T(8,128)(2,1)} %add_convert_fusion.1.second_ref, bf16[656,768]{1,0:T(8,128)(2,1)} %pad_maximum_fusion.1.dz_ref, bf16[768,3072]{1,0:T(8,128)(2,1)} %slice.184.up_ref, ...), custom_call_target="tpu_custom_call" | custom-call | flops 18572378112 | bytes 37748736 | tf_op jit(solution)/shard_map/mlp_both/pallas_call | solution.py:483
  210.1 1.3 convert_reduce_fusion.1
  211.4 1.4 reshape_reshape.8
  212.8 5.0 multiply_reduce_fusion
  219.1 1.3 reshape.183
  221.0 3.9 convert_reduce_fusion.2
  225.7 3.8 convolution_convert_fusion.2.grad_ref
  229.5 24.2 %attention_backward.1 = (bf16[656,768]{1,0:T(8,128)(2,1)}, bf16[656,768]{1,0:T(8,128)(2,1)}, bf16[656,768]{1,0:T(8,128)(2,1)}) custom-call(bf16[656,2304]{1,0:T(8,128)(2,1)} %add_convert_fusion.query_ref.key_ref.value_ref, bf16[656,2304]{1,0:T(8,128)(2,1)} %add_convert_fusion.query_ref.key_ref.value_ref, ...), custom_call_target="tpu_custom_call" | custom-call | flops 6609960960 | bytes 8060928 | tf_op jit(solution)/shard_map/attention_backward/pallas_call | solution.py:425
  253.8 2.6 fusion.23
  258.8 6.5 %convolution_convert_fusion = bf16[768,2304]{1,0:T(8,128)(2,1)} fusion(bf16[656,2304]{1,0:T(8,128)(2,1)} %get-tuple-element.56, f32[656,768]{1,0:T(8,128)S(1)} %copy-done.4, f32[768]{0:T(1024)S(1)} %copy-done.19, f32[768]{0:T(1024)S(1)} %mul.98), kind=kOutput, calls=%fused_computation.4 | convolution fusion | flops 2324828160 | bytes 8583168 | tf_op jit(solution)/shard_map/dot_general | solution.py:330
  265.3 4.2 fusion.20
  270.2 3.5 fusion.1
  275.3 2.4 convolution_convert_fusion.1
  277.7 5.4 %pad_maximum_fusion = bf16[768,3840]{1,0:T(8,128)(2,1)} fusion(bf16[768,3072]{1,0:T(8,128)(2,1)} %get-tuple-element.33, bf16[768,768]{1,0:T(8,128)(2,1)S(1)} %convolution_convert_fusion.1), kind=kLoop, calls=%fused_computation.3 | loop fusion | flops 11796480 | bytes 11796480 | tf_op jit(solution)/shard_map/concatenate | solution.py:625
  283.1 1.3 slice.223
  284.4 1.5 collective-permute-start.2
  285.9 2.5 multiply_add_fusion
  290.2 8.5 %collective-permute-done.2 = bf16[328,768]{1,0:T(8,128)(2,1)S(1)} collective-permute-done((bf16[328,768]{1,0:T(8,128)(2,1)S(1)}, bf16[328,768]{1,0:T(8,128)(2,1)S(1)}, u32[]{:S(2)}, u32[]{:S(2)}) %collective-permute-start.2) | collective-permute-done | bytes 503840 | tf_op jit(solution)/shard_map/ppermute | solution.py:526
  298.9 10.1 %collective-permute-done.3 = bf16[328,768]{1,0:T(8,128)(2,1)S(1)} collective-permute-done((bf16[328,768]{1,0:T(8,128)(2,1)S(1)}, bf16[328,768]{1,0:T(8,128)(2,1)S(1)}, u32[]{:S(2)}, u32[]{:S(2)}) %collective-permute-start.3) | collective-permute-done | bytes 503840 | tf_op jit(solution)/shard_map/ppermute | solution.py:526
  309.0 33.6 %reduce-scatter.4.cloned.1.call-done = bf16[48,2560]{1,0:T(8,128)(2,1)} async-done(((bf16[768,2560]{1,0:T(8,128)(2,1)}), bf16[48,2560]{1,0:T(8,128)(2,1)}) %reduce-scatter.4.cloned.1.call-update) | async-done | bytes 245776 | tf_op jit(solution)/shard_map/reduce_scatter | solution.py:535
  342.6 1.4 collective-permute-start.4
  344.0 3.0 maximum_select_fusion
  347.0 1.4 maximum_select_fusion.1
  348.4 72.9 %reduce-scatter.8.cloned.1.call-done = bf16[192,768]{1,0:T(8,128)(2,1)} async-done(((bf16[3072,768]{1,0:T(8,128)(2,1)}), bf16[192,768]{1,0:T(8,128)(2,1)}) %reduce-scatter.8.cloned.1.call-update) | async-done | bytes 294928 | tf_op jit(solution)/shard_map/reduce_scatter | solution.py:535
  421.3 1.5 collective-permute-start.6
  424.3 82.5 %reduce-scatter.6.cloned.1.call-done = bf16[48,3840]{1,0:T(8,128)(2,1)} async-done(((bf16[768,3840]{1,0:T(8,128)(2,1)}), bf16[48,3840]{1,0:T(8,128)(2,1)}) %reduce-scatter.6.cloned.1.call-update) | async-done | bytes 368656 | tf_op jit(solution)/shard_map/reduce_scatter | solution.py:535
  506.7 1.5 collective-permute-start.5
  513.9 2.8 collective-permute-done.5
  (127 shorter events, 31.2 us)
Async XLA Ops:
  7.2 10.6 %copy-start.17 = (s32[2,328]{1,0:T(2,128)S(1)}, s32[2,328]{1,0:T(2,128)}, u32[]{:S(2)}) copy-start(s32[2,328]{1,0:T(2,128)} %param.17) | copy-start | bytes 7876
  7.2 10.6 %copy-start.6 = (bf16[2,328,768]{2,1,0:T(8,128)(2,1)S(1)}, bf16[2,328,768]{2,1,0:T(8,128)(2,1)}, u32[]{:S(2)}) copy-start(bf16[2,328,768]{2,1,0:T(8,128)(2,1)} %param.31) | copy-start | bytes 3022852
  7.2 58.7 %all-gather.4.cloned.1.call-start = ((), (), s32[]{:S(2)}) async-start(), calls=%async_computation.3 | async-start | bytes 3969024 | tf_op jit(solution)/shard_map/all_gather | solution.py:531
  15.2 112.3 %all-gather.6.cloned.1.call-start = ((), (), s32[]{:S(2)}) async-start(), calls=%async_computation.4 | async-start | bytes 6266880 | tf_op jit(solution)/shard_map/all_gather | solution.py:531
  17.0 164.7 %all-gather.8.cloned.1.call-start = ((), (), s32[]{:S(2)}) async-start(), calls=%async_computation.5 | async-start | bytes 5013504 | tf_op jit(solution)/shard_map/all_gather | solution.py:531
  17.7 324.8 %reduce-scatter.4.cloned.1.call-start = ((), (), s32[]{:S(2)}) async-start(), calls=%async_computation.6 | async-start | bytes 4177920 | tf_op jit(solution)/shard_map/reduce_scatter | solution.py:535
  17.8 3.4 copy-start.8
  18.1 15.3 %collective-permute-start.1 = (bf16[328,768]{1,0:T(8,128)(2,1)S(1)}, bf16[328,768]{1,0:T(8,128)(2,1)S(1)}, u32[]{:S(2)}, u32[]{:S(2)}) collective-permute-start(bf16[328,768]{1,0:T(8,128)(2,1)S(1)} %get-tuple-element.53), channel_id=1, source_target_pairs={{0,1},{1,0},{2,3},{3,2},{4,5},{5,4},{6,7},{7,6},{8,9},{9,8},{10,11... | collective-permute-start | bytes 1511432 | tf_op jit(solution)/shard_map/ppermute | solution.py:519
  22.1 21.8 %collective-permute-start = (bf16[344,768]{1,0:T(8,128)(2,1)}, bf16[344,768]{1,0:T(8,128)(2,1)S(1)}, u32[]{:S(2)}, u32[]{:S(2)}) collective-permute-start(bf16[344,768]{1,0:T(8,128)(2,1)} %get-tuple-element.51), channel_id=1, source_target_pairs={{0,1},{1,0},{2,3},{3,2},{4,5},{5,4},{6,7},{7,6},{8,9},{9,8},{10,11... | collective-permute-start | bytes 1585160 | tf_op jit(solution)/shard_map/ppermute | solution.py:519
  33.5 10.5 %copy-start.2 = (bf16[328,768]{1,0:T(8,128)(2,1)}, bf16[328,768]{1,0:T(8,128)(2,1)S(1)}, u32[]{:S(2)}) copy-start(bf16[328,768]{1,0:T(8,128)(2,1)S(1)} %collective-permute-done.1) | copy-start | bytes 1511428
  46.1 39.7 %copy-start.3 = (f32[656,768]{1,0:T(8,128)}, f32[656,768]{1,0:T(8,128)S(1)}, u32[]{:S(2)}) copy-start(f32[656,768]{1,0:T(8,128)S(1)} %fusion.7) | copy-start | bytes 6045700
  127.5 4.9 copy-start.20
  134.7 0.7 copy-start.13
  253.8 2.7 copy-start.7
  253.8 3.8 copy-start.5
  256.5 2.3 copy-start.4
  256.5 2.3 copy-start.19
  258.8 6.5 %copy-start.9 = (bf16[656,2304]{1,0:T(8,128)(2,1)S(1)}, bf16[656,2304]{1,0:T(8,128)(2,1)}, u32[]{:S(2)}) copy-start(bf16[656,2304]{1,0:T(8,128)(2,1)} %get-tuple-element.56) | copy-start | bytes 9068548
  258.8 6.5 %copy-start.18 = (bf16[768,2432]{1,0:T(8,128)(2,1)S(1)}, bf16[768,2432]{1,0:T(8,128)(2,1)}, u32[]{:S(2)}) copy-start(bf16[768,2432]{1,0:T(8,128)(2,1)} %all-gather.4.cloned.1.call-done) | copy-start | bytes 11206660
  265.3 4.5 copy-start.12
  265.3 4.5 copy-start.14
  265.3 4.5 copy-start.15
  265.3 4.5 copy-start.16
  273.7 147.6 %reduce-scatter.8.cloned.1.call-start = ((), (), s32[]{:S(2)}) async-start(), calls=%async_computation.8 | async-start | bytes 5013504 | tf_op jit(solution)/shard_map/reduce_scatter | solution.py:535
  273.7 1.6 copy-start
  274.3 232.5 %reduce-scatter.6.cloned.1.call-start = ((), (), s32[]{:S(2)}) async-start(), calls=%async_computation.7 | async-start | bytes 6266880 | tf_op jit(solution)/shard_map/reduce_scatter | solution.py:535
  284.4 14.4 %collective-permute-start.2 = (bf16[328,768]{1,0:T(8,128)(2,1)S(1)}, bf16[328,768]{1,0:T(8,128)(2,1)S(1)}, u32[]{:S(2)}, u32[]{:S(2)}) collective-permute-start(bf16[328,768]{1,0:T(8,128)(2,1)S(1)} %slice.223), channel_id=1, source_target_pairs={{0,1},{1,0},{2,3},{3,2},{4,5},{5,4},{6,7},{7,6},{8,9},{9,8},{10,11... | collective-permute-start | bytes 1511432 | tf_op jit(solution)/shard_map/ppermute | solution.py:526
  285.9 3.3 copy-start.1
  288.5 20.4 %collective-permute-start.3 = (bf16[328,768]{1,0:T(8,128)(2,1)S(1)}, bf16[328,768]{1,0:T(8,128)(2,1)S(1)}, u32[]{:S(2)}, u32[]{:S(2)}) collective-permute-start(bf16[328,768]{1,0:T(8,128)(2,1)S(1)} %slice.222), channel_id=1, source_target_pairs={{0,1},{1,0},{2,3},{3,2},{4,5},{5,4},{6,7},{7,6},{8,9},{9,8},{10,11... | collective-permute-start | bytes 1511432 | tf_op jit(solution)/shard_map/ppermute | solution.py:526
  342.6 80.2 %collective-permute-start.4 = (bf16[48,2560]{1,0:T(8,128)(2,1)}, bf16[48,2560]{1,0:T(8,128)(2,1)S(1)}, u32[]{:S(2)}, u32[]{:S(2)}) collective-permute-start(bf16[48,2560]{1,0:T(8,128)(2,1)} %reduce-scatter.4.cloned.1.call-done), channel_id=1, source_target_pairs={{0,1},{1,0},{2,3},{3,2},{4,5},{5,4},{6,7},{7,6},{8,9},{9,8},{10,11... | collective-permute-start | bytes 737288 | tf_op jit(solution)/shard_map/ppermute | solution.py:536
  347.0 75.8 %copy-start.11 = (bf16[48,2560]{1,0:T(8,128)(2,1)S(1)}, bf16[48,2560]{1,0:T(8,128)(2,1)}, u32[]{:S(2)}) copy-start(bf16[48,2560]{1,0:T(8,128)(2,1)} %reduce-scatter.4.cloned.1.call-done) | copy-start | bytes 737284
  421.3 91.7 %copy-start.10 = (bf16[192,768]{1,0:T(8,128)(2,1)S(1)}, bf16[192,768]{1,0:T(8,128)(2,1)}, u32[]{:S(2)}) copy-start(bf16[192,768]{1,0:T(8,128)(2,1)} %reduce-scatter.8.cloned.1.call-done) | copy-start | bytes 884740
  421.3 91.7 %collective-permute-start.6 = (bf16[192,768]{1,0:T(8,128)(2,1)}, bf16[192,768]{1,0:T(8,128)(2,1)S(1)}, u32[]{:S(2)}, u32[]{:S(2)}) collective-permute-start(bf16[192,768]{1,0:T(8,128)(2,1)} %reduce-scatter.8.cloned.1.call-done), channel_id=1, source_target_pairs={{0,1},{1,0},{2,3},{3,2},{4,5},{5,4},{6,7},{7,6},{8,9},{9,8},{10,11... | collective-permute-start | bytes 884744 | tf_op jit(solution)/shard_map/ppermute | solution.py:536
  506.7 9.9 %collective-permute-start.5 = (bf16[48,3840]{1,0:T(8,128)(2,1)}, bf16[48,3840]{1,0:T(8,128)(2,1)S(1)}, u32[]{:S(2)}, u32[]{:S(2)}) collective-permute-start(bf16[48,3840]{1,0:T(8,128)(2,1)} %reduce-scatter.6.cloned.1.call-done), channel_id=1, source_target_pairs={{0,1},{1,0},{2,3},{3,2},{4,5},{5,4},{6,7},{7,6},{8,9},{9,8},{10,11... | collective-permute-start | bytes 1105928 | tf_op jit(solution)/shard_map/ppermute | solution.py:536
Sparse Core Ops, SparseCore 0:
  15.3 50.5 all-gather.3
  68.7 58.7 all-gather.5
  129.8 51.8 all-gather.7
  273.8 68.6 reduce-scatter.3
  346.7 74.5 reduce-scatter.7
  425.1 81.6 reduce-scatter.5

commit v2 on v1

--- a/solution.py
+++ b/solution.py
@@ -316,6 +316,11 @@
 LOW = jnp.bfloat16
 F32 = jnp.float32
 VMEM = 56 * 1024 * 1024
+SMALL_PAD = 256
+
+
+def cost(microseconds):
+    return pl.CostEstimate(flops=int(microseconds * 1.15e9), bytes_accessed=1, transcendentals=0)
 
 
 def dot_nt(left, right):
@@ -375,9 +380,7 @@
             jax.ShapeDtypeStruct((pairs, 2, rows), F32),
         ],
         compiler_params=pltpu.CompilerParams(vmem_limit_bytes=VMEM),
-        cost_estimate=pl.CostEstimate(
-            flops=8 * rows * rows * dim, bytes_accessed=8 * rows * dim, transcendentals=HEADS * rows * rows
-        ),
+        cost_estimate=cost(13),
         name="attention_forward",
     )(qkv, qkv, qkv, mask_column)
 
@@ -415,125 +418,152 @@
     dv_ref[...] = jnp.where(real, value_grad, 0.0).astype(LOW)
 
 
-def attention_backward(qkv, mask_column, logs, grad):
+def attention_backward(qkv, mask_column, logs, grad, first, count):
     rows, width = qkv.shape
     dim = width // 3
     size = dim // HEADS
     pairs = HEADS // 2
     block = (rows, 2 * size)
-    spec = pl.BlockSpec(block, lambda p: (0, p))
+    spec = pl.BlockSpec(block, lambda p: (0, first + p))
+    out_spec = pl.BlockSpec(block, lambda p: (0, p))
     return pl.pallas_call(
         functools.partial(attention_backward_kernel, size ** (-0.5), size),
-        grid=(pairs,),
+        grid=(count,),
         in_specs=[
             spec,
-            pl.BlockSpec(block, lambda p: (0, pairs + p)),
-            pl.BlockSpec(block, lambda p: (0, 2 * pairs + p)),
+            pl.BlockSpec(block, lambda p: (0, pairs + first + p)),
+            pl.BlockSpec(block, lambda p: (0, 2 * pairs + first + p)),
             pl.BlockSpec((rows, 1), lambda p: (0, 0)),
-            pl.BlockSpec((1, 2, rows), lambda p: (p, 0, 0)),
+            pl.BlockSpec((1, 2, rows), lambda p: (first + p, 0, 0)),
             spec,
         ],
-        out_specs=[spec, spec, spec],
-        out_shape=[jax.ShapeDtypeStruct((rows, dim), LOW)] * 3,
+        out_specs=[out_spec] * 3,
+        out_shape=[jax.ShapeDtypeStruct((rows, 2 * size * count), LOW)] * 3,
         compiler_params=pltpu.CompilerParams(vmem_limit_bytes=VMEM),
-        cost_estimate=pl.CostEstimate(
-            flops=20 * rows * rows * dim, bytes_accessed=16 * rows * dim, transcendentals=HEADS * rows * rows
-        ),
+        cost_estimate=cost(1),
         name="attention_backward",
     )(qkv, qkv, qkv, mask_column, logs, grad)
 
 
-def mlp_kernel(
-    second_ref, dz_ref, up_ref, up_bias_ref, down_ref,
-    out_ref, second_grad_ref, down_grad_ref, up_grad_ref, up_bias_grad_ref,
+def split_cores(total_ref, kept_ref, sent_ref, first, columns):
+    core = lax.axis_index("img") % 2
+    shard = kept_ref.shape[2]
+    for pair in range(total_ref.shape[0] // (2 * shard)):
+        z, x = first + pair // 2, pair % 2
+        kept_ref[z, x, :, columns] = total_ref[pl.ds(pl.multiple_of((2 * pair + core) * shard, 16), shard), :]
+        sent_ref[z, x, :, columns] = total_ref[pl.ds(pl.multiple_of((2 * pair + 1 - core) * shard, 16), shard), :]
+
+
+def mlp_first_kernel(
+    shape, second_ref, dz_ref, up_ref, up_bias_ref, down_ref,
+    out_ref, kept_ref, sent_ref, pre_grad_ref, up_bias_grad_ref, down_grad_ref,
 ):
     step = pl.program_id(0)
-    second = second_ref[...]
+    owners, pieces, dim = shape
     dz = dz_ref[...]
-    up = up_ref[...]
-    down = down_ref[...]
-    pre_act = dot_nn(second, up) + up_bias_ref[...]
+    down = jnp.concatenate(
+        [down_ref[o, :, i * dim : (i + 1) * dim] for o in range(owners) for i in range(pieces)], axis=0
+    )
+    pre_act = dot_nn(second_ref[...], up_ref[...]) + up_bias_ref[...]
     hidden_grad = dot_nt(dz, down)
     cumulative = 0.5 + 0.5 * lax.erf(pre_act * (0.5 ** 0.5))
     density = jnp.exp(-0.5 * pre_act * pre_act) * 0.3989422804014327
     hidden = (pre_act * cumulative).astype(LOW)
-    pre_grad = hidden_grad * (cumulative + pre_act * density)
-    pre_grad_low = pre_grad.astype(LOW)
-    up_bias_grad_ref[...] = jnp.sum(pre_grad_low.astype(F32), axis=0, keepdims=True)
+    pre_grad = (hidden_grad * (cumulative + pre_act * density)).astype(LOW)
+    pre_grad_ref[...] = pre_grad
+    up_bias_grad_ref[...] = jnp.sum(pre_grad.astype(F32), axis=0, keepdims=True)
     out_part = dot_nn(hidden, down)
-    second_part = dot_nt(pre_grad_low, up)
     down_grad_ref[...] = dot_tn(hidden, dz).astype(LOW)
-    up_grad_ref[...] = dot_tn(second, pre_grad_low).astype(LOW)
+    split_cores(down_grad_ref, kept_ref, sent_ref, 0, slice(None))
 
     @pl.when(step == 0)
     def _():
         out_ref[...] = out_part
-        second_grad_ref[...] = second_part
 
     @pl.when(step > 0)
     def _():
         out_ref[...] += out_part
-        second_grad_ref[...] += second_part
-
-
-def mlp_both(second, dz, up, up_bias, down, block=512):
+
+
+def mlp_first(second, dz, up_down, up_bias, owners):
     rows, dim = second.shape
-    width = up.shape[1]
+    width = up_bias.shape[1]
+    shard = dim // owners
+    pieces = width // dim
+    some = owners // pieces
     whole = pl.BlockSpec((rows, dim), lambda j: (0, 0))
     return pl.pallas_call(
-        mlp_kernel,
-        grid=(width // block,),
+        functools.partial(mlp_first_kernel, (some, pieces, dim)),
+        grid=(pieces,),
         in_specs=[
             whole,
             whole,
-            pl.BlockSpec((dim, block), lambda j: (0, j)),
-            pl.BlockSpec((1, block), lambda j: (0, j)),
-            pl.BlockSpec((block, dim), lambda j: (j, 0)),
+            pl.BlockSpec((dim, dim), lambda j: (0, j)),
+            pl.BlockSpec((1, dim), lambda j: (0, j)),
+            pl.BlockSpec((some, shard, width), lambda j: (j, 0, 1)),
         ],
         out_specs=[
             whole,
-            whole,
-            pl.BlockSpec((block, dim), lambda j: (j, 0)),
-            pl.BlockSpec((dim, block), lambda j: (0, j)),
-            pl.BlockSpec((1, block), lambda j: (0, j)),
+            pl.BlockSpec((1, 2, width // owners, dim), lambda j: (j, 0, 0, 0)),
+            pl.BlockSpec((1, 2, width // owners, dim), lambda j: (j, 0, 0, 0)),
+            pl.BlockSpec((rows, dim), lambda j: (0, j)),
+            pl.BlockSpec((1, dim), lambda j: (0, j)),
         ],
         out_shape=[
             jax.ShapeDtypeStruct((rows, dim), F32),
+            jax.ShapeDtypeStruct((4, 2, width // owners, dim), LOW),
+            jax.ShapeDtypeStruct((4, 2, width // owners, dim), LOW),
+            jax.ShapeDtypeStruct((rows, width), LOW),
+            jax.ShapeDtypeStruct((1, width), F32),
+        ],
+        scratch_shapes=[pltpu.VMEM((dim, dim), LOW)],
+        compiler_params=pltpu.CompilerParams(vmem_limit_bytes=VMEM),
+        cost_estimate=cost(19),
+        name="mlp_first",
+    )(second, dz, up_down, up_bias, up_down.reshape(owners, shard, 2 * width))
+
+
+def mlp_second_kernel(second_ref, pre_grad_ref, up_ref, second_grad_ref, kept_ref, sent_ref, up_grad_ref):
+    step = pl.program_id(0)
+    pre_grad = pre_grad_ref[...]
+    up_grad_ref[...] = dot_tn(second_ref[...], pre_grad).astype(LOW)
+    split_cores(up_grad_ref, kept_ref, sent_ref, 0, slice(None))
+    part = dot_nt(pre_grad, up_ref[...])
+
+    @pl.when(step == 0)
+    def _():
+        second_grad_ref[...] = part
+
+    @pl.when(step > 0)
+    def _():
+        second_grad_ref[...] += part
+
+
+def mlp_second(second, pre_grad, up_down, owners):
+    rows, dim = second.shape
+    width = pre_grad.shape[1]
+    shard = dim // owners
+    whole = pl.BlockSpec((rows, dim), lambda j: (0, 0))
+    split = pl.BlockSpec((4, 2, shard, dim), lambda j: (0, 0, 0, j))
+    return pl.pallas_call(
+        mlp_second_kernel,
+        grid=(width // dim,),
+        in_specs=[
+            whole,
+            pl.BlockSpec((rows, dim), lambda j: (0, j)),
+            pl.BlockSpec((dim, dim), lambda j: (0, j)),
+        ],
+        out_specs=[whole, split, split],
+        out_shape=[
             jax.ShapeDtypeStruct((rows, dim), F32),
-            jax.ShapeDtypeStruct((width, dim), LOW),
-            jax.ShapeDtypeStruct((dim, width), LOW),
-            jax.ShapeDtypeStruct((1, width), F32),
-        ],
+            jax.ShapeDtypeStruct((4, 2, shard, width), LOW),
+            jax.ShapeDtypeStruct((4, 2, shard, width), LOW),
+        ],
+        scratch_shapes=[pltpu.VMEM((dim, dim), LOW)],
         compiler_params=pltpu.CompilerParams(vmem_limit_bytes=VMEM),
-        cost_estimate=pl.CostEstimate(
-            flops=12 * rows * dim * width, bytes_accessed=16 * dim * width, transcendentals=3 * rows * width
-        ),
-        name="mlp_both",
-    )(second, dz, up, up_bias, down)
-
-
-def exchange_rows(blocks):
-    here = lax.axis_index("seq")
-    own = lax.dynamic_index_in_dim(blocks, here, 0, keepdims=False)
-    away = lax.dynamic_index_in_dim(blocks, 1 - here, 0, keepdims=False)
-    return own, lax.ppermute(away, "seq", [(0, 1), (1, 0)])
-
-
-def return_rows(rows):
-    here = lax.axis_index("seq")
-    half = rows.shape[0] // 2
-    own = rows[:half]
-    back = lax.ppermute(rows[half:].astype(LOW), "seq", [(0, 1), (1, 0)]).astype(F32)
-    return jnp.where(here == 0, jnp.stack([own, back]), jnp.stack([back, own]))
-
-
-def gather(block):
-    return lax.all_gather(block, "img", axis=0, tiled=True)
-
-
-def reduce(total):
-    part = lax.psum_scatter(total, "img", scatter_dimension=0, tiled=True)
-    return part.astype(F32) + lax.ppermute(part, "seq", [(0, 1), (1, 0)]).astype(F32)
+        cost_estimate=cost(1),
+        name="mlp_second",
+    )(second, pre_grad, up_down)
 
 
 def norm_parts(values):
@@ -546,10 +576,213 @@
     scaled = grad * gain
     across = jnp.mean(scaled, axis=-1, keepdims=True)
     along = jnp.mean(scaled * unit, axis=-1, keepdims=True)
-    return inverse * (scaled - across - unit * along), jnp.sum(grad * unit, axis=0), jnp.sum(grad, axis=0)
-
-
-SMALL_PAD = 256
+    return inverse * (scaled - across - unit * along)
+
+
+def column_sums(values):
+    return jnp.sum(values, axis=0, keepdims=True)
+
+
+def middle_kernel(
+    middle_ref, grad_ref, dz_ref, gain_ref, out_full_ref, merged_ref,
+    middle_grad_ref, merged_grad_ref, out_grad_ref, small_ref,
+):
+    unit, inverse = norm_parts(middle_ref[...])
+    grad = grad_ref[...]
+    upstream = dz_ref[...].astype(F32)
+    middle_grad = upstream + norm_back(unit, inverse, gain_ref[...], grad)
+    middle_grad_ref[...] = middle_grad
+    low = middle_grad.astype(LOW)
+    merged_grad_ref[...] = dot_nt(low, out_full_ref[...]).astype(LOW)
+    out_grad_ref[...] = dot_tn(merged_ref[...], low).astype(LOW)
+    small_ref[0:1] = column_sums(low.astype(F32))
+    small_ref[1:2] = column_sums(grad * unit)
+    small_ref[2:3] = column_sums(grad)
+    small_ref[3:4] = column_sums(upstream)
+
+
+def middle_backward(middle, second_grad, dz, gain, first, merged):
+    rows, dim = middle.shape
+    whole = pl.BlockSpec((rows, dim), lambda j: (0, 0))
+    return pl.pallas_call(
+        middle_kernel,
+        grid=(1,),
+        in_specs=[
+            whole,
+            whole,
+            whole,
+            pl.BlockSpec((1, dim), lambda j: (0, 0)),
+            pl.BlockSpec((dim, dim), lambda j: (0, 3)),
+            whole,
+        ],
+        out_specs=[
+            whole,
+            whole,
+            pl.BlockSpec((dim, dim), lambda j: (0, 0)),
+            pl.BlockSpec((4, dim), lambda j: (0, 0)),
+        ],
+        out_shape=[
+            jax.ShapeDtypeStruct((rows, dim), F32),
+            jax.ShapeDtypeStruct((rows, dim), LOW),
+            jax.ShapeDtypeStruct((dim, dim), LOW),
+            jax.ShapeDtypeStruct((4, dim), F32),
+        ],
+        compiler_params=pltpu.CompilerParams(vmem_limit_bytes=VMEM),
+        cost_estimate=cost(1),
+        name="middle_backward",
+    )(middle, second_grad, dz, gain, first, merged)
+
+
+def last_kernel(
+    inputs_ref, gain_ref, shift_ref, q_low, k_low, v_low, q_high, k_high, v_high, qkv_full_ref,
+    middle_grad_ref, out_grad_ref, small_ref, up_bias_ref, input_grad_ref, kept_ref, sent_ref, total_ref,
+):
+    unit, inverse = norm_parts(inputs_ref[...].astype(F32))
+    gain = gain_ref[...]
+    normed = (unit * gain + shift_ref[...]).astype(LOW)
+    grads = [ref[...] for ref in (q_low, q_high, k_low, k_high, v_low, v_high)]
+    qkv_grad = jnp.concatenate(grads, axis=1)
+    dim = unit.shape[1]
+    normed_grad = dot_nt(qkv_grad, qkv_full_ref[...])
+    input_grad_ref[...] = middle_grad_ref[...] + norm_back(unit, inverse, gain, normed_grad)
+    total_ref[:, : 3 * dim] = dot_tn(normed, qkv_grad).astype(LOW)
+    total_ref[:, 3 * dim : 4 * dim] = out_grad_ref[...]
+    bias_of = column_sums(qkv_grad.astype(F32))
+    rows = [column_sums(normed_grad * unit), column_sums(normed_grad), bias_of[:, :dim], bias_of[:, 2 * dim :]]
+    rows += [small_ref[...], up_bias_ref[...]]
+    taken = sum(row.shape[0] for row in rows)
+    rows.append(jnp.zeros((128 - taken, dim), F32))
+    total_ref[:, 4 * dim : 4 * dim + 128] = jnp.concatenate(rows, axis=0).T.astype(LOW)
+    total_ref[:, 4 * dim + 128 :] = jnp.zeros((dim, SMALL_PAD - 128), LOW)
+    split_cores(total_ref, kept_ref, sent_ref, 0, slice(None))
+
+
+def last_backward(inputs, gain, shift, grads_low, grads_high, first, middle_grad, out_grad, small, up_bias, owners):
+    rows, dim = inputs.shape
+    columns = 4 * dim + SMALL_PAD
+
+    def whole(*shape):
+        return pl.BlockSpec(shape, lambda j: (0,) * len(shape))
+
+    split = jax.ShapeDtypeStruct((4, 2, dim // owners, columns), LOW)
+    return pl.pallas_call(
+        last_kernel,
+        grid=(1,),
+        in_specs=[whole(rows, dim), whole(1, dim), whole(1, dim)]
+        + [whole(*g.shape) for g in (*grads_low, *grads_high)]
+        + [whole(dim, 3 * dim), whole(rows, dim), whole(dim, dim), whole(*small.shape), whole(*up_bias.shape)],
+        out_specs=[whole(rows, dim), whole(*split.shape), whole(*split.shape)],
+        out_shape=[jax.ShapeDtypeStruct((rows, dim), F32), split, split],
+        scratch_shapes=[pltpu.VMEM((dim, columns), LOW)],
+        compiler_params=pltpu.CompilerParams(vmem_limit_bytes=VMEM),
+        cost_estimate=cost(1),
+        name="last_backward",
+    )(inputs, gain, shift, *grads_low, *grads_high, first, middle_grad, out_grad, small, up_bias)
+
+
+def own_and_away(blocks):
+    here = lax.axis_index("seq")
+    own = lax.dynamic_index_in_dim(blocks, here, 0, keepdims=False)
+    return own, lax.dynamic_index_in_dim(blocks, 1 - here, 0, keepdims=False)
+
+
+def both_images(own, back):
+    here = lax.axis_index("seq")
+    back = back.astype(F32)
+    return jnp.where(here == 0, jnp.stack([own, back]), jnp.stack([back, own]))
+
+
+def gather(block):
+    return lax.all_gather(block, "img", axis=0, tiled=True)
+
+
+def place():
+    img = lax.axis_index("img")
+    return img // 4, (img // 2) % 2, img % 2, lax.axis_index("seq")
+
+
+def swap(block, z=0, x=0, core=0, y=0):
+    bits = z * 8 + x * 4 + core * 2 + y
+    return lax.ppermute(block, ("img", "seq"), [(i, i ^ bits) for i in range(32)])
+
+
+def assemble_kernel(small_at, *refs):
+    refs, out_ref, small_ref = refs[:-2], refs[-2], refs[-1]
+    here_z, here_x, here_core, here_y = place()
+    half = out_ref.shape[2] // 2
+    for index, ref in enumerate(refs):
+        x, y, core = index // 4 % 2, index // 2 % 2, index % 2
+        columns = pl.ds(pl.multiple_of((here_y ^ y) * half, half), half)
+        for z in range(4):
+            owner = (here_z ^ z) * 4 + (here_x ^ x) * 2 + (here_core ^ core)
+            out_ref[owner, :, columns] = ref[z]
+    small = jnp.concatenate([out_ref[i, :, small_at : small_at + 128] for i in range(16)], axis=0)
+    small_ref[...] = small.astype(F32).T[:16]
+
+
+def gather_links(block, rows):
+    shard, columns = block.shape
+    half = columns // 2
+    own = lax.dynamic_slice_in_dim(block, lax.axis_index("seq") * half, half, 1)
+    rows = swap(rows, y=1)
+    line = jnp.stack([own] + [swap(own, z=z) for z in (1, 2, 3)])
+    line, rows = tie(line, rows)
+    across = swap(line, x=1)
+    plane = [line, swap(line, y=1), across, swap(across, y=1)]
+    refs = []
+    for part in plane:
+        refs += [part, swap(part, core=1)]
+    whole, small = pl.pallas_call(
+        functools.partial(assemble_kernel, columns - SMALL_PAD),
+        out_shape=[
+            jax.ShapeDtypeStruct((16, shard, columns), LOW),
+            jax.ShapeDtypeStruct((16, 16 * shard), F32),
+        ],
+        compiler_params=pltpu.CompilerParams(vmem_limit_bytes=VMEM),
+        name="assemble",
+    )(*refs)
+    return whole.reshape(16 * shard, columns), small, rows
+
+
+def total(pieces):
+    result = pieces[0].astype(F32)
+    for piece in pieces[1:]:
+        result = result + piece.astype(F32)
+    return result.astype(LOW)
+
+
+def plane_pieces(paired):
+    _, x, _, y = place()
+    rows, half = paired.shape[2], paired.shape[3] // 2
+
+    def part(x_index, y_index):
+        return lax.dynamic_slice(paired, (0, x_index, 0, y_index * half), (4, 1, rows, half))[:, 0]
+
+    return [part(x, y), part(1 - x, y), part(x, 1 - y), part(1 - x, 1 - y)]
+
+
+def plane_swaps(pieces):
+    return [pieces[0], swap(pieces[1], x=1), swap(pieces[2], y=1), swap(pieces[3], x=1, y=1)]
+
+
+def line_pieces(line):
+    z = place()[0]
+    return [lax.dynamic_index_in_dim(line, z ^ step, 0, keepdims=False) for step in range(4)]
+
+
+def line_swaps(pieces):
+    return [pieces[0]] + [swap(pieces[step], z=step) for step in (1, 2, 3)]
+
+
+def join_halves(own, other):
+    here = lax.axis_index("seq")
+    return jnp.where(
+        here == 0, jnp.concatenate([own, other], axis=1), jnp.concatenate([other, own], axis=1)
+    ).astype(F32)
+
+
+def tie(*values):
+    return lax.optimization_barrier(values)
 
 
 def image_body(
@@ -560,78 +793,102 @@
     owners = lax.axis_size("img")
     shard = dim // owners
     width = bias_up.shape[0] * owners
-    smalls = (ln1_gain, ln1_bias, bias_q, bias_v, bias_out, ln2_gain, ln2_bias, bias_down, bias_up)
-    sizes = [s.shape[0] for s in smalls]
-    columns = sum(sizes) // shard
-
-    packed = jnp.concatenate(smalls).reshape(shard, columns)
-    first = gather(jnp.concatenate([w_qkv, jnp.pad(packed, ((0, 0), (0, 128 - columns)))], axis=1))
-    qkv_full = first[:, : 3 * dim]
-    small_full = first[:, 3 * dim : 3 * dim + columns].reshape(owners, shard * columns).astype(F32)
-    cuts = [sum(sizes[:i]) for i in range(len(sizes) + 1)]
-    (gain_one, shift_one, query_bias, value_bias, out_bias, gain_two, shift_two, down_bias, up_bias) = [
-        small_full[:, a:b].reshape(-1) for a, b in zip(cuts[:-1], cuts[1:])
-    ]
-    second_gather = gather(jnp.concatenate([w_out, w_up], axis=1))
-    out_full, up_full = second_gather[:, :dim], second_gather[:, dim:]
-    down_full = gather(w_down)
-
+    pieces = width // dim
+
+    up_down = gather(
+        jnp.concatenate([w_up, w_down.reshape(pieces, shard, dim).swapaxes(0, 1).reshape(shard, width)], axis=1)
+    )
+    rows_small = jnp.concatenate(
+        [jnp.stack([ln1_gain, ln1_bias, bias_q, bias_v, bias_out, ln2_gain, ln2_bias, bias_down])]
+        + [bias_up.reshape(pieces, shard)]
+    )
+    count = rows_small.shape[0]
+    padding = jnp.pad(rows_small.T, ((0, 0), (0, SMALL_PAD - count)))
     mask_rows = jnp.broadcast_to(
         jnp.pad(token_mask.astype(LOW), ((0, 0), (0, dim - shard_rows)))[:, None, :], (2, 16, dim)
     )
-    own, away = exchange_rows(jnp.concatenate([tokens, mask_rows], axis=1))
+    own, away = own_and_away(jnp.concatenate([tokens, mask_rows], axis=1))
+    first, small, away = gather_links(jnp.concatenate([w_qkv, w_out, padding], axis=1), away)
+    masked = jnp.where(token_mask[..., None] > 0, cotangent, jnp.zeros_like(cotangent))
+    own_in, away_in = own_and_away(masked)
+    first, away_in = tie(first, away_in)
+    down_in = jnp.concatenate([own_in, swap(away_in, y=1)], axis=0)
+    qkv_full, out_full = first[:, : 3 * dim], first[:, 3 * dim : 4 * dim]
+    gain_one, shift_one, query_bias, value_bias, out_bias, gain_two, shift_two, down_bias = [
+        small[i : i + 1] for i in range(8)
+    ]
+    up_bias = small[8:count].reshape(pieces, owners, shard).swapaxes(0, 1).reshape(1, width)
+
     both = jnp.stack([own, away])
-    inputs = both[:, :shard_rows].reshape(2 * shard_rows, dim).astype(F32)
+    inputs_low = both[:, :shard_rows].reshape(2 * shard_rows, dim)
+    inputs = inputs_low.astype(F32)
     mask_column = both[:, shard_rows, :shard_rows].astype(F32).reshape(2 * shard_rows, 1)
-    masked = jnp.where(token_mask[..., None] > 0, cotangent, jnp.zeros_like(cotangent))
-    down_in = jnp.concatenate(exchange_rows(masked), axis=0)
-
-    unit_one, inverse_one = norm_parts(inputs)
+    unit_one, _ = norm_parts(inputs)
     normed = (unit_one * gain_one + shift_one).astype(LOW)
-    qkv_bias = jnp.concatenate([query_bias, jnp.zeros_like(query_bias), value_bias])
+    qkv_bias = jnp.concatenate([query_bias, jnp.zeros_like(query_bias), value_bias], axis=1)
     qkv = (dot_nn(normed, qkv_full) + qkv_bias).astype(LOW)
     merged, logs = attention_forward(qkv, mask_column)
     middle = inputs + dot_nn(merged, out_full) + out_bias
-    unit_two, inverse_two = norm_parts(middle)
+    unit_two, _ = norm_parts(middle)
     second = (unit_two * gain_two + shift_two).astype(LOW)
-    mlp_out, second_grad, grad_down, grad_up, grad_up_bias = mlp_both(
-        second, down_in, up_full, up_bias.reshape(1, width), down_full
-    )
+    mlp_out, down_kept, down_sent, pre_grad, grad_up_bias = mlp_first(second, down_in, up_down, up_bias, owners)
     output = middle + mlp_out + down_bias
-    upstream = down_in.astype(F32)
-    grad_down_bias = jnp.sum(upstream, axis=0)
-    middle_ln, grad_gain_two, grad_shift_two = norm_back(unit_two, inverse_two, gain_two, second_grad)
-    middle_grad = upstream + middle_ln
-    branch_grad = middle_grad.astype(LOW)
-    grad_out = dot_tn(merged, branch_grad).astype(LOW)
-    grad_out_bias = jnp.sum(branch_grad.astype(F32), axis=0)
-    merged_grad = dot_nt(branch_grad, out_full).astype(LOW)
-    query_grad, key_grad, value_grad = attention_backward(qkv, mask_column, logs, merged_grad)
-    qkv_grad = jnp.concatenate([query_grad, key_grad, value_grad], axis=1)
-    grad_qkv = dot_tn(normed, qkv_grad).astype(LOW)
-    grad_query_bias = jnp.sum(query_grad.astype(F32), axis=0)
-    grad_value_bias = jnp.sum(value_grad.astype(F32), axis=0)
-    normed_grad = dot_nt(qkv_grad, qkv_full)
-    input_ln, grad_gain_one, grad_shift_one = norm_back(unit_one, inverse_one, gain_one, normed_grad)
-    input_grad = middle_grad + input_ln
-
-    small_grads = (
-        grad_gain_one, grad_shift_one, grad_query_bias, grad_value_bias, grad_out_bias,
-        grad_gain_two, grad_shift_two, grad_down_bias, grad_up_bias.reshape(-1),
-    )
-    small_packed = jnp.concatenate([g.reshape(owners, -1) for g in small_grads], axis=1)
-    small_packed = jnp.pad(small_packed.reshape(dim, columns), ((0, 0), (0, SMALL_PAD - columns))).astype(LOW)
-    down_sum = reduce(grad_down)
-    up_sum = reduce(jnp.concatenate([grad_out, grad_up], axis=1))
-    qkv_sum = reduce(jnp.concatenate([grad_qkv, small_packed], axis=1))
-    small_sum = qkv_sum[:, 3 * dim : 3 * dim + columns].reshape(-1)
-    (sum_gain_one, sum_shift_one, sum_query, sum_value, sum_out, sum_gain_two, sum_shift_two, sum_down, sum_up) = [
-        small_sum[a:b] for a, b in zip(cuts[:-1], cuts[1:])
-    ]
+    output_own, output_away = output[:shard_rows], output[shard_rows:].astype(LOW)
+    pre_grad, output_away, down_sent = tie(pre_grad, output_away, down_sent)
+    output_back, down_sent = swap(output_away, y=1), swap(down_sent, core=1)
+    second_grad, up_kept, up_sent = mlp_second(second, pre_grad, up_down, owners)
+    second_grad, up_kept, up_sent, output_back, down_sent = tie(second_grad, up_kept, up_sent, output_back, down_sent)
+    down_pieces = plane_pieces(total([down_kept, down_sent]))
+    second_grad, up_sent, *down_pieces = tie(second_grad, up_sent, *down_pieces)
+    down_pieces, up_sent = plane_swaps(down_pieces), swap(up_sent, core=1)
+    middle_grad, merged_grad, grad_out, small_grads = middle_backward(
+        middle, second_grad, down_in, gain_two, first, merged
+    )
+    middle_grad, merged_grad, grad_out, small_grads, up_sent = tie(
+        middle_grad, merged_grad, grad_out, small_grads, up_sent
+    )
+    up_pieces = plane_pieces(total([up_kept, up_sent]))
+    merged_grad, *up_pieces = tie(merged_grad, *up_pieces)
+    up_pieces = plane_swaps(up_pieces)
+    pairs = HEADS // 2
+    grads_low = attention_backward(qkv, mask_column, logs, merged_grad, 0, pairs // 2)
+    tied = tie(merged_grad, *grads_low, *down_pieces)
+    merged_grad, grads_low, down_pieces = tied[0], tied[1:4], tied[4:]
+    down_pieces = line_pieces(total(down_pieces))
+    merged_grad, *down_pieces = tie(merged_grad, *down_pieces)
+    down_pieces = line_swaps(down_pieces)
+    grads_high = attention_backward(qkv, mask_column, logs, merged_grad, pairs // 2, pairs - pairs // 2)
+    tied = tie(*grads_high, *down_pieces)
+    grads_high, down_own = tied[:3], total(tied[3:])
+    up_bias_rows = grad_up_bias.reshape(owners, pieces, shard).swapaxes(0, 1).reshape(pieces, dim)
+    up_bias_rows, down_own = tie(up_bias_rows, down_own)
+    down_other = swap(down_own, y=1)
+    input_grad, last_kept, last_sent = last_backward(
+        inputs_low, gain_one, shift_one, grads_low, grads_high, first, middle_grad, grad_out, small_grads,
+        up_bias_rows, owners,
+    )
+    tied = tie(input_grad, last_kept, last_sent, down_other, *up_pieces)
+    input_grad, last_kept, last_sent, down_other = tied[:4]
+    up_pieces = line_pieces(total(tied[4:]))
+    last_sent = swap(last_sent, core=1)
+    last_pieces = plane_pieces(total([last_kept, last_sent]))
+    tied = tie(*last_pieces, *up_pieces)
+    last_pieces, up_pieces = plane_swaps(tied[:4]), line_swaps(tied[4:])
+    tied = tie(input_grad, *last_pieces, *up_pieces)
+    input_grad, last_pieces, up_own = tied[0], line_pieces(total(tied[1:5])), total(tied[5:])
+    input_away = input_grad[shard_rows:].astype(LOW)
+    tied = tie(input_away, up_own, *last_pieces)
+    input_away, up_own, last_pieces = tied[0], tied[1], tied[2:]
+    last_pieces = line_swaps(last_pieces)
+    input_back, up_other = swap(input_away, y=1), swap(up_own, y=1)
+    last_own = total(last_pieces)
+    last_sum = join_halves(last_own, swap(last_own, y=1))
+    smalls = last_sum[:, 4 * dim : 4 * dim + count].T
     return (
-        return_rows(output), return_rows(input_grad), sum_gain_one, sum_shift_one, qkv_sum[:, : 3 * dim],
-        sum_query, sum_value, up_sum[:, :dim], sum_out, sum_gain_two, sum_shift_two, up_sum[:, dim:],
-        sum_up, down_sum, sum_down,
+        both_images(output_own, output_back), both_images(input_grad[:shard_rows], input_back),
+        smalls[0], smalls[1], last_sum[:, : 3 * dim], smalls[2], smalls[3], last_sum[:, 3 * dim : 4 * dim],
+        smalls[4], smalls[5], smalls[6], join_halves(up_own, up_other), smalls[8:].reshape(-1),
+        join_halves(down_own, down_other), smalls[7],
     )
 
 

time: 527 us -> 298 us (0.57)
  waiting for transfers between devices: 324 us -> 83.6 us
  starting transfers between devices: 10.6 us -> 50.5 us
  Pallas kernels: 66 us -> 99.5 us
  local copies, waits for them, and re-layouts: 42.6 us -> 16.4 us
  other arithmetic: 43.2 us -> 19.3 us
  matrix products: 25.4 us -> 8.91 us
    reduce_scatter x3 -> x0, waiting for transfers between devices: 189 us -> none  [reduce(): part = lax.psum_scatter(total, 'img', scatter_dimension=0, tiled=True)]
    all_gather x3 -> x1, waiting for transfers between devices: 93 us -> 4.39 us  [gather(): return lax.all_gather(block, 'img', axis=0, tiled=True)]
    ppermute x7 -> x38, starting transfers between devices: 10.3 us -> 50.4 us  [swap(): lax.ppermute(block, ('img', 'seq'), [(i, i ^ bits) for i in range(32)])]
    ppermute x7 -> x38, waiting for transfers between devices: 40.6 us -> 79.2 us  [swap(): lax.ppermute(block, ('img', 'seq'), [(i, i ^ bits) for i in range(32)])]
    pallas_call x1 -> x5, Pallas kernels: 28.3 us -> 59.4 us  [the longest x1 20.4 us: mlp_first(): pl.pallas_call(functools.partial(mlp_first_kernel, (some, pieces, dim)),...]
    dot_general x4 -> x0, matrix products: 16.9 us -> none  [the longest x2 8.83 us: dot_tn(): lax.dot_general(left, right, (((0,), (0,)), ((), ())), preferred_element_...]
    reduce_sum x7 -> x0, other arithmetic: 13 us -> none  [the longest x1 4.98 us: norm_back(): jnp.sum(grad * unit, axis=0)]
    slice x19 -> x9, local copies, waits for them, and re-layouts: 16.2 us -> 4.94 us  [the longest x1 1.65 us: image_body(): small[i:i + 1]]
  transfers between devices with their start and end apart: 13 -> 39, of which waited for: 11 -> 17; matrix products, arithmetic and copies ran while one was open for 11% -> 11% of each run, Pallas kernels for 3% -> 27%
where the time goes in v2:
time: 298 us; the launch traced here: 293 us
  Pallas kernels  99.5 us (33%)
  waiting for transfers between devices  83.6 us (28%)
  starting transfers between devices  50.5 us (17%)
  other arithmetic  19.3 us (6%)
  local copies, waits for them, and re-layouts  16.4 us (6%)
  between operations  15.1 us (5%)
  matrix products  8.91 us (3%)
    ppermute x38, waiting for transfers between devices, swap(): lax.ppermute(block, ('img', 'seq'), [(i, i ^ bits) for i in range(32)])  79.2 us
    ppermute x38, starting transfers between devices, swap(): lax.ppermute(block, ('img', 'seq'), [(i, i ^ bits) for i in range(32)])  50.4 us
    pallas_call x2, Pallas kernels, attention_backward(): pl.pallas_call(functools.partial(attention_backward_kernel, size ** (-0.5...  26.7 us
    pallas_call x1, Pallas kernels, mlp_first(): pl.pallas_call(functools.partial(mlp_first_kernel, (some, pieces, dim)),...  20.4 us
    pallas_call x1, Pallas kernels, mlp_second(): pl.pallas_call(mlp_second_kernel, grid=(width // dim,), in_specs=[whole,...  13.6 us
    pallas_call x1, Pallas kernels, attention_forward(): pl.pallas_call(functools.partial(attention_forward_kernel, size ** (-0.5)...  13.4 us
    pallas_call x1, Pallas kernels, last_backward(): pl.pallas_call(last_kernel, grid=(1,), in_specs=[whole(rows, dim), whole(...  13 us
    dot_general x2, matrix products, dot_nn(): lax.dot_general(left, right, (((1,), (0,)), ((), ())), preferred_element_...  8.91 us
  transfers between devices with their start and end apart: 39, of which 17 were waited for; matrix products, arithmetic and copies ran while one was open for 11% of the time, Pallas kernels for 27%

profile of v2, /device:TPU:0, one launch (start us, length us, event | category | flops | bytes accessed | tf_op | source)
XLA Modules:
  0.0 293.2 jit_solution(12776052951896476201)
XLA Ops:
  8.6 1.9 pad_maximum_fusion.2
  10.7 3.0 %collective-permute-start.3 = (bf16[344,768]{1,0:T(8,128)(2,1)S(1)}, bf16[344,768]{1,0:T(8,128)(2,1)S(1)}, u32[]{:S(2)}, u32[]{:S(2)}) collective-permute-start(bf16[344,768]{1,0:T(8,128)(2,1)S(1)} %get-tuple-element.256), channel_id=1, source_target_pairs={{0,1},{1,0},{2,3},{3,2},{4,5},{5,4},{6,7},{7,6},{8,9},{9,8},{10,11... | collective-permute-start | bytes 1585160 | tf_op jit(solution)/shard_map/ppermute | solution.py:706
  15.4 2.7 collective-permute-start.1
  18.1 1.6 collective-permute-start
  19.9 11.7 %collective-permute-done.1 = bf16[48,1664]{1,0:T(8,128)(2,1)S(1)} collective-permute-done((bf16[48,1664]{1,0:T(8,128)(2,1)S(1)}, bf16[48,1664]{1,0:T(8,128)(2,1)S(1)}, u32[]{:S(2)}, u32[]{:S(2)}) %collective-permute-start.1) | collective-permute-done | bytes 159776 | tf_op jit(solution)/shard_map/ppermute | solution.py:706
  31.6 3.3 %collective-permute-done.2 = bf16[48,1664]{1,0:T(8,128)(2,1)S(1)} collective-permute-done((bf16[48,1664]{1,0:T(8,128)(2,1)S(1)}, bf16[48,1664]{1,0:T(8,128)(2,1)S(1)}, u32[]{:S(2)}, u32[]{:S(2)}) %collective-permute-start.2) | collective-permute-done | bytes 159776 | tf_op jit(solution)/shard_map/ppermute | solution.py:706
  35.0 1.3 collective-permute-start.7
  36.3 10.8 %collective-permute-done.7.refs_4_ = bf16[4,48,1664]{2,1,0:T(8,128)(2,1)} collective-permute-done((bf16[4,48,1664]{2,1,0:T(8,128)(2,1)S(1)}, bf16[4,48,1664]{2,1,0:T(8,128)(2,1)}, u32[]{:S(2)}, u32[]{:S(2)}) %collective-permute-start.7) | collective-permute-done | bytes 639008 | tf_op jit(solution)/shard_map/ppermute | solution.py:706
  48.8 2.6 collective-permute-done.5.refs_2_
  51.4 10.5 %collective-permute-done.9.refs_6_ = bf16[4,48,1664]{2,1,0:T(8,128)(2,1)} collective-permute-done((bf16[4,48,1664]{2,1,0:T(8,128)(2,1)}, bf16[4,48,1664]{2,1,0:T(8,128)(2,1)}, u32[]{:S(2)}, u32[]{:S(2)}) %collective-permute-start.9) | collective-permute-done | bytes 639008 | tf_op jit(solution)/shard_map/ppermute | solution.py:706
  64.3 5.2 %assemble.1 = (bf16[16,48,3328]{2,1,0:T(8,128)(2,1)}, f32[16,768]{1,0:T(8,128)}) custom-call(bf16[4,48,1664]{2,1,0:T(8,128)(2,1)} %copy-done.4, bf16[4,48,1664]{2,1,0:T(8,128)(2,1)} %collective-permute-done.4.refs_1_, bf16[4,48,1664]{2,1,0:T(8,128)(2,1)} %collective-permute-done.5.refs_2_, bf16[4,48,1664]{2,1,0:T(8,128)(2,1)} %collective-permute-done.6.refs_3_, ...), custom_call_target="tpu_custom_call" | custom-call | tf_op jit(solution)/shard_map/assemble/pallas_call | solution.py:735
  71.3 1.6 slice_reduce_fusion.8
  73.0 6.4 %add_convert_fusion.query_ref.key_ref.value_ref = bf16[656,2304]{1,0:T(8,128)(2,1)} fusion(bf16[768,3328]{1,0:T(8,128)(2,1)} %bitcast.95, f32[2304]{0:T(1024)S(1)} %fusion.26, bf16[656,768]{1,0:T(8,128)(2,1)S(1)} %bitcast.100, f32[768]{0:T(1024)S(1)} %get-tuple-element.229, f32[768]{0:T(1024)S(1)} %get-tuple-element.228, f32[656]{0:T(1024)S(1)} %rsqrt.20, ...), kind=kOutput, calls=%fused_computation | convolution fusion | flops 2327592960 | bytes 7590016 | tf_op jit(solution)/shard_map/dot_general | solution.py:331
  79.3 13.4 %attention_forward.1 = (bf16[656,768]{1,0:T(8,128)(2,1)}, f32[6,2,656]{2,1,0:T(2,128)}) custom-call(bf16[656,2304]{1,0:T(8,128)(2,1)} %add_convert_fusion.query_ref.key_ref.value_ref, bf16[656,2304]{1,0:T(8,128)(2,1)} %add_convert_fusion.query_ref.key_ref.value_ref, bf16[656,2304]{1,0:T(8,128)(2,1)} %add_convert_fusion.query_ref.key_ref.value_ref, ...), custom_call_target="tpu_custom_call" | custom-call | flops 14949999616 | bytes 1 | tf_op jit(solution)/shard_map/attention_forward/pallas_call | solution.py:365
  92.7 2.5 fusion.5.middle_ref
  95.8 1.4 add_convert_fusion.4.second_ref
  97.2 2.1 pad_maximum_fusion.dz_ref
  99.3 4.4 %all-gather.2.cloned.1.call-done.up_ref = bf16[768,6144]{1,0:T(8,128)(2,1)} async-done(((bf16[48,6144]{1,0:T(8,128)(2,1)}), bf16[768,6144]{1,0:T(8,128)(2,1)}) %all-gather.2.cloned.1.call-update) | async-done | bytes 9437200 | tf_op jit(solution)/shard_map/all_gather | solution.py:696
  103.7 20.4 %mlp_first.1 = (f32[656,768]{1,0:T(8,128)}, bf16[4,2,192,768]{3,2,1,0:T(8,128)(2,1)}, bf16[4,2,192,768]{3,2,1,0:T(8,128)(2,1)}, bf16[656,3072]{1,0:T(8,128)(2,1)}, f32[1,3072]{1,0:T(1,128)}) custom-call(bf16[656,768]{1,0:T(8,128)(2,1)} %add_convert_fusion.4.second_ref, bf16[656,768]{1,0:T(8,128)(2,1)} %pad_maximum_fusion.dz_ref, ...), custom_call_target="tpu_custom_call" | custom-call | flops 21849999360 | bytes 1 | tf_op jit(solution)/shard_map/mlp_first/pallas_call | solution.py:495
  124.1 1.8 add_add_fusion
  128.1 13.6 %mlp_second.1 = (f32[656,768]{1,0:T(8,128)}, bf16[4,2,48,3072]{3,2,1,0:T(8,128)(2,1)}, bf16[4,2,48,3072]{3,2,1,0:T(8,128)(2,1)}) custom-call(bf16[656,768]{1,0:T(8,128)(2,1)} %add_convert_fusion.4.second_ref, bf16[656,3072]{1,0:T(8,128)(2,1)} %get-tuple-element.131.pre_grad_ref, bf16[768,6144]{1,0:T(8,128)(2,1)} %all-gather.2.cloned.1.call-done.up_ref), custom_call_target="tpu_custom_call" | custom-call | flops 1150000000 | bytes 1 | tf_op jit(solution)/shard_map/mlp_second/pallas_call | solution.py:548
  142.5 1.5 dynamic-slice_bitcast_fusion.8
  147.5 7.3 %middle_backward.1 = (f32[656,768]{1,0:T(8,128)}, bf16[656,768]{1,0:T(8,128)(2,1)}, bf16[768,768]{1,0:T(8,128)(2,1)}, f32[4,768]{1,0:T(4,128)}) custom-call(f32[656,768]{1,0:T(8,128)} %copy-done, f32[656,768]{1,0:T(8,128)} %get-tuple-element.142.grad_ref, bf16[656,768]{1,0:T(8,128)(2,1)} %pad_maximum_fusion.dz_ref, f32[1,768]{1,0:T(1,128)} %get-tuple-element.271.gain_ref, ...), custom_call_target="tpu_custom_call" | custom-call | flops 1150000000 | bytes 1 | tf_op jit(solution)/shard_map/middle_backward/pallas_call | solution.py:607
  155.9 13.3 %attention_backward.2 = (bf16[656,384]{1,0:T(8,128)(2,1)}, bf16[656,384]{1,0:T(8,128)(2,1)}, bf16[656,384]{1,0:T(8,128)(2,1)}) custom-call(bf16[656,2304]{1,0:T(8,128)(2,1)} %add_convert_fusion.query_ref.key_ref.value_ref, bf16[656,2304]{1,0:T(8,128)(2,1)} %add_convert_fusion.query_ref.key_ref.value_ref, ...), custom_call_target="tpu_custom_call" | custom-call | flops 1150000000 | bytes 1 | tf_op jit(solution)/shard_map/attention_backward/pallas_call | solution.py:429
  169.2 3.2 %collective-permute-done.16 = bf16[4,192,384]{2,1,0:T(8,128)(2,1)S(1)} collective-permute-done((bf16[4,192,384]{2,1,0:T(8,128)(2,1)}, bf16[4,192,384]{2,1,0:T(8,128)(2,1)S(1)}, u32[]{:S(2)}, u32[]{:S(2)}) %collective-permute-start.16) | collective-permute-done | bytes 589856 | tf_op jit(solution)/shard_map/ppermute | solution.py:706
  174.0 10.2 %collective-permute-start.18 = (bf16[192,384]{1,0:T(8,128)(2,1)S(1)}, bf16[192,384]{1,0:T(8,128)(2,1)S(1)}, u32[]{:S(2)}, u32[]{:S(2)}) collective-permute-start(bf16[192,384]{1,0:T(8,128)(2,1)S(1)} %get-tuple-element.173), channel_id=1, source_target_pairs={{0,8},{1,9},{2,10},{3,11},{4,12},{5,13},{6,14},{7,15},{8,0},{9,1},... | collective-permute-start | bytes 442376 | tf_op jit(solution)/shard_map/ppermute | solution.py:706
  186.0 1.7 collective-permute-start.24
  187.7 3.8 %collective-permute-start.19 = (bf16[192,384]{1,0:T(8,128)(2,1)S(1)}, bf16[192,384]{1,0:T(8,128)(2,1)S(1)}, u32[]{:S(2)}, u32[]{:S(2)}) collective-permute-start(bf16[192,384]{1,0:T(8,128)(2,1)S(1)} %get-tuple-element.174), channel_id=1, source_target_pairs={{0,16},{1,17},{2,18},{3,19},{4,20},{5,21},{6,22},{7,23},{8,24},{9,... | collective-permute-start | bytes 442376 | tf_op jit(solution)/shard_map/ppermute | solution.py:706
  191.5 1.4 collective-permute-start.20
  194.9 13.4 %attention_backward.3 = (bf16[656,384]{1,0:T(8,128)(2,1)}, bf16[656,384]{1,0:T(8,128)(2,1)}, bf16[656,384]{1,0:T(8,128)(2,1)}) custom-call(bf16[656,2304]{1,0:T(8,128)(2,1)} %add_convert_fusion.query_ref.key_ref.value_ref, bf16[656,2304]{1,0:T(8,128)(2,1)} %add_convert_fusion.query_ref.key_ref.value_ref, ...), custom_call_target="tpu_custom_call" | custom-call | flops 1150000000 | bytes 1 | tf_op jit(solution)/shard_map/attention_backward/pallas_call | solution.py:429
  208.8 13.0 %last_backward.1 = (f32[656,768]{1,0:T(8,128)}, bf16[4,2,48,3328]{3,2,1,0:T(8,128)(2,1)}, bf16[4,2,48,3328]{3,2,1,0:T(8,128)(2,1)}) custom-call(bf16[656,768]{1,0:T(8,128)(2,1)} %bitcast.101, f32[1,768]{1,0:T(1,128)} %get-tuple-element.273.gain_ref, f32[1,768]{1,0:T(1,128)} %get-tuple-element.272.shift_ref, bf16[656,384]{1,0:T(8,128)(2,1)} %get-tuple-element.160.q_low, ...), custom_call_target="tpu_custom_call" | custom-call | flops 1150000000 | bytes 1 | tf_op jit(solution)/shard_map/last_backward/pallas_call | solution.py:668
  222.0 1.9 add_convert_fusion.6
  223.9 3.1 %collective-permute-done.25 = bf16[4,2,48,3328]{3,2,1,0:T(8,128)(2,1)S(1)} collective-permute-done((bf16[4,2,48,3328]{3,2,1,0:T(8,128)(2,1)}, bf16[4,2,48,3328]{3,2,1,0:T(8,128)(2,1)S(1)}, u32[]{:S(2)}, u32[]{:S(2)}) %collective-permute-start.25) | collective-permute-done | bytes 2555936 | tf_op jit(solution)/shard_map/ppermute | solution.py:706
  227.8 1.5 collective-permute-start.26
  231.5 1.4 collective-permute-start.29
  232.9 1.7 collective-permute-start.30
  234.6 3.9 %collective-permute-done.29 = bf16[48,1536]{1,0:T(8,128)(2,1)S(1)} collective-permute-done((bf16[48,1536]{1,0:T(8,128)(2,1)S(1)}, bf16[48,1536]{1,0:T(8,128)(2,1)S(1)}, u32[]{:S(2)}, u32[]{:S(2)}) %collective-permute-start.29) | collective-permute-done | bytes 147488 | tf_op jit(solution)/shard_map/ppermute | solution.py:706
  238.5 2.4 collective-permute-start.31
  240.9 1.4 maximum_select_fusion
  243.2 3.1 %collective-permute-done.30 = bf16[48,1536]{1,0:T(8,128)(2,1)S(1)} collective-permute-done((bf16[48,1536]{1,0:T(8,128)(2,1)S(1)}, bf16[48,1536]{1,0:T(8,128)(2,1)S(1)}, u32[]{:S(2)}, u32[]{:S(2)}) %collective-permute-start.30) | collective-permute-done | bytes 147488 | tf_op jit(solution)/shard_map/ppermute | solution.py:706
  246.3 11.4 %collective-permute-done.27 = bf16[4,48,1664]{2,1,0:T(8,128)(2,1)S(1)} collective-permute-done((bf16[4,48,1664]{2,1,0:T(8,128)(2,1)S(1)}, bf16[4,48,1664]{2,1,0:T(8,128)(2,1)S(1)}, u32[]{:S(2)}, u32[]{:S(2)}) %collective-permute-start.27) | collective-permute-done | bytes 639008 | tf_op jit(solution)/shard_map/ppermute | solution.py:706
  257.7 1.4 collective-permute-done.28
  260.8 1.6 collective-permute-start.33
  263.6 1.6 collective-permute-start.35
  267.3 8.5 %collective-permute-done.34 = bf16[48,1664]{1,0:T(8,128)(2,1)S(1)} collective-permute-done((bf16[48,1664]{1,0:T(8,128)(2,1)S(1)}, bf16[48,1664]{1,0:T(8,128)(2,1)S(1)}, u32[]{:S(2)}, u32[]{:S(2)}) %collective-permute-start.34) | collective-permute-done | bytes 159776 | tf_op jit(solution)/shard_map/ppermute | solution.py:706
  275.8 1.6 collective-permute-start.36
  278.4 2.8 collective-permute-done.36
  284.5 1.4 maximum_select_fusion.1
  (163 shorter events, 36.8 us)
Async XLA Ops:
  7.2 96.5 %all-gather.2.cloned.1.call-start = ((), (), s32[]{:S(2)}) async-start(), calls=%async_computation | async-start | bytes 10027008 | tf_op jit(solution)/shard_map/all_gather | solution.py:696
  10.5 36.7 %copy-start.10 = (bf16[2,328,768]{2,1,0:T(8,128)(2,1)S(1)}, bf16[2,328,768]{2,1,0:T(8,128)(2,1)}, u32[]{:S(2)}) copy-start(bf16[2,328,768]{2,1,0:T(8,128)(2,1)} %param.31) | copy-start | bytes 3022852
  10.7 24.3 %collective-permute-start.3 = (bf16[344,768]{1,0:T(8,128)(2,1)S(1)}, bf16[344,768]{1,0:T(8,128)(2,1)S(1)}, u32[]{:S(2)}, u32[]{:S(2)}) collective-permute-start(bf16[344,768]{1,0:T(8,128)(2,1)S(1)} %get-tuple-element.256), channel_id=1, source_target_pairs={{0,1},{1,0},{2,3},{3,2},{4,5},{5,4},{6,7},{7,6},{8,9},{9,8},{10,11... | collective-permute-start | bytes 1585160 | tf_op jit(solution)/shard_map/ppermute | solution.py:706
  15.4 16.2 %collective-permute-start.1 = (bf16[48,1664]{1,0:T(8,128)(2,1)S(1)}, bf16[48,1664]{1,0:T(8,128)(2,1)S(1)}, u32[]{:S(2)}, u32[]{:S(2)}) collective-permute-start(bf16[48,1664]{1,0:T(8,128)(2,1)S(1)} %fusion.23), channel_id=1, source_target_pairs={{0,16},{1,17},{2,18},{3,19},{4,20},{5,21},{6,22},{7,23},{8,24},{9,... | collective-permute-start | bytes 479240 | tf_op jit(solution)/shard_map/ppermute | solution.py:706
  18.1 13.5 %collective-permute-start = (bf16[48,1664]{1,0:T(8,128)(2,1)S(1)}, bf16[48,1664]{1,0:T(8,128)(2,1)S(1)}, u32[]{:S(2)}, u32[]{:S(2)}) collective-permute-start(bf16[48,1664]{1,0:T(8,128)(2,1)S(1)} %fusion.23), channel_id=1, source_target_pairs={{0,8},{1,9},{2,10},{3,11},{4,12},{5,13},{6,14},{7,15},{8,0},{9,1},... | collective-permute-start | bytes 479240 | tf_op jit(solution)/shard_map/ppermute | solution.py:706
  19.7 15.2 %collective-permute-start.2 = (bf16[48,1664]{1,0:T(8,128)(2,1)S(1)}, bf16[48,1664]{1,0:T(8,128)(2,1)S(1)}, u32[]{:S(2)}, u32[]{:S(2)}) collective-permute-start(bf16[48,1664]{1,0:T(8,128)(2,1)S(1)} %fusion.23), channel_id=1, source_target_pairs={{0,24},{1,25},{2,26},{3,27},{4,28},{5,29},{6,30},{7,31},{8,16},{9,... | collective-permute-start | bytes 479240 | tf_op jit(solution)/shard_map/ppermute | solution.py:706
  35.0 13.3 %copy-start.4 = (bf16[4,48,1664]{2,1,0:T(8,128)(2,1)}, bf16[4,48,1664]{2,1,0:T(8,128)(2,1)S(1)}, u32[]{:S(2)}) copy-start(bf16[4,48,1664]{2,1,0:T(8,128)(2,1)S(1)} %pad_maximum_fusion.1.refs_0_) | copy-start | bytes 1916932
  35.0 12.2 %collective-permute-start.7 = (bf16[4,48,1664]{2,1,0:T(8,128)(2,1)S(1)}, bf16[4,48,1664]{2,1,0:T(8,128)(2,1)}, u32[]{:S(2)}, u32[]{:S(2)}) collective-permute-start(bf16[4,48,1664]{2,1,0:T(8,128)(2,1)S(1)} %pad_maximum_fusion.1.refs_0_), channel_id=1, source_target_pairs={{0,4},{1,5},{2,6},{3,7},{4,0},{5,1},{6,2},{7,3},{8,12},{9,13},{10,... | collective-permute-start | bytes 1916936 | tf_op jit(solution)/shard_map/ppermute | solution.py:706
  36.3 15.0 %collective-permute-start.5 = (bf16[4,48,1664]{2,1,0:T(8,128)(2,1)S(1)}, bf16[4,48,1664]{2,1,0:T(8,128)(2,1)}, u32[]{:S(2)}, u32[]{:S(2)}) collective-permute-start(bf16[4,48,1664]{2,1,0:T(8,128)(2,1)S(1)} %pad_maximum_fusion.1.refs_0_), channel_id=1, source_target_pairs={{0,1},{1,0},{2,3},{3,2},{4,5},{5,4},{6,7},{7,6},{8,9},{9,8},{10,11... | collective-permute-start | bytes 1916936 | tf_op jit(solution)/shard_map/ppermute | solution.py:706
  47.2 14.7 %collective-permute-start.9 = (bf16[4,48,1664]{2,1,0:T(8,128)(2,1)}, bf16[4,48,1664]{2,1,0:T(8,128)(2,1)}, u32[]{:S(2)}, u32[]{:S(2)}) collective-permute-start(bf16[4,48,1664]{2,1,0:T(8,128)(2,1)} %collective-permute-done.7.refs_4_), channel_id=1, source_target_pairs={{0,1},{1,0},{2,3},{3,2},{4,5},{5,4},{6,7},{7,6},{8,9},{9,8},{10,11... | collective-permute-start | bytes 1916936 | tf_op jit(solution)/shard_map/ppermute | solution.py:706
  48.3 15.4 %collective-permute-start.4 = (bf16[4,48,1664]{2,1,0:T(8,128)(2,1)S(1)}, bf16[4,48,1664]{2,1,0:T(8,128)(2,1)}, u32[]{:S(2)}, u32[]{:S(2)}) collective-permute-start(bf16[4,48,1664]{2,1,0:T(8,128)(2,1)S(1)} %pad_maximum_fusion.1.refs_0_), channel_id=1, source_target_pairs={{0,2},{1,3},{2,0},{3,1},{4,6},{5,7},{6,4},{7,5},{8,10},{9,11},{10,... | collective-permute-start | bytes 1916936 | tf_op jit(solution)/shard_map/ppermute | solution.py:706
  48.3 15.4 %collective-permute-start.8 = (bf16[4,48,1664]{2,1,0:T(8,128)(2,1)}, bf16[4,48,1664]{2,1,0:T(8,128)(2,1)}, u32[]{:S(2)}, u32[]{:S(2)}) collective-permute-start(bf16[4,48,1664]{2,1,0:T(8,128)(2,1)} %collective-permute-done.7.refs_4_), channel_id=1, source_target_pairs={{0,2},{1,3},{2,0},{3,1},{4,6},{5,7},{6,4},{7,5},{8,10},{9,11},{10,... | collective-permute-start | bytes 1916936 | tf_op jit(solution)/shard_map/ppermute | solution.py:706
  51.4 12.3 %collective-permute-start.6 = (bf16[4,48,1664]{2,1,0:T(8,128)(2,1)}, bf16[4,48,1664]{2,1,0:T(8,128)(2,1)}, u32[]{:S(2)}, u32[]{:S(2)}) collective-permute-start(bf16[4,48,1664]{2,1,0:T(8,128)(2,1)} %collective-permute-done.5.refs_2_), channel_id=1, source_target_pairs={{0,2},{1,3},{2,0},{3,1},{4,6},{5,7},{6,4},{7,5},{8,10},{9,11},{10,... | collective-permute-start | bytes 1916936 | tf_op jit(solution)/shard_map/ppermute | solution.py:706
  61.8 2.4 collective-permute-start.10
  62.1 30.7 %copy-start.1 = (bf16[2,328,768]{2,1,0:T(8,128)(2,1)}, bf16[2,328,768]{2,1,0:T(8,128)(2,1)S(1)}, u32[]{:S(2)}) copy-start(bf16[2,328,768]{2,1,0:T(8,128)(2,1)S(1)} %get-tuple-element.242) | copy-start | bytes 3022852
  71.0 26.2 %collective-permute-start.11 = (bf16[328,768]{1,0:T(8,128)(2,1)}, bf16[328,768]{1,0:T(8,128)(2,1)}, u32[]{:S(2)}, u32[]{:S(2)}) collective-permute-start(bf16[328,768]{1,0:T(8,128)(2,1)} %get-tuple-element.127), channel_id=1, source_target_pairs={{0,1},{1,0},{2,3},{3,2},{4,5},{5,4},{6,7},{7,6},{8,9},{9,8},{10,11... | collective-permute-start | bytes 1511432 | tf_op jit(solution)/shard_map/ppermute | solution.py:706
  95.3 28.9 %copy-start = (f32[656,768]{1,0:T(8,128)}, f32[656,768]{1,0:T(8,128)S(1)}, u32[]{:S(2)}) copy-start(f32[656,768]{1,0:T(8,128)S(1)} %fusion.5.middle_ref) | copy-start | bytes 6045700
  127.3 14.4 %collective-permute-start.13 = (bf16[4,2,192,768]{3,2,1,0:T(8,128)(2,1)}, bf16[4,2,192,768]{3,2,1,0:T(8,128)(2,1)S(1)}, u32[]{:S(2)}, u32[]{:S(2)}) collective-permute-start(bf16[4,2,192,768]{3,2,1,0:T(8,128)(2,1)} %get-tuple-element.136), channel_id=1, source_target_pairs={{0,2},{1,3},{2,0},{3,1},{4,6},{5,7},{6,4},{7,5},{8,10},{9,11},{10,... | collective-permute-start | bytes 7077896 | tf_op jit(solution)/shard_map/ppermute | solution.py:706
  127.6 14.1 %collective-permute-start.12 = (bf16[328,768]{1,0:T(8,128)(2,1)S(1)}, bf16[328,768]{1,0:T(8,128)(2,1)S(1)}, u32[]{:S(2)}, u32[]{:S(2)}) collective-permute-start(bf16[328,768]{1,0:T(8,128)(2,1)S(1)} %slice.165), channel_id=1, source_target_pairs={{0,1},{1,0},{2,3},{3,2},{4,5},{5,4},{6,7},{7,6},{8,9},{9,8},{10,11... | collective-permute-start | bytes 1511432 | tf_op jit(solution)/shard_map/ppermute | solution.py:706
  128.1 13.6 %copy-start.7 = (bf16[4,2,192,768]{3,2,1,0:T(8,128)(2,1)S(1)}, bf16[4,2,192,768]{3,2,1,0:T(8,128)(2,1)}, u32[]{:S(2)}) copy-start(bf16[4,2,192,768]{3,2,1,0:T(8,128)(2,1)} %get-tuple-element.140) | copy-start | bytes 7077892
  144.0 10.8 %collective-permute-start.14 = (bf16[4,2,48,3072]{3,2,1,0:T(8,128)(2,1)}, bf16[4,2,48,3072]{3,2,1,0:T(8,128)(2,1)S(1)}, u32[]{:S(2)}, u32[]{:S(2)}) collective-permute-start(bf16[4,2,48,3072]{3,2,1,0:T(8,128)(2,1)} %get-tuple-element.147), channel_id=1, source_target_pairs={{0,2},{1,3},{2,0},{3,1},{4,6},{5,7},{6,4},{7,5},{8,10},{9,11},{10,... | collective-permute-start | bytes 7077896 | tf_op jit(solution)/shard_map/ppermute | solution.py:706
  144.0 25.2 %collective-permute-start.15 = (bf16[4,192,384]{2,1,0:T(8,128)(2,1)}, bf16[4,192,384]{2,1,0:T(8,128)(2,1)S(1)}, u32[]{:S(2)}, u32[]{:S(2)}) collective-permute-start(bf16[4,192,384]{2,1,0:T(8,128)(2,1)} %get-tuple-element.157), channel_id=1, source_target_pairs={{0,4},{1,5},{2,6},{3,7},{4,0},{5,1},{6,2},{7,3},{8,12},{9,13},{10,... | collective-permute-start | bytes 1769480 | tf_op jit(solution)/shard_map/ppermute | solution.py:706
  145.3 27.1 %collective-permute-start.16 = (bf16[4,192,384]{2,1,0:T(8,128)(2,1)}, bf16[4,192,384]{2,1,0:T(8,128)(2,1)S(1)}, u32[]{:S(2)}, u32[]{:S(2)}) collective-permute-start(bf16[4,192,384]{2,1,0:T(8,128)(2,1)} %get-tuple-element.158), channel_id=1, source_target_pairs={{0,1},{1,0},{2,3},{3,2},{4,5},{5,4},{6,7},{7,6},{8,9},{9,8},{10,11... | collective-permute-start | bytes 1769480 | tf_op jit(solution)/shard_map/ppermute | solution.py:706
  146.5 27.1 %collective-permute-start.17 = (bf16[4,192,384]{2,1,0:T(8,128)(2,1)}, bf16[4,192,384]{2,1,0:T(8,128)(2,1)S(1)}, u32[]{:S(2)}, u32[]{:S(2)}) collective-permute-start(bf16[4,192,384]{2,1,0:T(8,128)(2,1)} %get-tuple-element.159), channel_id=1, source_target_pairs={{0,5},{1,4},{2,7},{3,6},{4,1},{5,0},{6,3},{7,2},{8,13},{9,12},{10,... | collective-permute-start | bytes 1769480 | tf_op jit(solution)/shard_map/ppermute | solution.py:706
  147.5 7.3 %copy-start.6 = (bf16[4,2,48,3072]{3,2,1,0:T(8,128)(2,1)S(1)}, bf16[4,2,48,3072]{3,2,1,0:T(8,128)(2,1)}, u32[]{:S(2)}) copy-start(bf16[4,2,48,3072]{3,2,1,0:T(8,128)(2,1)} %get-tuple-element.149) | copy-start | bytes 7077892
  155.9 17.7 %copy-start.8 = (bf16[4,192,384]{2,1,0:T(8,128)(2,1)S(1)}, bf16[4,192,384]{2,1,0:T(8,128)(2,1)}, u32[]{:S(2)}) copy-start(bf16[4,192,384]{2,1,0:T(8,128)(2,1)} %get-tuple-element.164) | copy-start | bytes 1769476
  173.6 19.8 %copy-start.16 = (f32[1,3072]{1,0:T(1,128)S(1)}, f32[1,3072]{1,0:T(1,128)}, u32[]{:S(2)}) copy-start(f32[1,3072]{1,0:T(1,128)} %get-tuple-element.182) | copy-start | bytes 36868
  174.0 17.5 %collective-permute-start.18 = (bf16[192,384]{1,0:T(8,128)(2,1)S(1)}, bf16[192,384]{1,0:T(8,128)(2,1)S(1)}, u32[]{:S(2)}, u32[]{:S(2)}) collective-permute-start(bf16[192,384]{1,0:T(8,128)(2,1)S(1)} %get-tuple-element.173), channel_id=1, source_target_pairs={{0,8},{1,9},{2,10},{3,11},{4,12},{5,13},{6,14},{7,15},{8,0},{9,1},... | collective-permute-start | bytes 442376 | tf_op jit(solution)/shard_map/ppermute | solution.py:706
  184.2 37.7 %collective-permute-start.22 = (bf16[4,48,1536]{2,1,0:T(8,128)(2,1)S(1)}, bf16[4,48,1536]{2,1,0:T(8,128)(2,1)}, u32[]{:S(2)}, u32[]{:S(2)}) collective-permute-start(bf16[4,48,1536]{2,1,0:T(8,128)(2,1)S(1)} %get-tuple-element.193), channel_id=1, source_target_pairs={{0,4},{1,5},{2,6},{3,7},{4,0},{5,1},{6,2},{7,3},{8,12},{9,13},{10,... | collective-permute-start | bytes 1769480 | tf_op jit(solution)/shard_map/ppermute | solution.py:706
  185.2 36.6 %collective-permute-start.23 = (bf16[4,48,1536]{2,1,0:T(8,128)(2,1)S(1)}, bf16[4,48,1536]{2,1,0:T(8,128)(2,1)}, u32[]{:S(2)}, u32[]{:S(2)}) collective-permute-start(bf16[4,48,1536]{2,1,0:T(8,128)(2,1)S(1)} %get-tuple-element.194), channel_id=1, source_target_pairs={{0,1},{1,0},{2,3},{3,2},{4,5},{5,4},{6,7},{7,6},{8,9},{9,8},{10,11... | collective-permute-start | bytes 1769480 | tf_op jit(solution)/shard_map/ppermute | solution.py:706
  186.0 35.8 %collective-permute-start.24 = (bf16[4,48,1536]{2,1,0:T(8,128)(2,1)S(1)}, bf16[4,48,1536]{2,1,0:T(8,128)(2,1)}, u32[]{:S(2)}, u32[]{:S(2)}) collective-permute-start(bf16[4,48,1536]{2,1,0:T(8,128)(2,1)S(1)} %get-tuple-element.195), channel_id=1, source_target_pairs={{0,5},{1,4},{2,7},{3,6},{4,1},{5,0},{6,3},{7,2},{8,13},{9,12},{10,... | collective-permute-start | bytes 1769480 | tf_op jit(solution)/shard_map/ppermute | solution.py:706
  187.7 20.6 %collective-permute-start.19 = (bf16[192,384]{1,0:T(8,128)(2,1)S(1)}, bf16[192,384]{1,0:T(8,128)(2,1)S(1)}, u32[]{:S(2)}, u32[]{:S(2)}) collective-permute-start(bf16[192,384]{1,0:T(8,128)(2,1)S(1)} %get-tuple-element.174), channel_id=1, source_target_pairs={{0,16},{1,17},{2,18},{3,19},{4,20},{5,21},{6,22},{7,23},{8,24},{9,... | collective-permute-start | bytes 442376 | tf_op jit(solution)/shard_map/ppermute | solution.py:706
  191.5 16.8 %collective-permute-start.20 = (bf16[192,384]{1,0:T(8,128)(2,1)S(1)}, bf16[192,384]{1,0:T(8,128)(2,1)S(1)}, u32[]{:S(2)}, u32[]{:S(2)}) collective-permute-start(bf16[192,384]{1,0:T(8,128)(2,1)S(1)} %get-tuple-element.175), channel_id=1, source_target_pairs={{0,24},{1,25},{2,26},{3,27},{4,28},{5,29},{6,30},{7,31},{8,16},{9,... | collective-permute-start | bytes 442376 | tf_op jit(solution)/shard_map/ppermute | solution.py:706
  208.4 13.4 %collective-permute-start.21 = (bf16[192,384]{1,0:T(8,128)(2,1)S(1)}, bf16[192,384]{1,0:T(8,128)(2,1)S(1)}, u32[]{:S(2)}, u32[]{:S(2)}) collective-permute-start(bf16[192,384]{1,0:T(8,128)(2,1)S(1)} %add_convert_fusion.10), channel_id=1, source_target_pairs={{0,1},{1,0},{2,3},{3,2},{4,5},{5,4},{6,7},{7,6},{8,9},{9,8},{10,11... | collective-permute-start | bytes 442376 | tf_op jit(solution)/shard_map/ppermute | solution.py:706
  221.9 5.1 %collective-permute-start.25 = (bf16[4,2,48,3328]{3,2,1,0:T(8,128)(2,1)}, bf16[4,2,48,3328]{3,2,1,0:T(8,128)(2,1)S(1)}, u32[]{:S(2)}, u32[]{:S(2)}) collective-permute-start(bf16[4,2,48,3328]{3,2,1,0:T(8,128)(2,1)} %get-tuple-element.198), channel_id=1, source_target_pairs={{0,2},{1,3},{2,0},{3,1},{4,6},{5,7},{6,4},{7,5},{8,10},{9,11},{10,... | collective-permute-start | bytes 7667720 | tf_op jit(solution)/shard_map/ppermute | solution.py:706
  227.8 18.5 %collective-permute-start.26 = (bf16[4,48,1664]{2,1,0:T(8,128)(2,1)S(1)}, bf16[4,48,1664]{2,1,0:T(8,128)(2,1)S(1)}, u32[]{:S(2)}, u32[]{:S(2)}) collective-permute-start(bf16[4,48,1664]{2,1,0:T(8,128)(2,1)S(1)} %get-tuple-element.204), channel_id=1, source_target_pairs={{0,4},{1,5},{2,6},{3,7},{4,0},{5,1},{6,2},{7,3},{8,12},{9,13},{10,... | collective-permute-start | bytes 1916936 | tf_op jit(solution)/shard_map/ppermute | solution.py:706
  229.3 28.4 %collective-permute-start.27 = (bf16[4,48,1664]{2,1,0:T(8,128)(2,1)S(1)}, bf16[4,48,1664]{2,1,0:T(8,128)(2,1)S(1)}, u32[]{:S(2)}, u32[]{:S(2)}) collective-permute-start(bf16[4,48,1664]{2,1,0:T(8,128)(2,1)S(1)} %get-tuple-element.205), channel_id=1, source_target_pairs={{0,1},{1,0},{2,3},{3,2},{4,5},{5,4},{6,7},{7,6},{8,9},{9,8},{10,11... | collective-permute-start | bytes 1916936 | tf_op jit(solution)/shard_map/ppermute | solution.py:706
  230.4 28.8 %collective-permute-start.28 = (bf16[4,48,1664]{2,1,0:T(8,128)(2,1)S(1)}, bf16[4,48,1664]{2,1,0:T(8,128)(2,1)S(1)}, u32[]{:S(2)}, u32[]{:S(2)}) collective-permute-start(bf16[4,48,1664]{2,1,0:T(8,128)(2,1)S(1)} %get-tuple-element.206), channel_id=1, source_target_pairs={{0,5},{1,4},{2,7},{3,6},{4,1},{5,0},{6,3},{7,2},{8,13},{9,12},{10,... | collective-permute-start | bytes 1916936 | tf_op jit(solution)/shard_map/ppermute | solution.py:706
  231.5 7.1 %collective-permute-start.29 = (bf16[48,1536]{1,0:T(8,128)(2,1)S(1)}, bf16[48,1536]{1,0:T(8,128)(2,1)S(1)}, u32[]{:S(2)}, u32[]{:S(2)}) collective-permute-start(bf16[48,1536]{1,0:T(8,128)(2,1)S(1)} %get-tuple-element.208), channel_id=1, source_target_pairs={{0,8},{1,9},{2,10},{3,11},{4,12},{5,13},{6,14},{7,15},{8,0},{9,1},... | collective-permute-start | bytes 442376 | tf_op jit(solution)/shard_map/ppermute | solution.py:706
  232.9 26.2 %copy-start.9 = (f32[656,768]{1,0:T(8,128)S(1)}, f32[656,768]{1,0:T(8,128)}, u32[]{:S(2)}) copy-start(f32[656,768]{1,0:T(8,128)} %get-tuple-element.211) | copy-start | bytes 6045700
  232.9 13.4 %collective-permute-start.30 = (bf16[48,1536]{1,0:T(8,128)(2,1)S(1)}, bf16[48,1536]{1,0:T(8,128)(2,1)S(1)}, u32[]{:S(2)}, u32[]{:S(2)}) collective-permute-start(bf16[48,1536]{1,0:T(8,128)(2,1)S(1)} %get-tuple-element.209), channel_id=1, source_target_pairs={{0,16},{1,17},{2,18},{3,19},{4,20},{5,21},{6,22},{7,23},{8,24},{9,... | collective-permute-start | bytes 442376 | tf_op jit(solution)/shard_map/ppermute | solution.py:706
  238.5 7.8 %collective-permute-start.31 = (bf16[48,1536]{1,0:T(8,128)(2,1)S(1)}, bf16[48,1536]{1,0:T(8,128)(2,1)S(1)}, u32[]{:S(2)}, u32[]{:S(2)}) collective-permute-start(bf16[48,1536]{1,0:T(8,128)(2,1)S(1)} %get-tuple-element.210), channel_id=1, source_target_pairs={{0,24},{1,25},{2,26},{3,27},{4,28},{5,29},{6,30},{7,31},{8,16},{9,... | collective-permute-start | bytes 442376 | tf_op jit(solution)/shard_map/ppermute | solution.py:706
  259.7 17.8 %collective-permute-start.37 = (bf16[48,1536]{1,0:T(8,128)(2,1)S(1)}, bf16[48,1536]{1,0:T(8,128)(2,1)S(1)}, u32[]{:S(2)}, u32[]{:S(2)}) collective-permute-start(bf16[48,1536]{1,0:T(8,128)(2,1)S(1)} %add_convert_fusion.9), channel_id=1, source_target_pairs={{0,1},{1,0},{2,3},{3,2},{4,5},{5,4},{6,7},{7,6},{8,9},{9,8},{10,11... | collective-permute-start | bytes 442376 | tf_op jit(solution)/shard_map/ppermute | solution.py:706
  260.8 6.4 %collective-permute-start.33 = (bf16[48,1664]{1,0:T(8,128)(2,1)S(1)}, bf16[48,1664]{1,0:T(8,128)(2,1)S(1)}, u32[]{:S(2)}, u32[]{:S(2)}) collective-permute-start(bf16[48,1664]{1,0:T(8,128)(2,1)S(1)} %get-tuple-element.222), channel_id=1, source_target_pairs={{0,8},{1,9},{2,10},{3,11},{4,12},{5,13},{6,14},{7,15},{8,0},{9,1},... | collective-permute-start | bytes 479240 | tf_op jit(solution)/shard_map/ppermute | solution.py:706
  262.4 13.3 %collective-permute-start.34 = (bf16[48,1664]{1,0:T(8,128)(2,1)S(1)}, bf16[48,1664]{1,0:T(8,128)(2,1)S(1)}, u32[]{:S(2)}, u32[]{:S(2)}) collective-permute-start(bf16[48,1664]{1,0:T(8,128)(2,1)S(1)} %get-tuple-element.223), channel_id=1, source_target_pairs={{0,16},{1,17},{2,18},{3,19},{4,20},{5,21},{6,22},{7,23},{8,24},{9,... | collective-permute-start | bytes 479240 | tf_op jit(solution)/shard_map/ppermute | solution.py:706
  263.6 12.1 %collective-permute-start.35 = (bf16[48,1664]{1,0:T(8,128)(2,1)S(1)}, bf16[48,1664]{1,0:T(8,128)(2,1)S(1)}, u32[]{:S(2)}, u32[]{:S(2)}) collective-permute-start(bf16[48,1664]{1,0:T(8,128)(2,1)S(1)} %get-tuple-element.224), channel_id=1, source_target_pairs={{0,24},{1,25},{2,26},{3,27},{4,28},{5,29},{6,30},{7,31},{8,16},{9,... | collective-permute-start | bytes 479240 | tf_op jit(solution)/shard_map/ppermute | solution.py:706
  265.2 19.2 %collective-permute-start.32 = (bf16[328,768]{1,0:T(8,128)(2,1)S(1)}, bf16[328,768]{1,0:T(8,128)(2,1)S(1)}, u32[]{:S(2)}, u32[]{:S(2)}) collective-permute-start(bf16[328,768]{1,0:T(8,128)(2,1)S(1)} %slice.164), channel_id=1, source_target_pairs={{0,1},{1,0},{2,3},{3,2},{4,5},{5,4},{6,7},{7,6},{8,9},{9,8},{10,11... | collective-permute-start | bytes 1511432 | tf_op jit(solution)/shard_map/ppermute | solution.py:706
  275.8 5.3 %collective-permute-start.36 = (bf16[48,1664]{1,0:T(8,128)(2,1)S(1)}, bf16[48,1664]{1,0:T(8,128)(2,1)S(1)}, u32[]{:S(2)}, u32[]{:S(2)}) collective-permute-start(bf16[48,1664]{1,0:T(8,128)(2,1)S(1)} %add_convert_fusion.8), channel_id=1, source_target_pairs={{0,1},{1,0},{2,3},{3,2},{4,5},{5,4},{6,7},{7,6},{8,9},{9,8},{10,11... | collective-permute-start | bytes 479240 | tf_op jit(solution)/shard_map/ppermute | solution.py:706
  (14 other events, 65.6 us)
Sparse Core Ops, SparseCore 0:
  10.9 92.7 all-gather.1

commit v3 on v2

--- a/solution.py
+++ b/solution.py
@@ -335,7 +335,20 @@
     return lax.dot_general(left, right, (((0,), (0,)), ((), ())), preferred_element_type=F32)
 
 
-def attention_forward_kernel(scale, size, query_ref, key_ref, value_ref, mask_ref, out_ref, log_ref):
+def attention_forward_kernel(
+    scale, size, inputs_ref, gain_ref, shift_ref, q_weight_ref, k_weight_ref, v_weight_ref, q_bias_ref, v_bias_ref,
+    mask_ref, out_ref, log_ref, query_ref, key_ref, value_ref, normed_ref,
+):
+    @pl.when(pl.program_id(0) == 0)
+    def _():
+        unit, _ = norm_parts(inputs_ref[...].astype(F32))
+        normed_ref[...] = (unit * gain_ref[...] + shift_ref[...]).astype(LOW)
+
+    weight = jnp.concatenate([q_weight_ref[...], k_weight_ref[...], v_weight_ref[...]], axis=1)
+    projected = dot_nn(normed_ref[...], weight)
+    query_ref[...] = (projected[:, : 2 * size] + q_bias_ref[...]).astype(LOW)
+    key_ref[...] = projected[:, 2 * size : 4 * size].astype(LOW)
+    value_ref[...] = (projected[:, 4 * size :] + v_bias_ref[...]).astype(LOW)
     real = mask_ref[...] > 0.5
     query = query_ref[...] * jnp.asarray(scale, LOW)
     key = jnp.where(real, key_ref[...], key_ref[0:1, :])
@@ -356,33 +369,40 @@
     out_ref[...] = jnp.concatenate(pieces, axis=0).T.astype(LOW)
 
 
-def attention_forward(qkv, mask_column):
-    rows, width = qkv.shape
-    dim = width // 3
+def attention_forward(inputs, gain, shift, first, query_bias, value_bias, mask_column):
+    rows, dim = inputs.shape
     size = dim // HEADS
     pairs = HEADS // 2
-    block = (rows, 2 * size)
+    spec = pl.BlockSpec((rows, 2 * size), lambda p: (0, p))
+    bias = pl.BlockSpec((1, 2 * size), lambda p: (0, p))
+    row = pl.BlockSpec((1, dim), lambda p: (0, 0))
     return pl.pallas_call(
         functools.partial(attention_forward_kernel, size ** (-0.5), size),
         grid=(pairs,),
         in_specs=[
-            pl.BlockSpec(block, lambda p: (0, p)),
-            pl.BlockSpec(block, lambda p: (0, pairs + p)),
-            pl.BlockSpec(block, lambda p: (0, 2 * pairs + p)),
+            pl.BlockSpec((rows, dim), lambda p: (0, 0)),
+            row,
+            row,
+            pl.BlockSpec((dim, 2 * size), lambda p: (0, p)),
+            pl.BlockSpec((dim, 2 * size), lambda p: (0, pairs + p)),
+            pl.BlockSpec((dim, 2 * size), lambda p: (0, 2 * pairs + p)),
+            bias,
+            bias,
             pl.BlockSpec((rows, 1), lambda p: (0, 0)),
         ],
-        out_specs=[
-            pl.BlockSpec(block, lambda p: (0, p)),
-            pl.BlockSpec((1, 2, rows), lambda p: (p, 0, 0)),
-        ],
+        out_specs=[spec, pl.BlockSpec((1, 2, rows), lambda p: (p, 0, 0)), spec, spec, spec],
         out_shape=[
             jax.ShapeDtypeStruct((rows, dim), LOW),
             jax.ShapeDtypeStruct((pairs, 2, rows), F32),
-        ],
+            jax.ShapeDtypeStruct((rows, dim), LOW),
+            jax.ShapeDtypeStruct((rows, dim), LOW),
+            jax.ShapeDtypeStruct((rows, dim), LOW),
+        ],
+        scratch_shapes=[pltpu.VMEM((rows, dim), LOW)],
         compiler_params=pltpu.CompilerParams(vmem_limit_bytes=VMEM),
-        cost_estimate=cost(13),
+        cost_estimate=cost(16),
         name="attention_forward",
-    )(qkv, qkv, qkv, mask_column)
+    )(inputs, gain, shift, first, first, first, query_bias, value_bias, mask_column)
 
 
 def attention_backward_kernel(
@@ -419,10 +439,8 @@
 
 
 def attention_backward(qkv, mask_column, logs, grad, first, count):
-    rows, width = qkv.shape
-    dim = width // 3
+    rows, dim = grad.shape
     size = dim // HEADS
-    pairs = HEADS // 2
     block = (rows, 2 * size)
     spec = pl.BlockSpec(block, lambda p: (0, first + p))
     out_spec = pl.BlockSpec(block, lambda p: (0, p))
@@ -431,8 +449,8 @@
         grid=(count,),
         in_specs=[
             spec,
-            pl.BlockSpec(block, lambda p: (0, pairs + first + p)),
-            pl.BlockSpec(block, lambda p: (0, 2 * pairs + first + p)),
+            spec,
+            spec,
             pl.BlockSpec((rows, 1), lambda p: (0, 0)),
             pl.BlockSpec((1, 2, rows), lambda p: (first + p, 0, 0)),
             spec,
@@ -442,7 +460,7 @@
         compiler_params=pltpu.CompilerParams(vmem_limit_bytes=VMEM),
         cost_estimate=cost(1),
         name="attention_backward",
-    )(qkv, qkv, qkv, mask_column, logs, grad)
+    )(*qkv, mask_column, logs, grad)
 
 
 def split_cores(total_ref, kept_ref, sent_ref, first, columns):
@@ -455,7 +473,7 @@
 
 
 def mlp_first_kernel(
-    shape, second_ref, dz_ref, up_ref, up_bias_ref, down_ref,
+    shape, second_ref, dz_ref, up_ref, up_bias_ref, down_ref, middle_ref, down_bias_ref,
     out_ref, kept_ref, sent_ref, pre_grad_ref, up_bias_grad_ref, down_grad_ref,
 ):
     step = pl.program_id(0)
@@ -471,21 +489,35 @@
     hidden = (pre_act * cumulative).astype(LOW)
     pre_grad = (hidden_grad * (cumulative + pre_act * density)).astype(LOW)
     pre_grad_ref[...] = pre_grad
-    up_bias_grad_ref[...] = jnp.sum(pre_grad.astype(F32), axis=0, keepdims=True)
+    bias_grad = jnp.sum(pre_grad.astype(F32), axis=0, keepdims=True)
+    turned = jnp.broadcast_to(bias_grad, (128, bias_grad.shape[1])).T
+    shard = kept_ref.shape[2]
+    lane = lax.broadcasted_iota(jnp.int32, (shard, 128), 1)
+    for o in range(owners):
+        tile = jnp.zeros((shard, 128), F32)
+        for i in range(pieces):
+            start = (o * pieces + i) * shard
+            tile = jnp.where(lane == i, turned[start : start + shard], tile)
+        up_bias_grad_ref[o * shard : (o + 1) * shard, :] = tile.astype(LOW)
     out_part = dot_nn(hidden, down)
     down_grad_ref[...] = dot_tn(hidden, dz).astype(LOW)
-    split_cores(down_grad_ref, kept_ref, sent_ref, 0, slice(None))
+    core = lax.axis_index("img") % 2
+    for x in range(2):
+        for ref, side in ((kept_ref, core), (sent_ref, 1 - core)):
+            for i in range(pieces):
+                start = pl.multiple_of(((2 * x + side) * pieces + i) * shard, 16)
+                ref[0, x, :, i * dim : (i + 1) * dim] = down_grad_ref[pl.ds(start, shard), :]
 
     @pl.when(step == 0)
     def _():
-        out_ref[...] = out_part
+        out_ref[...] = middle_ref[...] + down_bias_ref[...] + out_part
 
     @pl.when(step > 0)
     def _():
         out_ref[...] += out_part
 
 
-def mlp_first(second, dz, up_down, up_bias, owners):
+def mlp_first(second, dz, up_down, up_bias, middle, down_bias, owners):
     rows, dim = second.shape
     width = up_bias.shape[1]
     shard = dim // owners
@@ -501,26 +533,28 @@
             pl.BlockSpec((dim, dim), lambda j: (0, j)),
             pl.BlockSpec((1, dim), lambda j: (0, j)),
             pl.BlockSpec((some, shard, width), lambda j: (j, 0, 1)),
+            whole,
+            pl.BlockSpec((1, dim), lambda j: (0, 0)),
         ],
         out_specs=[
             whole,
-            pl.BlockSpec((1, 2, width // owners, dim), lambda j: (j, 0, 0, 0)),
-            pl.BlockSpec((1, 2, width // owners, dim), lambda j: (j, 0, 0, 0)),
+            pl.BlockSpec((1, 2, shard, width), lambda j: (j, 0, 0, 0)),
+            pl.BlockSpec((1, 2, shard, width), lambda j: (j, 0, 0, 0)),
             pl.BlockSpec((rows, dim), lambda j: (0, j)),
-            pl.BlockSpec((1, dim), lambda j: (0, j)),
+            pl.BlockSpec((some * shard, 128), lambda j: (j, 0)),
         ],
         out_shape=[
             jax.ShapeDtypeStruct((rows, dim), F32),
-            jax.ShapeDtypeStruct((4, 2, width // owners, dim), LOW),
-            jax.ShapeDtypeStruct((4, 2, width // owners, dim), LOW),
+            jax.ShapeDtypeStruct((4, 2, shard, width), LOW),
+            jax.ShapeDtypeStruct((4, 2, shard, width), LOW),
             jax.ShapeDtypeStruct((rows, width), LOW),
-            jax.ShapeDtypeStruct((1, width), F32),
+            jax.ShapeDtypeStruct((dim, 128), LOW),
         ],
         scratch_shapes=[pltpu.VMEM((dim, dim), LOW)],
         compiler_params=pltpu.CompilerParams(vmem_limit_bytes=VMEM),
         cost_estimate=cost(19),
         name="mlp_first",
-    )(second, dz, up_down, up_bias, up_down.reshape(owners, shard, 2 * width))
+    )(second, dz, up_down, up_bias, up_down.reshape(owners, shard, 2 * width), middle, down_bias)
 
 
 def mlp_second_kernel(second_ref, pre_grad_ref, up_ref, second_grad_ref, kept_ref, sent_ref, up_grad_ref):
@@ -585,7 +619,7 @@
 
 def middle_kernel(
     middle_ref, grad_ref, dz_ref, gain_ref, out_full_ref, merged_ref,
-    middle_grad_ref, merged_grad_ref, out_grad_ref, small_ref,
+    middle_grad_ref, merged_grad_ref, kept_ref, sent_ref, small_ref, out_grad_ref,
 ):
     unit, inverse = norm_parts(middle_ref[...])
     grad = grad_ref[...]
@@ -595,14 +629,16 @@
     low = middle_grad.astype(LOW)
     merged_grad_ref[...] = dot_nt(low, out_full_ref[...]).astype(LOW)
     out_grad_ref[...] = dot_tn(merged_ref[...], low).astype(LOW)
+    split_cores(out_grad_ref, kept_ref, sent_ref, 0, slice(None))
     small_ref[0:1] = column_sums(low.astype(F32))
     small_ref[1:2] = column_sums(grad * unit)
     small_ref[2:3] = column_sums(grad)
     small_ref[3:4] = column_sums(upstream)
 
 
-def middle_backward(middle, second_grad, dz, gain, first, merged):
+def middle_backward(middle, second_grad, dz, gain, first, merged, owners):
     rows, dim = middle.shape
+    split = (4, 2, dim // owners, dim)
     whole = pl.BlockSpec((rows, dim), lambda j: (0, 0))
     return pl.pallas_call(
         middle_kernel,
@@ -618,15 +654,18 @@
         out_specs=[
             whole,
             whole,
-            pl.BlockSpec((dim, dim), lambda j: (0, 0)),
+            pl.BlockSpec(split, lambda j: (0, 0, 0, 0)),
+            pl.BlockSpec(split, lambda j: (0, 0, 0, 0)),
             pl.BlockSpec((4, dim), lambda j: (0, 0)),
         ],
         out_shape=[
             jax.ShapeDtypeStruct((rows, dim), F32),
             jax.ShapeDtypeStruct((rows, dim), LOW),
-            jax.ShapeDtypeStruct((dim, dim), LOW),
+            jax.ShapeDtypeStruct(split, LOW),
+            jax.ShapeDtypeStruct(split, LOW),
             jax.ShapeDtypeStruct((4, dim), F32),
         ],
+        scratch_shapes=[pltpu.VMEM((dim, dim), LOW)],
         compiler_params=pltpu.CompilerParams(vmem_limit_bytes=VMEM),
         cost_estimate=cost(1),
         name="middle_backward",
@@ -635,7 +674,7 @@
 
 def last_kernel(
     inputs_ref, gain_ref, shift_ref, q_low, k_low, v_low, q_high, k_high, v_high, qkv_full_ref,
-    middle_grad_ref, out_grad_ref, small_ref, up_bias_ref, input_grad_ref, kept_ref, sent_ref, total_ref,
+    middle_grad_ref, small_ref, up_bias_ref, input_grad_ref, kept_ref, sent_ref, total_ref,
 ):
     unit, inverse = norm_parts(inputs_ref[...].astype(F32))
     gain = gain_ref[...]
@@ -646,20 +685,19 @@
     normed_grad = dot_nt(qkv_grad, qkv_full_ref[...])
     input_grad_ref[...] = middle_grad_ref[...] + norm_back(unit, inverse, gain, normed_grad)
     total_ref[:, : 3 * dim] = dot_tn(normed, qkv_grad).astype(LOW)
-    total_ref[:, 3 * dim : 4 * dim] = out_grad_ref[...]
     bias_of = column_sums(qkv_grad.astype(F32))
     rows = [column_sums(normed_grad * unit), column_sums(normed_grad), bias_of[:, :dim], bias_of[:, 2 * dim :]]
-    rows += [small_ref[...], up_bias_ref[...]]
+    rows += [small_ref[...]]
     taken = sum(row.shape[0] for row in rows)
     rows.append(jnp.zeros((128 - taken, dim), F32))
-    total_ref[:, 4 * dim : 4 * dim + 128] = jnp.concatenate(rows, axis=0).T.astype(LOW)
-    total_ref[:, 4 * dim + 128 :] = jnp.zeros((dim, SMALL_PAD - 128), LOW)
+    total_ref[:, 3 * dim : 3 * dim + 128] = jnp.concatenate(rows, axis=0).T.astype(LOW)
+    total_ref[:, 3 * dim + 128 :] = up_bias_ref[...]
     split_cores(total_ref, kept_ref, sent_ref, 0, slice(None))
 
 
-def last_backward(inputs, gain, shift, grads_low, grads_high, first, middle_grad, out_grad, small, up_bias, owners):
+def last_backward(inputs, gain, shift, grads_low, grads_high, first, middle_grad, small, up_bias, owners):
     rows, dim = inputs.shape
-    columns = 4 * dim + SMALL_PAD
+    columns = 3 * dim + SMALL_PAD
 
     def whole(*shape):
         return pl.BlockSpec(shape, lambda j: (0,) * len(shape))
@@ -670,14 +708,14 @@
         grid=(1,),
         in_specs=[whole(rows, dim), whole(1, dim), whole(1, dim)]
         + [whole(*g.shape) for g in (*grads_low, *grads_high)]
-        + [whole(dim, 3 * dim), whole(rows, dim), whole(dim, dim), whole(*small.shape), whole(*up_bias.shape)],
+        + [whole(dim, 3 * dim), whole(rows, dim), whole(*small.shape), whole(*up_bias.shape)],
         out_specs=[whole(rows, dim), whole(*split.shape), whole(*split.shape)],
         out_shape=[jax.ShapeDtypeStruct((rows, dim), F32), split, split],
         scratch_shapes=[pltpu.VMEM((dim, columns), LOW)],
         compiler_params=pltpu.CompilerParams(vmem_limit_bytes=VMEM),
         cost_estimate=cost(1),
         name="last_backward",
-    )(inputs, gain, shift, *grads_low, *grads_high, first, middle_grad, out_grad, small, up_bias)
+    )(inputs, gain, shift, *grads_low, *grads_high, first, middle_grad, small, up_bias)
 
 
 def own_and_away(blocks):
@@ -711,26 +749,27 @@
     here_z, here_x, here_core, here_y = place()
     half = out_ref.shape[2] // 2
     for index, ref in enumerate(refs):
-        x, y, core = index // 4 % 2, index // 2 % 2, index % 2
+        first, x, y, core = index // 8, index // 4 % 2, index // 2 % 2, index % 2
         columns = pl.ds(pl.multiple_of((here_y ^ y) * half, half), half)
-        for z in range(4):
-            owner = (here_z ^ z) * 4 + (here_x ^ x) * 2 + (here_core ^ core)
-            out_ref[owner, :, columns] = ref[z]
+        for i in range(ref.shape[0]):
+            owner = (here_z ^ (first + i)) * 4 + (here_x ^ x) * 2 + (here_core ^ core)
+            out_ref[owner, :, columns] = ref[i]
     small = jnp.concatenate([out_ref[i, :, small_at : small_at + 128] for i in range(16)], axis=0)
     small_ref[...] = small.astype(F32).T[:16]
 
 
-def gather_links(block, rows):
+def gather_links(block, rows, later):
     shard, columns = block.shape
     half = columns // 2
-    own = lax.dynamic_slice_in_dim(block, lax.axis_index("seq") * half, half, 1)
+    own = lax.dynamic_slice_in_dim(block, lax.axis_index("seq") * half, half, 1)[None]
     rows = swap(rows, y=1)
-    line = jnp.stack([own] + [swap(own, z=z) for z in (1, 2, 3)])
-    line, rows = tie(line, rows)
-    across = swap(line, x=1)
-    plane = [line, swap(line, y=1), across, swap(across, y=1)]
+    line = [swap(own, z=z) for z in (1, 2, 3)]
+    own_x, own_y = swap(own, x=1), swap(own, y=1)
+    rest = jnp.concatenate(line)
+    rest, rows, own_x, own_y = tie(rest, rows, own_x, own_y)
+    rest_x = swap(rest, x=1)
     refs = []
-    for part in plane:
+    for part in (own, own_y, own_x, swap(own_x, y=1), rest, swap(rest, y=1), rest_x, swap(rest_x, y=1)):
         refs += [part, swap(part, core=1)]
     whole, small = pl.pallas_call(
         functools.partial(assemble_kernel, columns - SMALL_PAD),
@@ -741,7 +780,7 @@
         compiler_params=pltpu.CompilerParams(vmem_limit_bytes=VMEM),
         name="assemble",
     )(*refs)
-    return whole.reshape(16 * shard, columns), small, rows
+    return whole.reshape(16 * shard, columns), small, rows, later
 
 
 def total(pieces):
@@ -768,6 +807,10 @@
 def line_pieces(line):
     z = place()[0]
     return [lax.dynamic_index_in_dim(line, z ^ step, 0, keepdims=False) for step in range(4)]
+
+
+def half_line(line, bit):
+    return lax.dynamic_slice_in_dim(line, bit * (line.shape[0] // 2), line.shape[0] // 2, 0)
 
 
 def line_swaps(pieces):
@@ -795,8 +838,8 @@
     width = bias_up.shape[0] * owners
     pieces = width // dim
 
-    up_down = gather(
-        jnp.concatenate([w_up, w_down.reshape(pieces, shard, dim).swapaxes(0, 1).reshape(shard, width)], axis=1)
+    up_down = jnp.concatenate(
+        [w_up, w_down.reshape(pieces, shard, dim).swapaxes(0, 1).reshape(shard, width)], axis=1
     )
     rows_small = jnp.concatenate(
         [jnp.stack([ln1_gain, ln1_bias, bias_q, bias_v, bias_out, ln2_gain, ln2_bias, bias_down])]
@@ -808,12 +851,13 @@
         jnp.pad(token_mask.astype(LOW), ((0, 0), (0, dim - shard_rows)))[:, None, :], (2, 16, dim)
     )
     own, away = own_and_away(jnp.concatenate([tokens, mask_rows], axis=1))
-    first, small, away = gather_links(jnp.concatenate([w_qkv, w_out, padding], axis=1), away)
+    first, small, away, up_down = gather_links(jnp.concatenate([w_qkv, w_out, padding], axis=1), away, up_down)
+    up_down = gather(up_down)
     masked = jnp.where(token_mask[..., None] > 0, cotangent, jnp.zeros_like(cotangent))
     own_in, away_in = own_and_away(masked)
     first, away_in = tie(first, away_in)
     down_in = jnp.concatenate([own_in, swap(away_in, y=1)], axis=0)
-    qkv_full, out_full = first[:, : 3 * dim], first[:, 3 * dim : 4 * dim]
+    out_full = first[:, 3 * dim : 4 * dim]
     gain_one, shift_one, query_bias, value_bias, out_bias, gain_two, shift_two, down_bias = [
         small[i : i + 1] for i in range(8)
     ]
@@ -823,16 +867,15 @@
     inputs_low = both[:, :shard_rows].reshape(2 * shard_rows, dim)
     inputs = inputs_low.astype(F32)
     mask_column = both[:, shard_rows, :shard_rows].astype(F32).reshape(2 * shard_rows, 1)
-    unit_one, _ = norm_parts(inputs)
-    normed = (unit_one * gain_one + shift_one).astype(LOW)
-    qkv_bias = jnp.concatenate([query_bias, jnp.zeros_like(query_bias), value_bias], axis=1)
-    qkv = (dot_nn(normed, qkv_full) + qkv_bias).astype(LOW)
-    merged, logs = attention_forward(qkv, mask_column)
+    merged, logs, *qkv = attention_forward(
+        inputs_low, gain_one, shift_one, first, query_bias, value_bias, mask_column
+    )
     middle = inputs + dot_nn(merged, out_full) + out_bias
     unit_two, _ = norm_parts(middle)
     second = (unit_two * gain_two + shift_two).astype(LOW)
-    mlp_out, down_kept, down_sent, pre_grad, grad_up_bias = mlp_first(second, down_in, up_down, up_bias, owners)
-    output = middle + mlp_out + down_bias
+    output, down_kept, down_sent, pre_grad, grad_up_bias = mlp_first(
+        second, down_in, up_down, up_bias, middle, down_bias, owners
+    )
     output_own, output_away = output[:shard_rows], output[shard_rows:].astype(LOW)
     pre_grad, output_away, down_sent = tie(pre_grad, output_away, down_sent)
     output_back, down_sent = swap(output_away, y=1), swap(down_sent, core=1)
@@ -841,54 +884,64 @@
     down_pieces = plane_pieces(total([down_kept, down_sent]))
     second_grad, up_sent, *down_pieces = tie(second_grad, up_sent, *down_pieces)
     down_pieces, up_sent = plane_swaps(down_pieces), swap(up_sent, core=1)
-    middle_grad, merged_grad, grad_out, small_grads = middle_backward(
-        middle, second_grad, down_in, gain_two, first, merged
-    )
-    middle_grad, merged_grad, grad_out, small_grads, up_sent = tie(
-        middle_grad, merged_grad, grad_out, small_grads, up_sent
-    )
-    up_pieces = plane_pieces(total([up_kept, up_sent]))
-    merged_grad, *up_pieces = tie(merged_grad, *up_pieces)
-    up_pieces = plane_swaps(up_pieces)
+    middle_grad, merged_grad, out_kept, out_sent, small_grads = middle_backward(
+        middle, second_grad, down_in, gain_two, first, merged, owners
+    )
+    middle_grad, merged_grad, out_kept, out_sent, small_grads, up_sent = tie(
+        middle_grad, merged_grad, out_kept, out_sent, small_grads, up_sent
+    )
+    out_sent = swap(out_sent, core=1)
+    up_paired = total([up_kept, up_sent])
+    merged_grad, up_paired = tie(merged_grad, up_paired)
     pairs = HEADS // 2
     grads_low = attention_backward(qkv, mask_column, logs, merged_grad, 0, pairs // 2)
-    tied = tie(merged_grad, *grads_low, *down_pieces)
-    merged_grad, grads_low, down_pieces = tied[0], tied[1:4], tied[4:]
-    down_pieces = line_pieces(total(down_pieces))
-    merged_grad, *down_pieces = tie(merged_grad, *down_pieces)
-    down_pieces = line_swaps(down_pieces)
+    tied = tie(merged_grad, out_sent, *grads_low)
+    merged_grad, grads_low = tied[0], tied[2:]
+    up_pieces = [
+        jnp.concatenate(both, axis=2)
+        for both in zip(plane_pieces(up_paired), plane_pieces(total([out_kept, tied[1]])))
+    ]
+    tied = tie(merged_grad, *down_pieces, *up_pieces)
+    merged_grad, down_line, up_pieces = tied[0], total(tied[1:5]), tied[5:]
+    z = place()[0]
+    merged_grad, down_away, *up_pieces = tie(merged_grad, half_line(down_line, 1 - z // 2), *up_pieces)
+    down_away, up_pieces = swap(down_away, z=2), plane_swaps(up_pieces)
     grads_high = attention_backward(qkv, mask_column, logs, merged_grad, pairs // 2, pairs - pairs // 2)
-    tied = tie(*grads_high, *down_pieces)
-    grads_high, down_own = tied[:3], total(tied[3:])
-    up_bias_rows = grad_up_bias.reshape(owners, pieces, shard).swapaxes(0, 1).reshape(pieces, dim)
-    up_bias_rows, down_own = tie(up_bias_rows, down_own)
-    down_other = swap(down_own, y=1)
+    *grads_high, down_away = tie(*grads_high, down_away)
+    down_two = total([half_line(down_line, z // 2), down_away])
+    grad_up_bias, down_away = tie(grad_up_bias, half_line(down_two, 1 - z % 2))
+    down_away = swap(down_away, z=1)
     input_grad, last_kept, last_sent = last_backward(
-        inputs_low, gain_one, shift_one, grads_low, grads_high, first, middle_grad, grad_out, small_grads,
-        up_bias_rows, owners,
-    )
-    tied = tie(input_grad, last_kept, last_sent, down_other, *up_pieces)
-    input_grad, last_kept, last_sent, down_other = tied[:4]
-    up_pieces = line_pieces(total(tied[4:]))
+        inputs_low, gain_one, shift_one, grads_low, grads_high, first, middle_grad, small_grads, grad_up_bias, owners
+    )
+    tied = tie(input_grad, last_kept, last_sent, down_away, *up_pieces)
+    input_grad, last_kept, last_sent, down_away = tied[:4]
+    up_line = total(tied[4:])
+    input_away = input_grad[shard_rows:].astype(LOW)
     last_sent = swap(last_sent, core=1)
     last_pieces = plane_pieces(total([last_kept, last_sent]))
-    tied = tie(*last_pieces, *up_pieces)
+    tied = tie(*last_pieces, *line_pieces(up_line))
     last_pieces, up_pieces = plane_swaps(tied[:4]), line_swaps(tied[4:])
-    tied = tie(input_grad, *last_pieces, *up_pieces)
-    input_grad, last_pieces, up_own = tied[0], line_pieces(total(tied[1:5])), total(tied[5:])
-    input_away = input_grad[shard_rows:].astype(LOW)
-    tied = tie(input_away, up_own, *last_pieces)
-    input_away, up_own, last_pieces = tied[0], tied[1], tied[2:]
-    last_pieces = line_swaps(last_pieces)
-    input_back, up_other = swap(input_away, y=1), swap(up_own, y=1)
+    down_own = total([half_line(down_two, z % 2), down_away])[0]
+    mlp_own = jnp.concatenate([down_own, total(up_pieces)], axis=1)
+    tied = tie(input_away, *last_pieces)
+    input_away, last_pieces = tied[0], line_pieces(total(tied[1:]))
+    tied = tie(input_away, mlp_own, *last_pieces)
+    input_away, mlp_own, last_pieces = tied[0], tied[1], line_swaps(tied[2:])
+    mlp_other, input_back = swap(mlp_own, y=1), swap(input_away, y=1)
+    tied = tie(mlp_other, input_back, *last_pieces)
+    mlp_other, input_back, last_pieces = tied[0], tied[1], tied[2:]
     last_own = total(last_pieces)
     last_sum = join_halves(last_own, swap(last_own, y=1))
-    smalls = last_sum[:, 4 * dim : 4 * dim + count].T
+    down_sum = join_halves(mlp_own[:, : width // 2], mlp_other[:, : width // 2])
+    up_sum = join_halves(mlp_own[:, width // 2 : width], mlp_other[:, width // 2 : width])
+    out_sum = join_halves(mlp_own[:, width:], mlp_other[:, width:])
+    smalls = last_sum[:, 3 * dim : 3 * dim + 8].T
     return (
         both_images(output_own, output_back), both_images(input_grad[:shard_rows], input_back),
-        smalls[0], smalls[1], last_sum[:, : 3 * dim], smalls[2], smalls[3], last_sum[:, 3 * dim : 4 * dim],
-        smalls[4], smalls[5], smalls[6], join_halves(up_own, up_other), smalls[8:].reshape(-1),
-        join_halves(down_own, down_other), smalls[7],
+        smalls[0], smalls[1], last_sum[:, : 3 * dim], smalls[2], smalls[3], out_sum,
+        smalls[4], smalls[5], smalls[6], up_sum, last_sum[:, 3 * dim + 128 : 3 * dim + 128 + pieces].T.reshape(-1),
+        down_sum.reshape(shard, pieces, dim).swapaxes(0, 1).reshape(pieces * shard, dim), smalls[7],
     )
 
 

time: 298 us -> 287 us (0.963)
  starting transfers between devices: 50.5 us -> 41.7 us
  matrix products: 8.91 us -> 2.54 us
  Pallas kernels: 99.5 us -> 105 us
    ppermute x38 -> x44, starting transfers between devices: 50.4 us -> 41.7 us  [swap(): lax.ppermute(block, ('img', 'seq'), [(i, i ^ bits) for i in range(32)])]
    dot_general x2 -> x1, matrix products: 8.91 us -> 2.54 us  [dot_nn(): lax.dot_general(left, right, (((1,), (0,)), ((), ())), preferred_element_...]
    pallas_call x1, Pallas kernels: 13.4 us -> 18.1 us  [attention_forward(): pl.pallas_call(functools.partial(attention_forward_kernel, size ** (-0.5)...]
    all_gather x1, waiting for transfers between devices: 4.39 us -> 0.01 us  [gather(): return lax.all_gather(block, 'img', axis=0, tiled=True)]
    ppermute x38 -> x44, waiting for transfers between devices: 79.2 us -> 81.6 us  [swap(): lax.ppermute(block, ('img', 'seq'), [(i, i ^ bits) for i in range(32)])]
  transfers between devices with their start and end apart: 39 -> 45, of which waited for: 17 -> 13; matrix products, arithmetic and copies ran while one was open for 11% -> 8% of each run, Pallas kernels for 27% -> 30%
where the time goes in v3:
time: 287 us; the launch traced here: 283 us
  Pallas kernels  105 us (37%)
  waiting for transfers between devices  81.6 us (28%)
  starting transfers between devices  41.7 us (15%)
  other arithmetic  19.7 us (7%)
  local copies, waits for them, and re-layouts  16.8 us (6%)
  between operations  15.4 us (5%)
    ppermute x44, waiting for transfers between devices, swap(): lax.ppermute(block, ('img', 'seq'), [(i, i ^ bits) for i in range(32)])  81.6 us
    ppermute x44, starting transfers between devices, swap(): lax.ppermute(block, ('img', 'seq'), [(i, i ^ bits) for i in range(32)])  41.7 us
    pallas_call x2, Pallas kernels, attention_backward(): pl.pallas_call(functools.partial(attention_backward_kernel, size ** (-0.5...  26.5 us
    pallas_call x1, Pallas kernels, mlp_first(): pl.pallas_call(functools.partial(mlp_first_kernel, (some, pieces, dim)),...  21 us
    pallas_call x1, Pallas kernels, attention_forward(): pl.pallas_call(functools.partial(attention_forward_kernel, size ** (-0.5)...  18.1 us
    pallas_call x1, Pallas kernels, mlp_second(): pl.pallas_call(mlp_second_kernel, grid=(width // dim,), in_specs=[whole,...  13.5 us
    pallas_call x1, Pallas kernels, last_backward(): pl.pallas_call(last_kernel, grid=(1,), in_specs=[whole(rows, dim), whole(...  12.6 us
    pallas_call x1, Pallas kernels, middle_backward(): pl.pallas_call(middle_kernel, grid=(1,), in_specs=[whole, whole, whole, p...  8.28 us
  transfers between devices with their start and end apart: 45, of which 13 were waited for; matrix products, arithmetic and copies ran while one was open for 8% of the time, Pallas kernels for 30%

profile of v3, /device:TPU:0, one launch (start us, length us, event | category | flops | bytes accessed | tf_op | source)
XLA Modules:
  0.0 283.1 jit_solution(17763698289934398764)
XLA Ops:
  7.2 1.2 copy.47
  8.6 1.9 pad_maximum_fusion.5
  10.7 3.1 %collective-permute-start.3 = (bf16[344,768]{1,0:T(8,128)(2,1)S(1)}, bf16[344,768]{1,0:T(8,128)(2,1)S(1)}, u32[]{:S(2)}, u32[]{:S(2)}) collective-permute-start(bf16[344,768]{1,0:T(8,128)(2,1)S(1)} %get-tuple-element.270), channel_id=1, source_target_pairs={{0,1},{1,0},{2,3},{3,2},{4,5},{5,4},{6,7},{7,6},{8,9},{9,8},{10,11... | collective-permute-start | bytes 1585160 | tf_op jit(solution)/shard_map/ppermute | solution.py:744
  14.2 3.7 %collective-permute-start.2 = (bf16[1,48,1664]{2,1,0:T(8,128)(2,1)S(1)}, bf16[1,48,1664]{2,1,0:T(8,128)(2,1)S(1)}, u32[]{:S(2)}, u32[]{:S(2)}) collective-permute-start(bf16[1,48,1664]{2,1,0:T(8,128)(2,1)S(1)} %fusion.11.refs_0_), channel_id=1, source_target_pairs={{0,24},{1,25},{2,26},{3,27},{4,28},{5,29},{6,30},{7,31},{8,16},{9,... | collective-permute-start | bytes 479240 | tf_op jit(solution)/shard_map/ppermute | solution.py:744
  19.0 4.2 %collective-permute-done.2 = bf16[1,48,1664]{2,1,0:T(8,128)(2,1)S(1)} collective-permute-done((bf16[1,48,1664]{2,1,0:T(8,128)(2,1)S(1)}, bf16[1,48,1664]{2,1,0:T(8,128)(2,1)S(1)}, u32[]{:S(2)}, u32[]{:S(2)}) %collective-permute-start.2) | collective-permute-done | bytes 159776 | tf_op jit(solution)/shard_map/ppermute | solution.py:744
  23.2 1.5 collective-permute-start.4
  24.7 20.3 %collective-permute-done.1 = bf16[1,48,1664]{2,1,0:T(8,128)(2,1)S(1)} collective-permute-done((bf16[1,48,1664]{2,1,0:T(8,128)(2,1)S(1)}, bf16[1,48,1664]{2,1,0:T(8,128)(2,1)S(1)}, u32[]{:S(2)}, u32[]{:S(2)}) %collective-permute-start.1) | collective-permute-done | bytes 159776 | tf_op jit(solution)/shard_map/ppermute | solution.py:744
  45.1 1.6 collective-permute-start.14
  46.7 7.3 %collective-permute-done.14.refs_12_ = bf16[3,48,1664]{2,1,0:T(8,128)(2,1)} collective-permute-done((bf16[3,48,1664]{2,1,0:T(8,128)(2,1)S(1)}, bf16[3,48,1664]{2,1,0:T(8,128)(2,1)}, u32[]{:S(2)}, u32[]{:S(2)}) %collective-permute-start.14) | collective-permute-done | bytes 479264 | tf_op jit(solution)/shard_map/ppermute | solution.py:744
  54.5 2.0 collective-permute-start.9
  57.1 12.1 %collective-permute-done.9.refs_6_ = bf16[1,48,1664]{2,1,0:T(8,128)(2,1)} collective-permute-done((bf16[1,48,1664]{2,1,0:T(8,128)(2,1)S(1)}, bf16[1,48,1664]{2,1,0:T(8,128)(2,1)}, u32[]{:S(2)}, u32[]{:S(2)}) %collective-permute-start.9) | collective-permute-done | bytes 159776 | tf_op jit(solution)/shard_map/ppermute | solution.py:744
  73.9 5.3 %assemble.1 = (bf16[16,48,3328]{2,1,0:T(8,128)(2,1)}, f32[16,768]{1,0:T(8,128)}) custom-call(bf16[1,48,1664]{2,1,0:T(8,128)(2,1)} %copy-done.15, bf16[1,48,1664]{2,1,0:T(8,128)(2,1)} %copy-done.21, bf16[1,48,1664]{2,1,0:T(8,128)(2,1)} %copy-done.19, bf16[1,48,1664]{2,1,0:T(8,128)(2,1)} %copy-done.22, bf16[1,48,1664]{2,1,0:T(8,128)(2,1)} %copy-done.20, ...), custom_call_target="tpu_custom_call" | custom-call | tf_op jit(solution)/shard_map/assemble/pallas_call | solution.py:774
  80.7 1.7 slice_reduce_fusion.10
  82.4 18.1 %attention_forward.1 = (bf16[656,768]{1,0:T(8,128)(2,1)}, f32[6,2,656]{2,1,0:T(2,128)}, bf16[656,768]{1,0:T(8,128)(2,1)}, bf16[656,768]{1,0:T(8,128)(2,1)}, bf16[656,768]{1,0:T(8,128)(2,1)}) custom-call(bf16[656,768]{1,0:T(8,128)(2,1)} %bitcast.110, f32[1,768]{1,0:T(1,128)} %get-tuple-element.295.gain_ref, f32[1,768]{1,0:T(1,128)} %get-tuple-element.294.shift_ref, ...), custom_call_target="tpu_custom_call" | custom-call | flops 18400000000 | bytes 1 | tf_op jit(solution)/shard_map/attention_forward/pallas_call | solution.py:379
  100.5 2.5 add_add_fusion.middle_ref
  104.3 1.4 add_convert_fusion.3.second_ref
  105.7 2.1 pad_maximum_fusion.dz_ref
  107.8 21.0 %mlp_first.1 = (f32[656,768]{1,0:T(8,128)}, bf16[4,2,48,3072]{3,2,1,0:T(8,128)(2,1)}, bf16[4,2,48,3072]{3,2,1,0:T(8,128)(2,1)}, bf16[656,3072]{1,0:T(8,128)(2,1)}, bf16[768,128]{1,0:T(8,128)(2,1)}) custom-call(bf16[656,768]{1,0:T(8,128)(2,1)} %add_convert_fusion.3.second_ref, bf16[656,768]{1,0:T(8,128)(2,1)} %pad_maximum_fusion.dz_ref, ...), custom_call_target="tpu_custom_call" | custom-call | flops 21849999360 | bytes 1 | tf_op jit(solution)/shard_map/mlp_first/pallas_call | solution.py:527
  128.8 1.3 slice.175
  130.3 2.0 collective-permute-start.19
  132.3 13.5 %mlp_second.1 = (f32[656,768]{1,0:T(8,128)}, bf16[4,2,48,3072]{3,2,1,0:T(8,128)(2,1)}, bf16[4,2,48,3072]{3,2,1,0:T(8,128)(2,1)}) custom-call(bf16[656,768]{1,0:T(8,128)(2,1)} %add_convert_fusion.3.second_ref, bf16[656,3072]{1,0:T(8,128)(2,1)} %get-tuple-element.143.pre_grad_ref, bf16[768,6144]{1,0:T(8,128)(2,1)} %all-gather.2.cloned.1.call-done.up_ref), custom_call_target="tpu_custom_call" | custom-call | flops 1150000000 | bytes 1 | tf_op jit(solution)/shard_map/mlp_second/pallas_call | solution.py:582
  146.8 1.3 dynamic-slice_bitcast_fusion.4
  149.1 2.7 collective-permute-start.25
  151.8 8.3 %middle_backward.1 = (f32[656,768]{1,0:T(8,128)}, bf16[656,768]{1,0:T(8,128)(2,1)}, bf16[4,2,48,768]{3,2,1,0:T(8,128)(2,1)}, bf16[4,2,48,768]{3,2,1,0:T(8,128)(2,1)}, f32[4,768]{1,0:T(4,128)}) custom-call(f32[656,768]{1,0:T(8,128)} %copy-done, f32[656,768]{1,0:T(8,128)} %get-tuple-element.154.grad_ref, bf16[656,768]{1,0:T(8,128)(2,1)} %pad_maximum_fusion.dz_ref, ...), custom_call_target="tpu_custom_call" | custom-call | flops 1150000000 | bytes 1 | tf_op jit(solution)/shard_map/middle_backward/pallas_call | solution.py:643
  161.0 13.2 %attention_backward.2 = (bf16[656,384]{1,0:T(8,128)(2,1)}, bf16[656,384]{1,0:T(8,128)(2,1)}, bf16[656,384]{1,0:T(8,128)(2,1)}) custom-call(bf16[656,768]{1,0:T(8,128)(2,1)} %get-tuple-element.166.query_ref, bf16[656,768]{1,0:T(8,128)(2,1)} %get-tuple-element.167.key_ref, bf16[656,768]{1,0:T(8,128)(2,1)} %get-tuple-element.168.value_ref, ...), custom_call_target="tpu_custom_call" | custom-call | flops 1150000000 | bytes 1 | tf_op jit(solution)/shard_map/attention_backward/pallas_call | solution.py:447
  177.0 1.7 add_convert_fusion.5
  178.9 1.6 collective-permute-start.28
  180.8 1.7 collective-permute-start.30
  182.4 13.4 %attention_backward.3 = (bf16[656,384]{1,0:T(8,128)(2,1)}, bf16[656,384]{1,0:T(8,128)(2,1)}, bf16[656,384]{1,0:T(8,128)(2,1)}) custom-call(bf16[656,768]{1,0:T(8,128)(2,1)} %get-tuple-element.166.query_ref, bf16[656,768]{1,0:T(8,128)(2,1)} %get-tuple-element.167.key_ref, bf16[656,768]{1,0:T(8,128)(2,1)} %get-tuple-element.168.value_ref, ...), custom_call_target="tpu_custom_call" | custom-call | flops 1150000000 | bytes 1 | tf_op jit(solution)/shard_map/attention_backward/pallas_call | solution.py:447
  195.9 1.6 collective-permute-start.27
  197.5 12.6 %last_backward.1 = (f32[656,768]{1,0:T(8,128)}, bf16[4,2,48,2560]{3,2,1,0:T(8,128)(2,1)}, bf16[4,2,48,2560]{3,2,1,0:T(8,128)(2,1)}) custom-call(bf16[656,768]{1,0:T(8,128)(2,1)} %bitcast.111, f32[1,768]{1,0:T(1,128)} %get-tuple-element.295.gain_ref, f32[1,768]{1,0:T(1,128)} %get-tuple-element.294.shift_ref, bf16[656,384]{1,0:T(8,128)(2,1)} %get-tuple-element.173.q_low, ...), custom_call_target="tpu_custom_call" | custom-call | flops 1150000000 | bytes 1 | tf_op jit(solution)/shard_map/last_backward/pallas_call | solution.py:706
  210.2 3.4 %collective-permute-done.30 = bf16[4,48,1920]{2,1,0:T(8,128)(2,1)S(1)} collective-permute-done((bf16[4,48,1920]{2,1,0:T(8,128)(2,1)S(1)}, bf16[4,48,1920]{2,1,0:T(8,128)(2,1)S(1)}, u32[]{:S(2)}, u32[]{:S(2)}) %collective-permute-start.30) | collective-permute-done | bytes 737312 | tf_op jit(solution)/shard_map/ppermute | solution.py:744
  214.5 1.4 slice_bitcast_fusion.1
  217.6 1.1 collective-permute-done.31
  219.4 1.4 collective-permute-start.35
  220.8 1.3 collective-permute-start.36
  222.1 1.8 collective-permute-start.37
  223.9 1.7 collective-permute-start.32
  226.1 4.0 %collective-permute-done.35 = bf16[48,1920]{1,0:T(8,128)(2,1)S(1)} collective-permute-done((bf16[48,1920]{1,0:T(8,128)(2,1)S(1)}, bf16[48,1920]{1,0:T(8,128)(2,1)S(1)}, u32[]{:S(2)}, u32[]{:S(2)}) %collective-permute-start.35) | collective-permute-done | bytes 184352 | tf_op jit(solution)/shard_map/ppermute | solution.py:744
  230.0 1.7 collective-permute-start.34
  231.7 5.4 %collective-permute-done.36 = bf16[48,1920]{1,0:T(8,128)(2,1)S(1)} collective-permute-done((bf16[48,1920]{1,0:T(8,128)(2,1)S(1)}, bf16[48,1920]{1,0:T(8,128)(2,1)S(1)}, u32[]{:S(2)}, u32[]{:S(2)}) %collective-permute-start.36) | collective-permute-done | bytes 184352 | tf_op jit(solution)/shard_map/ppermute | solution.py:744
  238.1 10.4 %collective-permute-done.33 = bf16[4,48,1280]{2,1,0:T(8,128)(2,1)S(1)} collective-permute-done((bf16[4,48,1280]{2,1,0:T(8,128)(2,1)S(1)}, bf16[4,48,1280]{2,1,0:T(8,128)(2,1)S(1)}, u32[]{:S(2)}, u32[]{:S(2)}) %collective-permute-start.33) | collective-permute-done | bytes 491552 | tf_op jit(solution)/shard_map/ppermute | solution.py:744
  250.0 2.4 collective-permute-start.41
  252.5 1.5 collective-permute-start.42
  253.9 1.6 collective-permute-start.38
  255.6 5.2 %collective-permute-done.41 = bf16[48,1280]{1,0:T(8,128)(2,1)S(1)} collective-permute-done((bf16[48,1280]{1,0:T(8,128)(2,1)S(1)}, bf16[48,1280]{1,0:T(8,128)(2,1)S(1)}, u32[]{:S(2)}, u32[]{:S(2)}) %collective-permute-start.41) | collective-permute-done | bytes 122912 | tf_op jit(solution)/shard_map/ppermute | solution.py:744
  260.7 6.9 %collective-permute-done.38 = bf16[48,3456]{1,0:T(8,128)(2,1)S(1)} collective-permute-done((bf16[48,3456]{1,0:T(8,128)(2,1)S(1)}, bf16[48,3456]{1,0:T(8,128)(2,1)S(1)}, u32[]{:S(2)}, u32[]{:S(2)}) %collective-permute-start.38) | collective-permute-done | bytes 331808 | tf_op jit(solution)/shard_map/ppermute | solution.py:744
  270.2 2.3 maximum_select_fusion
  (199 shorter events, 28.7 us)
Async XLA Ops:
  7.2 100.6 %all-gather.2.cloned.1.call-start = ((), (), s32[]{:S(2)}) async-start(), calls=%async_computation | async-start | bytes 10027008 | tf_op jit(solution)/shard_map/all_gather | solution.py:734
  10.5 59.2 %copy-start.7 = (bf16[2,328,768]{2,1,0:T(8,128)(2,1)S(1)}, bf16[2,328,768]{2,1,0:T(8,128)(2,1)}, u32[]{:S(2)}) copy-start(bf16[2,328,768]{2,1,0:T(8,128)(2,1)} %param.31) | copy-start | bytes 3022852
  10.7 34.4 %collective-permute-start.3 = (bf16[344,768]{1,0:T(8,128)(2,1)S(1)}, bf16[344,768]{1,0:T(8,128)(2,1)S(1)}, u32[]{:S(2)}, u32[]{:S(2)}) collective-permute-start(bf16[344,768]{1,0:T(8,128)(2,1)S(1)} %get-tuple-element.270), channel_id=1, source_target_pairs={{0,1},{1,0},{2,3},{3,2},{4,5},{5,4},{6,7},{7,6},{8,9},{9,8},{10,11... | collective-permute-start | bytes 1585160 | tf_op jit(solution)/shard_map/ppermute | solution.py:744
  14.2 57.0 %copy-start.15 = (bf16[1,48,1664]{2,1,0:T(8,128)(2,1)}, bf16[1,48,1664]{2,1,0:T(8,128)(2,1)S(1)}, u32[]{:S(2)}) copy-start(bf16[1,48,1664]{2,1,0:T(8,128)(2,1)S(1)} %fusion.11.refs_0_) | copy-start | bytes 479236
  14.2 9.0 %collective-permute-start.2 = (bf16[1,48,1664]{2,1,0:T(8,128)(2,1)S(1)}, bf16[1,48,1664]{2,1,0:T(8,128)(2,1)S(1)}, u32[]{:S(2)}, u32[]{:S(2)}) collective-permute-start(bf16[1,48,1664]{2,1,0:T(8,128)(2,1)S(1)} %fusion.11.refs_0_), channel_id=1, source_target_pairs={{0,24},{1,25},{2,26},{3,27},{4,28},{5,29},{6,30},{7,31},{8,16},{9,... | collective-permute-start | bytes 479240 | tf_op jit(solution)/shard_map/ppermute | solution.py:744
  17.9 27.0 %collective-permute-start.1 = (bf16[1,48,1664]{2,1,0:T(8,128)(2,1)S(1)}, bf16[1,48,1664]{2,1,0:T(8,128)(2,1)S(1)}, u32[]{:S(2)}, u32[]{:S(2)}) collective-permute-start(bf16[1,48,1664]{2,1,0:T(8,128)(2,1)S(1)} %fusion.11.refs_0_), channel_id=1, source_target_pairs={{0,16},{1,17},{2,18},{3,19},{4,20},{5,21},{6,22},{7,23},{8,24},{9,... | collective-permute-start | bytes 479240 | tf_op jit(solution)/shard_map/ppermute | solution.py:744
  17.9 27.0 %collective-permute-start = (bf16[1,48,1664]{2,1,0:T(8,128)(2,1)S(1)}, bf16[1,48,1664]{2,1,0:T(8,128)(2,1)S(1)}, u32[]{:S(2)}, u32[]{:S(2)}) collective-permute-start(bf16[1,48,1664]{2,1,0:T(8,128)(2,1)S(1)} %fusion.11.refs_0_), channel_id=1, source_target_pairs={{0,8},{1,9},{2,10},{3,11},{4,12},{5,13},{6,14},{7,15},{8,0},{9,1},... | collective-permute-start | bytes 479240 | tf_op jit(solution)/shard_map/ppermute | solution.py:744
  18.7 26.3 %collective-permute-start.5 = (bf16[1,48,1664]{2,1,0:T(8,128)(2,1)S(1)}, bf16[1,48,1664]{2,1,0:T(8,128)(2,1)S(1)}, u32[]{:S(2)}, u32[]{:S(2)}) collective-permute-start(bf16[1,48,1664]{2,1,0:T(8,128)(2,1)S(1)} %fusion.11.refs_0_), channel_id=1, source_target_pairs={{0,1},{1,0},{2,3},{3,2},{4,5},{5,4},{6,7},{7,6},{8,9},{9,8},{10,11... | collective-permute-start | bytes 479240 | tf_op jit(solution)/shard_map/ppermute | solution.py:744
  23.2 21.9 %collective-permute-start.4 = (bf16[1,48,1664]{2,1,0:T(8,128)(2,1)S(1)}, bf16[1,48,1664]{2,1,0:T(8,128)(2,1)S(1)}, u32[]{:S(2)}, u32[]{:S(2)}) collective-permute-start(bf16[1,48,1664]{2,1,0:T(8,128)(2,1)S(1)} %fusion.11.refs_0_), channel_id=1, source_target_pairs={{0,4},{1,5},{2,6},{3,7},{4,0},{5,1},{6,2},{7,3},{8,12},{9,13},{10,... | collective-permute-start | bytes 479240 | tf_op jit(solution)/shard_map/ppermute | solution.py:744
  45.0 26.2 %copy-start.5 = (bf16[3,48,1664]{2,1,0:T(8,128)(2,1)}, bf16[3,48,1664]{2,1,0:T(8,128)(2,1)S(1)}, u32[]{:S(2)}) copy-start(bf16[3,48,1664]{2,1,0:T(8,128)(2,1)S(1)} %pad_maximum_fusion.6.refs_8_) | copy-start | bytes 1437700
  45.1 8.9 %collective-permute-start.14 = (bf16[3,48,1664]{2,1,0:T(8,128)(2,1)S(1)}, bf16[3,48,1664]{2,1,0:T(8,128)(2,1)}, u32[]{:S(2)}, u32[]{:S(2)}) collective-permute-start(bf16[3,48,1664]{2,1,0:T(8,128)(2,1)S(1)} %pad_maximum_fusion.6.refs_8_), channel_id=1, source_target_pairs={{0,4},{1,5},{2,6},{3,7},{4,0},{5,1},{6,2},{7,3},{8,12},{9,13},{10,... | collective-permute-start | bytes 1437704 | tf_op jit(solution)/shard_map/ppermute | solution.py:744
  46.7 22.5 %collective-permute-start.12 = (bf16[3,48,1664]{2,1,0:T(8,128)(2,1)S(1)}, bf16[3,48,1664]{2,1,0:T(8,128)(2,1)}, u32[]{:S(2)}, u32[]{:S(2)}) collective-permute-start(bf16[3,48,1664]{2,1,0:T(8,128)(2,1)S(1)} %pad_maximum_fusion.6.refs_8_), channel_id=1, source_target_pairs={{0,1},{1,0},{2,3},{3,2},{4,5},{5,4},{6,7},{7,6},{8,9},{9,8},{10,11... | collective-permute-start | bytes 1437704 | tf_op jit(solution)/shard_map/ppermute | solution.py:744
  54.0 15.7 %collective-permute-start.16 = (bf16[3,48,1664]{2,1,0:T(8,128)(2,1)}, bf16[3,48,1664]{2,1,0:T(8,128)(2,1)}, u32[]{:S(2)}, u32[]{:S(2)}) collective-permute-start(bf16[3,48,1664]{2,1,0:T(8,128)(2,1)} %collective-permute-done.14.refs_12_), channel_id=1, source_target_pairs={{0,1},{1,0},{2,3},{3,2},{4,5},{5,4},{6,7},{7,6},{8,9},{9,8},{10,11... | collective-permute-start | bytes 1437704 | tf_op jit(solution)/shard_map/ppermute | solution.py:744
  54.0 2.5 collective-permute-start.6
  54.0 2.6 collective-permute-start.7
  54.5 14.7 %collective-permute-start.9 = (bf16[1,48,1664]{2,1,0:T(8,128)(2,1)S(1)}, bf16[1,48,1664]{2,1,0:T(8,128)(2,1)}, u32[]{:S(2)}, u32[]{:S(2)}) collective-permute-start(bf16[1,48,1664]{2,1,0:T(8,128)(2,1)S(1)} %collective-permute-done.4.refs_4_), channel_id=1, source_target_pairs={{0,1},{1,0},{2,3},{3,2},{4,5},{5,4},{6,7},{7,6},{8,9},{9,8},{10,11... | collective-permute-start | bytes 479240 | tf_op jit(solution)/shard_map/ppermute | solution.py:744
  56.5 13.4 %collective-permute-start.8 = (bf16[1,48,1664]{2,1,0:T(8,128)(2,1)S(1)}, bf16[1,48,1664]{2,1,0:T(8,128)(2,1)S(1)}, u32[]{:S(2)}, u32[]{:S(2)}) collective-permute-start(bf16[1,48,1664]{2,1,0:T(8,128)(2,1)S(1)} %collective-permute-done.4.refs_4_), channel_id=1, source_target_pairs={{0,2},{1,3},{2,0},{3,1},{4,6},{5,7},{6,4},{7,5},{8,10},{9,11},{10,... | collective-permute-start | bytes 479240 | tf_op jit(solution)/shard_map/ppermute | solution.py:744
  56.6 16.6 %collective-permute-start.11 = (bf16[3,48,1664]{2,1,0:T(8,128)(2,1)S(1)}, bf16[3,48,1664]{2,1,0:T(8,128)(2,1)}, u32[]{:S(2)}, u32[]{:S(2)}) collective-permute-start(bf16[3,48,1664]{2,1,0:T(8,128)(2,1)S(1)} %pad_maximum_fusion.6.refs_8_), channel_id=1, source_target_pairs={{0,2},{1,3},{2,0},{3,1},{4,6},{5,7},{6,4},{7,5},{8,10},{9,11},{10,... | collective-permute-start | bytes 1437704 | tf_op jit(solution)/shard_map/ppermute | solution.py:744
  69.2 4.1 %collective-permute-start.15 = (bf16[3,48,1664]{2,1,0:T(8,128)(2,1)}, bf16[3,48,1664]{2,1,0:T(8,128)(2,1)}, u32[]{:S(2)}, u32[]{:S(2)}) collective-permute-start(bf16[3,48,1664]{2,1,0:T(8,128)(2,1)} %collective-permute-done.14.refs_12_), channel_id=1, source_target_pairs={{0,2},{1,3},{2,0},{3,1},{4,6},{5,7},{6,4},{7,5},{8,10},{9,11},{10,... | collective-permute-start | bytes 1437704 | tf_op jit(solution)/shard_map/ppermute | solution.py:744
  69.2 4.1 %collective-permute-start.13 = (bf16[3,48,1664]{2,1,0:T(8,128)(2,1)}, bf16[3,48,1664]{2,1,0:T(8,128)(2,1)}, u32[]{:S(2)}, u32[]{:S(2)}) collective-permute-start(bf16[3,48,1664]{2,1,0:T(8,128)(2,1)} %collective-permute-done.12.refs_10_), channel_id=1, source_target_pairs={{0,2},{1,3},{2,0},{3,1},{4,6},{5,7},{6,4},{7,5},{8,10},{9,11},{10,... | collective-permute-start | bytes 1437704 | tf_op jit(solution)/shard_map/ppermute | solution.py:744
  69.7 3.6 %collective-permute-start.17 = (bf16[3,48,1664]{2,1,0:T(8,128)(2,1)}, bf16[3,48,1664]{2,1,0:T(8,128)(2,1)}, u32[]{:S(2)}, u32[]{:S(2)}) collective-permute-start(bf16[3,48,1664]{2,1,0:T(8,128)(2,1)} %collective-permute-done.16.refs_14_), channel_id=1, source_target_pairs={{0,2},{1,3},{2,0},{3,1},{4,6},{5,7},{6,4},{7,5},{8,10},{9,11},{10,... | collective-permute-start | bytes 1437704 | tf_op jit(solution)/shard_map/ppermute | solution.py:744
  70.6 2.6 collective-permute-start.10
  80.7 25.0 %collective-permute-start.18 = (bf16[328,768]{1,0:T(8,128)(2,1)S(1)}, bf16[328,768]{1,0:T(8,128)(2,1)}, u32[]{:S(2)}, u32[]{:S(2)}) collective-permute-start(bf16[328,768]{1,0:T(8,128)(2,1)S(1)} %get-tuple-element.139), channel_id=1, source_target_pairs={{0,1},{1,0},{2,3},{3,2},{4,5},{5,4},{6,7},{7,6},{8,9},{9,8},{10,11... | collective-permute-start | bytes 1511432 | tf_op jit(solution)/shard_map/ppermute | solution.py:744
  130.1 15.7 %collective-permute-start.20 = (bf16[4,2,48,3072]{3,2,1,0:T(8,128)(2,1)}, bf16[4,2,48,3072]{3,2,1,0:T(8,128)(2,1)S(1)}, u32[]{:S(2)}, u32[]{:S(2)}) collective-permute-start(bf16[4,2,48,3072]{3,2,1,0:T(8,128)(2,1)} %get-tuple-element.148), channel_id=1, source_target_pairs={{0,2},{1,3},{2,0},{3,1},{4,6},{5,7},{6,4},{7,5},{8,10},{9,11},{10,... | collective-permute-start | bytes 7077896 | tf_op jit(solution)/shard_map/ppermute | solution.py:744
  130.3 15.6 %collective-permute-start.19 = (bf16[328,768]{1,0:T(8,128)(2,1)S(1)}, bf16[328,768]{1,0:T(8,128)(2,1)S(1)}, u32[]{:S(2)}, u32[]{:S(2)}) collective-permute-start(bf16[328,768]{1,0:T(8,128)(2,1)S(1)} %slice.175), channel_id=1, source_target_pairs={{0,1},{1,0},{2,3},{3,2},{4,5},{5,4},{6,7},{7,6},{8,9},{9,8},{10,11... | collective-permute-start | bytes 1511432 | tf_op jit(solution)/shard_map/ppermute | solution.py:744
  148.1 12.0 %collective-permute-start.21 = (bf16[4,2,48,3072]{3,2,1,0:T(8,128)(2,1)}, bf16[4,2,48,3072]{3,2,1,0:T(8,128)(2,1)S(1)}, u32[]{:S(2)}, u32[]{:S(2)}) collective-permute-start(bf16[4,2,48,3072]{3,2,1,0:T(8,128)(2,1)} %get-tuple-element.160), channel_id=1, source_target_pairs={{0,2},{1,3},{2,0},{3,1},{4,6},{5,7},{6,4},{7,5},{8,10},{9,11},{10,... | collective-permute-start | bytes 7077896 | tf_op jit(solution)/shard_map/ppermute | solution.py:744
  148.3 28.3 %collective-permute-start.23 = (bf16[4,48,1536]{2,1,0:T(8,128)(2,1)}, bf16[4,48,1536]{2,1,0:T(8,128)(2,1)}, u32[]{:S(2)}, u32[]{:S(2)}) collective-permute-start(bf16[4,48,1536]{2,1,0:T(8,128)(2,1)} %get-tuple-element.178), channel_id=1, source_target_pairs={{0,4},{1,5},{2,6},{3,7},{4,0},{5,1},{6,2},{7,3},{8,12},{9,13},{10,... | collective-permute-start | bytes 1769480 | tf_op jit(solution)/shard_map/ppermute | solution.py:744
  148.8 28.2 %collective-permute-start.24 = (bf16[4,48,1536]{2,1,0:T(8,128)(2,1)}, bf16[4,48,1536]{2,1,0:T(8,128)(2,1)}, u32[]{:S(2)}, u32[]{:S(2)}) collective-permute-start(bf16[4,48,1536]{2,1,0:T(8,128)(2,1)} %get-tuple-element.179), channel_id=1, source_target_pairs={{0,1},{1,0},{2,3},{3,2},{4,5},{5,4},{6,7},{7,6},{8,9},{9,8},{10,11... | collective-permute-start | bytes 1769480 | tf_op jit(solution)/shard_map/ppermute | solution.py:744
  149.1 28.0 %collective-permute-start.25 = (bf16[4,48,1536]{2,1,0:T(8,128)(2,1)}, bf16[4,48,1536]{2,1,0:T(8,128)(2,1)}, u32[]{:S(2)}, u32[]{:S(2)}) collective-permute-start(bf16[4,48,1536]{2,1,0:T(8,128)(2,1)} %get-tuple-element.180), channel_id=1, source_target_pairs={{0,5},{1,4},{2,7},{3,6},{4,1},{5,0},{6,3},{7,2},{8,13},{9,12},{10,... | collective-permute-start | bytes 1769480 | tf_op jit(solution)/shard_map/ppermute | solution.py:744
  160.1 14.3 %collective-permute-start.22 = (bf16[4,2,48,768]{3,2,1,0:T(8,128)(2,1)}, bf16[4,2,48,768]{3,2,1,0:T(8,128)(2,1)S(1)}, u32[]{:S(2)}, u32[]{:S(2)}) collective-permute-start(bf16[4,2,48,768]{3,2,1,0:T(8,128)(2,1)} %get-tuple-element.165), channel_id=1, source_target_pairs={{0,2},{1,3},{2,0},{3,1},{4,6},{5,7},{6,4},{7,5},{8,10},{9,11},{10,... | collective-permute-start | bytes 1769480 | tf_op jit(solution)/shard_map/ppermute | solution.py:744
  178.8 17.0 %collective-permute-start.26 = (bf16[2,48,1536]{2,1,0:T(8,128)(2,1)S(1)}, bf16[2,48,1536]{2,1,0:T(8,128)(2,1)S(1)}, u32[]{:S(2)}, u32[]{:S(2)}) collective-permute-start(bf16[2,48,1536]{2,1,0:T(8,128)(2,1)S(1)} %constant_dynamic-slice_fusion.1), channel_id=1, source_target_pairs={{0,16},{1,17},{2,18},{3,19},{4,20},{5,21},{6,22},{7,23},{8,24},{9,... | collective-permute-start | bytes 884744 | tf_op jit(solution)/shard_map/ppermute | solution.py:744
  178.9 31.3 %collective-permute-start.28 = (bf16[4,48,1920]{2,1,0:T(8,128)(2,1)}, bf16[4,48,1920]{2,1,0:T(8,128)(2,1)S(1)}, u32[]{:S(2)}, u32[]{:S(2)}) collective-permute-start(bf16[4,48,1920]{2,1,0:T(8,128)(2,1)} %pad_maximum_fusion.2), channel_id=1, source_target_pairs={{0,4},{1,5},{2,6},{3,7},{4,0},{5,1},{6,2},{7,3},{8,12},{9,13},{10,... | collective-permute-start | bytes 2211848 | tf_op jit(solution)/shard_map/ppermute | solution.py:744
  180.5 29.7 %collective-permute-start.29 = (bf16[4,48,1920]{2,1,0:T(8,128)(2,1)S(1)}, bf16[4,48,1920]{2,1,0:T(8,128)(2,1)S(1)}, u32[]{:S(2)}, u32[]{:S(2)}) collective-permute-start(bf16[4,48,1920]{2,1,0:T(8,128)(2,1)S(1)} %pad_maximum_fusion.3), channel_id=1, source_target_pairs={{0,1},{1,0},{2,3},{3,2},{4,5},{5,4},{6,7},{7,6},{8,9},{9,8},{10,11... | collective-permute-start | bytes 2211848 | tf_op jit(solution)/shard_map/ppermute | solution.py:744
  180.8 32.8 %collective-permute-start.30 = (bf16[4,48,1920]{2,1,0:T(8,128)(2,1)S(1)}, bf16[4,48,1920]{2,1,0:T(8,128)(2,1)S(1)}, u32[]{:S(2)}, u32[]{:S(2)}) collective-permute-start(bf16[4,48,1920]{2,1,0:T(8,128)(2,1)S(1)} %pad_maximum_fusion.4), channel_id=1, source_target_pairs={{0,5},{1,4},{2,7},{3,6},{4,1},{5,0},{6,3},{7,2},{8,13},{9,12},{10,... | collective-permute-start | bytes 2211848 | tf_op jit(solution)/shard_map/ppermute | solution.py:744
  195.9 14.3 %collective-permute-start.27 = (bf16[1,48,1536]{2,1,0:T(8,128)(2,1)S(1)}, bf16[1,48,1536]{2,1,0:T(8,128)(2,1)S(1)}, u32[]{:S(2)}, u32[]{:S(2)}) collective-permute-start(bf16[1,48,1536]{2,1,0:T(8,128)(2,1)S(1)} %constant_dynamic-slice_fusion), channel_id=1, source_target_pairs={{0,8},{1,9},{2,10},{3,11},{4,12},{5,13},{6,14},{7,15},{8,0},{9,1},... | collective-permute-start | bytes 442376 | tf_op jit(solution)/shard_map/ppermute | solution.py:744
  214.5 4.2 %collective-permute-start.31 = (bf16[4,2,48,2560]{3,2,1,0:T(8,128)(2,1)}, bf16[4,2,48,2560]{3,2,1,0:T(8,128)(2,1)S(1)}, u32[]{:S(2)}, u32[]{:S(2)}) collective-permute-start(bf16[4,2,48,2560]{3,2,1,0:T(8,128)(2,1)} %get-tuple-element.216), channel_id=1, source_target_pairs={{0,2},{1,3},{2,0},{3,1},{4,6},{5,7},{6,4},{7,5},{8,10},{9,11},{10,... | collective-permute-start | bytes 5898248 | tf_op jit(solution)/shard_map/ppermute | solution.py:744
  219.4 10.6 %collective-permute-start.35 = (bf16[48,1920]{1,0:T(8,128)(2,1)S(1)}, bf16[48,1920]{1,0:T(8,128)(2,1)S(1)}, u32[]{:S(2)}, u32[]{:S(2)}) collective-permute-start(bf16[48,1920]{1,0:T(8,128)(2,1)S(1)} %get-tuple-element.228), channel_id=1, source_target_pairs={{0,8},{1,9},{2,10},{3,11},{4,12},{5,13},{6,14},{7,15},{8,0},{9,1},... | collective-permute-start | bytes 552968 | tf_op jit(solution)/shard_map/ppermute | solution.py:744
  220.8 16.3 %collective-permute-start.36 = (bf16[48,1920]{1,0:T(8,128)(2,1)S(1)}, bf16[48,1920]{1,0:T(8,128)(2,1)S(1)}, u32[]{:S(2)}, u32[]{:S(2)}) collective-permute-start(bf16[48,1920]{1,0:T(8,128)(2,1)S(1)} %get-tuple-element.229), channel_id=1, source_target_pairs={{0,16},{1,17},{2,18},{3,19},{4,20},{5,21},{6,22},{7,23},{8,24},{9,... | collective-permute-start | bytes 552968 | tf_op jit(solution)/shard_map/ppermute | solution.py:744
  222.1 15.0 %collective-permute-start.37 = (bf16[48,1920]{1,0:T(8,128)(2,1)S(1)}, bf16[48,1920]{1,0:T(8,128)(2,1)S(1)}, u32[]{:S(2)}, u32[]{:S(2)}) collective-permute-start(bf16[48,1920]{1,0:T(8,128)(2,1)S(1)} %get-tuple-element.230), channel_id=1, source_target_pairs={{0,24},{1,25},{2,26},{3,27},{4,28},{5,29},{6,30},{7,31},{8,16},{9,... | collective-permute-start | bytes 552968 | tf_op jit(solution)/shard_map/ppermute | solution.py:744
  223.9 14.2 %collective-permute-start.32 = (bf16[4,48,1280]{2,1,0:T(8,128)(2,1)S(1)}, bf16[4,48,1280]{2,1,0:T(8,128)(2,1)S(1)}, u32[]{:S(2)}, u32[]{:S(2)}) collective-permute-start(bf16[4,48,1280]{2,1,0:T(8,128)(2,1)S(1)} %get-tuple-element.222), channel_id=1, source_target_pairs={{0,4},{1,5},{2,6},{3,7},{4,0},{5,1},{6,2},{7,3},{8,12},{9,13},{10,... | collective-permute-start | bytes 1474568 | tf_op jit(solution)/shard_map/ppermute | solution.py:744
  225.6 23.0 %collective-permute-start.33 = (bf16[4,48,1280]{2,1,0:T(8,128)(2,1)S(1)}, bf16[4,48,1280]{2,1,0:T(8,128)(2,1)S(1)}, u32[]{:S(2)}, u32[]{:S(2)}) collective-permute-start(bf16[4,48,1280]{2,1,0:T(8,128)(2,1)S(1)} %get-tuple-element.223), channel_id=1, source_target_pairs={{0,1},{1,0},{2,3},{3,2},{4,5},{5,4},{6,7},{7,6},{8,9},{9,8},{10,11... | collective-permute-start | bytes 1474568 | tf_op jit(solution)/shard_map/ppermute | solution.py:744
  230.0 18.6 %collective-permute-start.34 = (bf16[4,48,1280]{2,1,0:T(8,128)(2,1)S(1)}, bf16[4,48,1280]{2,1,0:T(8,128)(2,1)S(1)}, u32[]{:S(2)}, u32[]{:S(2)}) collective-permute-start(bf16[4,48,1280]{2,1,0:T(8,128)(2,1)S(1)} %get-tuple-element.224), channel_id=1, source_target_pairs={{0,5},{1,4},{2,7},{3,6},{4,1},{5,0},{6,3},{7,2},{8,13},{9,12},{10,... | collective-permute-start | bytes 1474568 | tf_op jit(solution)/shard_map/ppermute | solution.py:744
  248.9 18.7 %collective-permute-start.39 = (bf16[328,768]{1,0:T(8,128)(2,1)S(1)}, bf16[328,768]{1,0:T(8,128)(2,1)S(1)}, u32[]{:S(2)}, u32[]{:S(2)}) collective-permute-start(bf16[328,768]{1,0:T(8,128)(2,1)S(1)} %slice.174), channel_id=1, source_target_pairs={{0,1},{1,0},{2,3},{3,2},{4,5},{5,4},{6,7},{7,6},{8,9},{9,8},{10,11... | collective-permute-start | bytes 1511432 | tf_op jit(solution)/shard_map/ppermute | solution.py:744
  249.5 6.1 %collective-permute-start.40 = (bf16[48,1280]{1,0:T(8,128)(2,1)S(1)}, bf16[48,1280]{1,0:T(8,128)(2,1)S(1)}, u32[]{:S(2)}, u32[]{:S(2)}) collective-permute-start(bf16[48,1280]{1,0:T(8,128)(2,1)S(1)} %get-tuple-element.238), channel_id=1, source_target_pairs={{0,8},{1,9},{2,10},{3,11},{4,12},{5,13},{6,14},{7,15},{8,0},{9,1},... | collective-permute-start | bytes 368648 | tf_op jit(solution)/shard_map/ppermute | solution.py:744
  250.0 10.7 %collective-permute-start.41 = (bf16[48,1280]{1,0:T(8,128)(2,1)S(1)}, bf16[48,1280]{1,0:T(8,128)(2,1)S(1)}, u32[]{:S(2)}, u32[]{:S(2)}) collective-permute-start(bf16[48,1280]{1,0:T(8,128)(2,1)S(1)} %get-tuple-element.239), channel_id=1, source_target_pairs={{0,16},{1,17},{2,18},{3,19},{4,20},{5,21},{6,22},{7,23},{8,24},{9,... | collective-permute-start | bytes 368648 | tf_op jit(solution)/shard_map/ppermute | solution.py:744
  252.5 8.3 %collective-permute-start.42 = (bf16[48,1280]{1,0:T(8,128)(2,1)S(1)}, bf16[48,1280]{1,0:T(8,128)(2,1)S(1)}, u32[]{:S(2)}, u32[]{:S(2)}) collective-permute-start(bf16[48,1280]{1,0:T(8,128)(2,1)S(1)} %get-tuple-element.240), channel_id=1, source_target_pairs={{0,24},{1,25},{2,26},{3,27},{4,28},{5,29},{6,30},{7,31},{8,16},{9,... | collective-permute-start | bytes 368648 | tf_op jit(solution)/shard_map/ppermute | solution.py:744
  253.9 13.7 %collective-permute-start.38 = (bf16[48,3456]{1,0:T(8,128)(2,1)S(1)}, bf16[48,3456]{1,0:T(8,128)(2,1)S(1)}, u32[]{:S(2)}, u32[]{:S(2)}) collective-permute-start(bf16[48,3456]{1,0:T(8,128)(2,1)S(1)} %pad_maximum_fusion.7), channel_id=1, source_target_pairs={{0,1},{1,0},{2,3},{3,2},{4,5},{5,4},{6,7},{7,6},{8,9},{9,8},{10,11... | collective-permute-start | bytes 995336 | tf_op jit(solution)/shard_map/ppermute | solution.py:744
  267.7 5.7 %collective-permute-start.43 = (bf16[48,1280]{1,0:T(8,128)(2,1)S(1)}, bf16[48,1280]{1,0:T(8,128)(2,1)S(1)}, u32[]{:S(2)}, u32[]{:S(2)}) collective-permute-start(bf16[48,1280]{1,0:T(8,128)(2,1)S(1)} %add_convert_fusion.11), channel_id=1, source_target_pairs={{0,1},{1,0},{2,3},{3,2},{4,5},{5,4},{6,7},{7,6},{8,9},{9,8},{10,11... | collective-permute-start | bytes 368648 | tf_op jit(solution)/shard_map/ppermute | solution.py:744
  (33 other events, 211.0 us)
Sparse Core Ops, SparseCore 0:
  10.9 89.7 all-gather.1

commit v4 on v3

--- a/solution.py
+++ b/solution.py
@@ -336,19 +336,19 @@
 
 
 def attention_forward_kernel(
-    scale, size, inputs_ref, gain_ref, shift_ref, q_weight_ref, k_weight_ref, v_weight_ref, q_bias_ref, v_bias_ref,
-    mask_ref, out_ref, log_ref, query_ref, key_ref, value_ref, normed_ref,
+    scale, size, inputs_ref, small_ref, q_weight_ref, k_weight_ref, v_weight_ref, bias_ref, out_weight_ref, mask_ref,
+    out_ref, log_ref, query_ref, key_ref, value_ref, middle_ref, second_ref, normed_ref, merged_ref,
 ):
     @pl.when(pl.program_id(0) == 0)
     def _():
         unit, _ = norm_parts(inputs_ref[...].astype(F32))
-        normed_ref[...] = (unit * gain_ref[...] + shift_ref[...]).astype(LOW)
+        normed_ref[...] = (unit * small_ref[0:1] + small_ref[1:2]).astype(LOW)
 
     weight = jnp.concatenate([q_weight_ref[...], k_weight_ref[...], v_weight_ref[...]], axis=1)
     projected = dot_nn(normed_ref[...], weight)
-    query_ref[...] = (projected[:, : 2 * size] + q_bias_ref[...]).astype(LOW)
+    query_ref[...] = (projected[:, : 2 * size] + bias_ref[2:3]).astype(LOW)
     key_ref[...] = projected[:, 2 * size : 4 * size].astype(LOW)
-    value_ref[...] = (projected[:, 4 * size :] + v_bias_ref[...]).astype(LOW)
+    value_ref[...] = (projected[:, 4 * size :] + bias_ref[3:4]).astype(LOW)
     real = mask_ref[...] > 0.5
     query = query_ref[...] * jnp.asarray(scale, LOW)
     key = jnp.where(real, key_ref[...], key_ref[0:1, :])
@@ -366,43 +366,56 @@
         totals = mixed[other : other + size, :]
         pieces.append(mixed[own : own + size, :] / totals)
         log_ref[0, head : head + 1, :] = highest + jnp.log(totals[0:1, :])
-    out_ref[...] = jnp.concatenate(pieces, axis=0).T.astype(LOW)
-
-
-def attention_forward(inputs, gain, shift, first, query_bias, value_bias, mask_column):
+    out = jnp.concatenate(pieces, axis=0).T.astype(LOW)
+    out_ref[...] = out
+    for pair in range(HEADS // 2):
+
+        @pl.when(pl.program_id(0) == pair)
+        def _():
+            merged_ref[:, 2 * size * pair : 2 * size * (pair + 1)] = out
+
+    @pl.when(pl.program_id(0) == HEADS // 2 - 1)
+    def _():
+        middle = inputs_ref[...].astype(F32) + dot_nn(merged_ref[...], out_weight_ref[...]) + small_ref[4:5]
+        middle_ref[...] = middle
+        unit, _ = norm_parts(middle)
+        second_ref[...] = (unit * small_ref[5:6] + small_ref[6:7]).astype(LOW)
+
+
+def attention_forward(inputs, small, first, mask_column):
     rows, dim = inputs.shape
     size = dim // HEADS
     pairs = HEADS // 2
     spec = pl.BlockSpec((rows, 2 * size), lambda p: (0, p))
-    bias = pl.BlockSpec((1, 2 * size), lambda p: (0, p))
-    row = pl.BlockSpec((1, dim), lambda p: (0, 0))
+    whole = pl.BlockSpec((rows, dim), lambda p: (0, 0))
     return pl.pallas_call(
         functools.partial(attention_forward_kernel, size ** (-0.5), size),
         grid=(pairs,),
         in_specs=[
-            pl.BlockSpec((rows, dim), lambda p: (0, 0)),
-            row,
-            row,
+            whole,
+            pl.BlockSpec(small.shape, lambda p: (0, 0)),
             pl.BlockSpec((dim, 2 * size), lambda p: (0, p)),
             pl.BlockSpec((dim, 2 * size), lambda p: (0, pairs + p)),
             pl.BlockSpec((dim, 2 * size), lambda p: (0, 2 * pairs + p)),
-            bias,
-            bias,
+            pl.BlockSpec((small.shape[0], 2 * size), lambda p: (0, p)),
+            pl.BlockSpec((dim, dim), lambda p: (0, 3)),
             pl.BlockSpec((rows, 1), lambda p: (0, 0)),
         ],
-        out_specs=[spec, pl.BlockSpec((1, 2, rows), lambda p: (p, 0, 0)), spec, spec, spec],
+        out_specs=[spec, pl.BlockSpec((1, 2, rows), lambda p: (p, 0, 0)), spec, spec, spec, whole, whole],
         out_shape=[
             jax.ShapeDtypeStruct((rows, dim), LOW),
             jax.ShapeDtypeStruct((pairs, 2, rows), F32),
             jax.ShapeDtypeStruct((rows, dim), LOW),
             jax.ShapeDtypeStruct((rows, dim), LOW),
             jax.ShapeDtypeStruct((rows, dim), LOW),
-        ],
-        scratch_shapes=[pltpu.VMEM((rows, dim), LOW)],
+            jax.ShapeDtypeStruct((rows, dim), F32),
+            jax.ShapeDtypeStruct((rows, dim), LOW),
+        ],
+        scratch_shapes=[pltpu.VMEM((rows, dim), LOW), pltpu.VMEM((rows, dim), LOW)],
         compiler_params=pltpu.CompilerParams(vmem_limit_bytes=VMEM),
-        cost_estimate=cost(16),
+        cost_estimate=cost(18),
         name="attention_forward",
-    )(inputs, gain, shift, first, first, first, query_bias, value_bias, mask_column)
+    )(inputs, small, first, first, first, small, first, mask_column)
 
 
 def attention_backward_kernel(
@@ -473,7 +486,7 @@
 
 
 def mlp_first_kernel(
-    shape, second_ref, dz_ref, up_ref, up_bias_ref, down_ref, middle_ref, down_bias_ref,
+    shape, second_ref, dz_ref, up_ref, up_bias_ref, down_ref, middle_ref, small_ref,
     out_ref, kept_ref, sent_ref, pre_grad_ref, up_bias_grad_ref, down_grad_ref,
 ):
     step = pl.program_id(0)
@@ -510,14 +523,14 @@
 
     @pl.when(step == 0)
     def _():
-        out_ref[...] = middle_ref[...] + down_bias_ref[...] + out_part
+        out_ref[...] = middle_ref[...] + small_ref[7:8] + out_part
 
     @pl.when(step > 0)
     def _():
         out_ref[...] += out_part
 
 
-def mlp_first(second, dz, up_down, up_bias, middle, down_bias, owners):
+def mlp_first(second, dz, up_down, up_bias, middle, small, owners):
     rows, dim = second.shape
     width = up_bias.shape[1]
     shard = dim // owners
@@ -534,7 +547,7 @@
             pl.BlockSpec((1, dim), lambda j: (0, j)),
             pl.BlockSpec((some, shard, width), lambda j: (j, 0, 1)),
             whole,
-            pl.BlockSpec((1, dim), lambda j: (0, 0)),
+            pl.BlockSpec(small.shape, lambda j: (0, 0)),
         ],
         out_specs=[
             whole,
@@ -554,7 +567,7 @@
         compiler_params=pltpu.CompilerParams(vmem_limit_bytes=VMEM),
         cost_estimate=cost(19),
         name="mlp_first",
-    )(second, dz, up_down, up_bias, up_down.reshape(owners, shard, 2 * width), middle, down_bias)
+    )(second, dz, up_down, up_bias, up_down.reshape(owners, shard, 2 * width), middle, small)
 
 
 def mlp_second_kernel(second_ref, pre_grad_ref, up_ref, second_grad_ref, kept_ref, sent_ref, up_grad_ref):
@@ -618,13 +631,13 @@
 
 
 def middle_kernel(
-    middle_ref, grad_ref, dz_ref, gain_ref, out_full_ref, merged_ref,
+    middle_ref, grad_ref, dz_ref, rows_ref, out_full_ref, merged_ref,
     middle_grad_ref, merged_grad_ref, kept_ref, sent_ref, small_ref, out_grad_ref,
 ):
     unit, inverse = norm_parts(middle_ref[...])
     grad = grad_ref[...]
     upstream = dz_ref[...].astype(F32)
-    middle_grad = upstream + norm_back(unit, inverse, gain_ref[...], grad)
+    middle_grad = upstream + norm_back(unit, inverse, rows_ref[5:6], grad)
     middle_grad_ref[...] = middle_grad
     low = middle_grad.astype(LOW)
     merged_grad_ref[...] = dot_nt(low, out_full_ref[...]).astype(LOW)
@@ -636,7 +649,7 @@
     small_ref[3:4] = column_sums(upstream)
 
 
-def middle_backward(middle, second_grad, dz, gain, first, merged, owners):
+def middle_backward(middle, second_grad, dz, small, first, merged, owners):
     rows, dim = middle.shape
     split = (4, 2, dim // owners, dim)
     whole = pl.BlockSpec((rows, dim), lambda j: (0, 0))
@@ -647,7 +660,7 @@
             whole,
             whole,
             whole,
-            pl.BlockSpec((1, dim), lambda j: (0, 0)),
+            pl.BlockSpec(small.shape, lambda j: (0, 0)),
             pl.BlockSpec((dim, dim), lambda j: (0, 3)),
             whole,
         ],
@@ -669,16 +682,16 @@
         compiler_params=pltpu.CompilerParams(vmem_limit_bytes=VMEM),
         cost_estimate=cost(1),
         name="middle_backward",
-    )(middle, second_grad, dz, gain, first, merged)
+    )(middle, second_grad, dz, small, first, merged)
 
 
 def last_kernel(
-    inputs_ref, gain_ref, shift_ref, q_low, k_low, v_low, q_high, k_high, v_high, qkv_full_ref,
+    inputs_ref, rows_ref, q_low, k_low, v_low, q_high, k_high, v_high, qkv_full_ref,
     middle_grad_ref, small_ref, up_bias_ref, input_grad_ref, kept_ref, sent_ref, total_ref,
 ):
     unit, inverse = norm_parts(inputs_ref[...].astype(F32))
-    gain = gain_ref[...]
-    normed = (unit * gain + shift_ref[...]).astype(LOW)
+    gain = rows_ref[0:1]
+    normed = (unit * gain + rows_ref[1:2]).astype(LOW)
     grads = [ref[...] for ref in (q_low, q_high, k_low, k_high, v_low, v_high)]
     qkv_grad = jnp.concatenate(grads, axis=1)
     dim = unit.shape[1]
@@ -695,7 +708,7 @@
     split_cores(total_ref, kept_ref, sent_ref, 0, slice(None))
 
 
-def last_backward(inputs, gain, shift, grads_low, grads_high, first, middle_grad, small, up_bias, owners):
+def last_backward(inputs, small_rows, grads_low, grads_high, first, middle_grad, small, up_bias, owners):
     rows, dim = inputs.shape
     columns = 3 * dim + SMALL_PAD
 
@@ -706,7 +719,7 @@
     return pl.pallas_call(
         last_kernel,
         grid=(1,),
-        in_specs=[whole(rows, dim), whole(1, dim), whole(1, dim)]
+        in_specs=[whole(rows, dim), whole(*small_rows.shape)]
         + [whole(*g.shape) for g in (*grads_low, *grads_high)]
         + [whole(dim, 3 * dim), whole(rows, dim), whole(*small.shape), whole(*up_bias.shape)],
         out_specs=[whole(rows, dim), whole(*split.shape), whole(*split.shape)],
@@ -715,7 +728,7 @@
         compiler_params=pltpu.CompilerParams(vmem_limit_bytes=VMEM),
         cost_estimate=cost(1),
         name="last_backward",
-    )(inputs, gain, shift, *grads_low, *grads_high, first, middle_grad, small, up_bias)
+    )(inputs, small_rows, *grads_low, *grads_high, first, middle_grad, small, up_bias)
 
 
 def own_and_away(blocks):
@@ -857,24 +870,14 @@
     own_in, away_in = own_and_away(masked)
     first, away_in = tie(first, away_in)
     down_in = jnp.concatenate([own_in, swap(away_in, y=1)], axis=0)
-    out_full = first[:, 3 * dim : 4 * dim]
-    gain_one, shift_one, query_bias, value_bias, out_bias, gain_two, shift_two, down_bias = [
-        small[i : i + 1] for i in range(8)
-    ]
     up_bias = small[8:count].reshape(pieces, owners, shard).swapaxes(0, 1).reshape(1, width)
 
     both = jnp.stack([own, away])
     inputs_low = both[:, :shard_rows].reshape(2 * shard_rows, dim)
-    inputs = inputs_low.astype(F32)
     mask_column = both[:, shard_rows, :shard_rows].astype(F32).reshape(2 * shard_rows, 1)
-    merged, logs, *qkv = attention_forward(
-        inputs_low, gain_one, shift_one, first, query_bias, value_bias, mask_column
-    )
-    middle = inputs + dot_nn(merged, out_full) + out_bias
-    unit_two, _ = norm_parts(middle)
-    second = (unit_two * gain_two + shift_two).astype(LOW)
+    merged, logs, *qkv, middle, second = attention_forward(inputs_low, small, first, mask_column)
     output, down_kept, down_sent, pre_grad, grad_up_bias = mlp_first(
-        second, down_in, up_down, up_bias, middle, down_bias, owners
+        second, down_in, up_down, up_bias, middle, small, owners
     )
     output_own, output_away = output[:shard_rows], output[shard_rows:].astype(LOW)
     pre_grad, output_away, down_sent = tie(pre_grad, output_away, down_sent)
@@ -885,7 +888,7 @@
     second_grad, up_sent, *down_pieces = tie(second_grad, up_sent, *down_pieces)
     down_pieces, up_sent = plane_swaps(down_pieces), swap(up_sent, core=1)
     middle_grad, merged_grad, out_kept, out_sent, small_grads = middle_backward(
-        middle, second_grad, down_in, gain_two, first, merged, owners
+        middle, second_grad, down_in, small, first, merged, owners
     )
     middle_grad, merged_grad, out_kept, out_sent, small_grads, up_sent = tie(
         middle_grad, merged_grad, out_kept, out_sent, small_grads, up_sent
@@ -912,7 +915,7 @@
     grad_up_bias, down_away = tie(grad_up_bias, half_line(down_two, 1 - z % 2))
     down_away = swap(down_away, z=1)
     input_grad, last_kept, last_sent = last_backward(
-        inputs_low, gain_one, shift_one, grads_low, grads_high, first, middle_grad, small_grads, grad_up_bias, owners
+        inputs_low, small, grads_low, grads_high, first, middle_grad, small_grads, grad_up_bias, owners
     )
     tied = tie(input_grad, last_kept, last_sent, down_away, *up_pieces)
     input_grad, last_kept, last_sent, down_away = tied[:4]

time: 287 us -> 281 us (0.979)
  local copies, waits for them, and re-layouts: 16.8 us -> 13.1 us
  other arithmetic: 19.7 us -> 16.6 us
  Pallas kernels: 105 us -> 108 us
    pallas_call x1, Pallas kernels: 18.1 us -> 21 us  [attention_forward(): pl.pallas_call(functools.partial(attention_forward_kernel, size ** (-0.5)...]
  transfers between devices with their start and end apart: 45 -> 45, of which waited for: 13 -> 14; matrix products, arithmetic and copies ran while one was open for 8% -> 6% of each run, Pallas kernels for 30% -> 31%
where the time goes in v4:
time: 281 us; the launch traced here: 277 us
  Pallas kernels  108 us (38%)
  waiting for transfers between devices  82 us (29%)
  starting transfers between devices  41.9 us (15%)
  other arithmetic  16.6 us (6%)
  between operations  15.4 us (5%)
  local copies, waits for them, and re-layouts  13.1 us (5%)
    ppermute x44, waiting for transfers between devices, swap(): lax.ppermute(block, ('img', 'seq'), [(i, i ^ bits) for i in range(32)])  82 us
    ppermute x44, starting transfers between devices, swap(): lax.ppermute(block, ('img', 'seq'), [(i, i ^ bits) for i in range(32)])  41.8 us
    pallas_call x2, Pallas kernels, attention_backward(): pl.pallas_call(functools.partial(attention_backward_kernel, size ** (-0.5...  26.5 us
    pallas_call x1, Pallas kernels, attention_forward(): pl.pallas_call(functools.partial(attention_forward_kernel, size ** (-0.5)...  21 us
    pallas_call x1, Pallas kernels, mlp_first(): pl.pallas_call(functools.partial(mlp_first_kernel, (some, pieces, dim)),...  20.9 us
    pallas_call x1, Pallas kernels, mlp_second(): pl.pallas_call(mlp_second_kernel, grid=(width // dim,), in_specs=[whole,...  13.5 us
    pallas_call x1, Pallas kernels, last_backward(): pl.pallas_call(last_kernel, grid=(1,), in_specs=[whole(rows, dim), whole(...  12.7 us
    pallas_call x1, Pallas kernels, middle_backward(): pl.pallas_call(middle_kernel, grid=(1,), in_specs=[whole, whole, whole, p...  8.29 us
  transfers between devices with their start and end apart: 45, of which 14 were waited for; matrix products, arithmetic and copies ran while one was open for 6% of the time, Pallas kernels for 31%

profile of v4, /device:TPU:0, one launch (start us, length us, event | category | flops | bytes accessed | tf_op | source)
XLA Modules:
  0.0 277.2 jit_solution(10238901243370240324)
XLA Ops:
  7.2 1.2 copy.47
  8.6 1.9 pad_maximum_fusion.5
  10.7 3.1 %collective-permute-start.3 = (bf16[344,768]{1,0:T(8,128)(2,1)S(1)}, bf16[344,768]{1,0:T(8,128)(2,1)S(1)}, u32[]{:S(2)}, u32[]{:S(2)}) collective-permute-start(bf16[344,768]{1,0:T(8,128)(2,1)S(1)} %get-tuple-element.271), channel_id=1, source_target_pairs={{0,1},{1,0},{2,3},{3,2},{4,5},{5,4},{6,7},{7,6},{8,9},{9,8},{10,11... | collective-permute-start | bytes 1585160 | tf_op jit(solution)/shard_map/ppermute | solution.py:757
  14.2 3.7 %collective-permute-start.2 = (bf16[1,48,1664]{2,1,0:T(8,128)(2,1)S(1)}, bf16[1,48,1664]{2,1,0:T(8,128)(2,1)S(1)}, u32[]{:S(2)}, u32[]{:S(2)}) collective-permute-start(bf16[1,48,1664]{2,1,0:T(8,128)(2,1)S(1)} %fusion.9.refs_0_), channel_id=1, source_target_pairs={{0,24},{1,25},{2,26},{3,27},{4,28},{5,29},{6,30},{7,31},{8,16},{9,... | collective-permute-start | bytes 479240 | tf_op jit(solution)/shard_map/ppermute | solution.py:757
  19.0 4.2 %collective-permute-done.2 = bf16[1,48,1664]{2,1,0:T(8,128)(2,1)S(1)} collective-permute-done((bf16[1,48,1664]{2,1,0:T(8,128)(2,1)S(1)}, bf16[1,48,1664]{2,1,0:T(8,128)(2,1)S(1)}, u32[]{:S(2)}, u32[]{:S(2)}) %collective-permute-start.2) | collective-permute-done | bytes 159776 | tf_op jit(solution)/shard_map/ppermute | solution.py:757
  23.2 1.5 collective-permute-start.4
  24.7 20.3 %collective-permute-done.1 = bf16[1,48,1664]{2,1,0:T(8,128)(2,1)S(1)} collective-permute-done((bf16[1,48,1664]{2,1,0:T(8,128)(2,1)S(1)}, bf16[1,48,1664]{2,1,0:T(8,128)(2,1)S(1)}, u32[]{:S(2)}, u32[]{:S(2)}) %collective-permute-start.1) | collective-permute-done | bytes 159776 | tf_op jit(solution)/shard_map/ppermute | solution.py:757
  45.1 1.6 collective-permute-start.14
  46.7 7.2 %collective-permute-done.14.refs_12_ = bf16[3,48,1664]{2,1,0:T(8,128)(2,1)S(1)} collective-permute-done((bf16[3,48,1664]{2,1,0:T(8,128)(2,1)S(1)}, bf16[3,48,1664]{2,1,0:T(8,128)(2,1)S(1)}, u32[]{:S(2)}, u32[]{:S(2)}) %collective-permute-start.14) | collective-permute-done | bytes 479264 | tf_op jit(solution)/shard_map/ppermute | solution.py:757
  54.4 2.0 collective-permute-start.9
  57.0 12.2 %collective-permute-done.9.refs_6_ = bf16[1,48,1664]{2,1,0:T(8,128)(2,1)} collective-permute-done((bf16[1,48,1664]{2,1,0:T(8,128)(2,1)S(1)}, bf16[1,48,1664]{2,1,0:T(8,128)(2,1)}, u32[]{:S(2)}, u32[]{:S(2)}) %collective-permute-start.9) | collective-permute-done | bytes 159776 | tf_op jit(solution)/shard_map/ppermute | solution.py:757
  71.6 1.0 fusion
  73.2 5.3 %assemble.1 = (bf16[16,48,3328]{2,1,0:T(8,128)(2,1)}, f32[16,768]{1,0:T(8,128)}) custom-call(bf16[1,48,1664]{2,1,0:T(8,128)(2,1)} %copy-done.13, bf16[1,48,1664]{2,1,0:T(8,128)(2,1)} %copy-done.20, bf16[1,48,1664]{2,1,0:T(8,128)(2,1)} %copy-done.18, bf16[1,48,1664]{2,1,0:T(8,128)(2,1)} %copy-done.21, bf16[1,48,1664]{2,1,0:T(8,128)(2,1)} %copy-done.19, ...), custom_call_target="tpu_custom_call" | custom-call | tf_op jit(solution)/shard_map/assemble/pallas_call | solution.py:787
  78.5 21.0 %attention_forward.1 = (bf16[656,768]{1,0:T(8,128)(2,1)}, f32[6,2,656]{2,1,0:T(2,128)}, bf16[656,768]{1,0:T(8,128)(2,1)}, bf16[656,768]{1,0:T(8,128)(2,1)}, bf16...) custom-call(bf16[656,768]{1,0:T(8,128)(2,1)} %bitcast.108, ...), custom_call_target="tpu_custom_call" | custom-call | flops 20700000256 | bytes 1 | tf_op jit(solution)/shard_map/attention_forward/pallas_call | solution.py:391
  101.0 1.0 pad_maximum_fusion.dz_ref
  102.0 20.9 %mlp_first.1 = (f32[656,768]{1,0:T(8,128)}, bf16[4,2,48,3072]{3,2,1,0:T(8,128)(2,1)}, bf16[4,2,48,3072]{3,2,1,0:T(8,128)(2,1)}, bf16[656,3072]{1,0:T(8,128)(2,1)}, bf16[768,128]{1,0:T(8,128)(2,1)}) custom-call(bf16[656,768]{1,0:T(8,128)(2,1)} %get-tuple-element.140.second_ref, bf16[656,768]{1,0:T(8,128)(2,1)} %pad_maximum_fusion.dz_ref, ...), custom_call_target="tpu_custom_call" | custom-call | flops 21849999360 | bytes 1 | tf_op jit(solution)/shard_map/mlp_first/pallas_call | solution.py:540
  122.9 1.3 slice.134
  124.4 1.9 collective-permute-start.19
  126.3 13.5 %mlp_second.1 = (f32[656,768]{1,0:T(8,128)}, bf16[4,2,48,3072]{3,2,1,0:T(8,128)(2,1)}, bf16[4,2,48,3072]{3,2,1,0:T(8,128)(2,1)}) custom-call(bf16[656,768]{1,0:T(8,128)(2,1)} %get-tuple-element.140.second_ref, bf16[656,3072]{1,0:T(8,128)(2,1)} %get-tuple-element.146.pre_grad_ref, bf16[768,6144]{1,0:T(8,128)(2,1)} %all-gather.2.cloned.1.call-done.up_ref), custom_call_target="tpu_custom_call" | custom-call | flops 1150000000 | bytes 1 | tf_op jit(solution)/shard_map/mlp_second/pallas_call | solution.py:595
  140.8 1.3 dynamic-slice_bitcast_fusion.4
  143.1 2.7 collective-permute-start.25
  145.8 8.3 %middle_backward.1 = (f32[656,768]{1,0:T(8,128)}, bf16[656,768]{1,0:T(8,128)(2,1)}, bf16[4,2,48,768]{3,2,1,0:T(8,128)(2,1)}, bf16[4,2,48,768]{3,2,1,0:T(8,128)(2,1)}, f32[4,768]{1,0:T(4,128)}) custom-call(f32[656,768]{1,0:T(8,128)} %get-tuple-element.142.middle_ref, f32[656,768]{1,0:T(8,128)} %get-tuple-element.157.grad_ref, ...), custom_call_target="tpu_custom_call" | custom-call | flops 1150000000 | bytes 1 | tf_op jit(solution)/shard_map/middle_backward/pallas_call | solution.py:656
  155.0 13.1 %attention_backward.2 = (bf16[656,384]{1,0:T(8,128)(2,1)}, bf16[656,384]{1,0:T(8,128)(2,1)}, bf16[656,384]{1,0:T(8,128)(2,1)}) custom-call(bf16[656,768]{1,0:T(8,128)(2,1)} %get-tuple-element.170.query_ref, bf16[656,768]{1,0:T(8,128)(2,1)} %get-tuple-element.171.key_ref, bf16[656,768]{1,0:T(8,128)(2,1)} %get-tuple-element.172.value_ref, ...), custom_call_target="tpu_custom_call" | custom-call | flops 1150000000 | bytes 1 | tf_op jit(solution)/shard_map/attention_backward/pallas_call | solution.py:460
  169.6 0.9 pad_maximum_fusion.2
  171.1 1.7 add_convert_fusion.4
  173.0 1.6 collective-permute-start.28
  174.8 1.7 collective-permute-start.30
  176.5 13.3 %attention_backward.3 = (bf16[656,384]{1,0:T(8,128)(2,1)}, bf16[656,384]{1,0:T(8,128)(2,1)}, bf16[656,384]{1,0:T(8,128)(2,1)}) custom-call(bf16[656,768]{1,0:T(8,128)(2,1)} %get-tuple-element.170.query_ref, bf16[656,768]{1,0:T(8,128)(2,1)} %get-tuple-element.171.key_ref, bf16[656,768]{1,0:T(8,128)(2,1)} %get-tuple-element.172.value_ref, ...), custom_call_target="tpu_custom_call" | custom-call | flops 1150000000 | bytes 1 | tf_op jit(solution)/shard_map/attention_backward/pallas_call | solution.py:460
  190.0 1.7 collective-permute-start.27
  191.6 12.7 %last_backward.1 = (f32[656,768]{1,0:T(8,128)}, bf16[4,2,48,2560]{3,2,1,0:T(8,128)(2,1)}, bf16[4,2,48,2560]{3,2,1,0:T(8,128)(2,1)}) custom-call(bf16[656,768]{1,0:T(8,128)(2,1)} %bitcast.109, f32[16,768]{1,0:T(8,128)} %get-tuple-element.137.small_ref.bias_ref.rows_ref, bf16[656,384]{1,0:T(8,128)(2,1)} %get-tuple-element.177.q_low, ...), custom_call_target="tpu_custom_call" | custom-call | flops 1150000000 | bytes 1 | tf_op jit(solution)/shard_map/last_backward/pallas_call | solution.py:719
  204.3 3.3 %collective-permute-done.30 = bf16[4,48,1920]{2,1,0:T(8,128)(2,1)S(1)} collective-permute-done((bf16[4,48,1920]{2,1,0:T(8,128)(2,1)S(1)}, bf16[4,48,1920]{2,1,0:T(8,128)(2,1)S(1)}, u32[]{:S(2)}, u32[]{:S(2)}) %collective-permute-start.30) | collective-permute-done | bytes 737312 | tf_op jit(solution)/shard_map/ppermute | solution.py:757
  208.6 1.4 slice_bitcast_fusion.1
  210.0 1.1 bitcast_convert_fusion.1
  211.6 1.1 collective-permute-done.31
  213.4 1.5 collective-permute-start.35
  214.9 1.2 collective-permute-start.36
  216.1 1.8 collective-permute-start.37
  218.0 1.7 collective-permute-start.32
  220.1 3.9 %collective-permute-done.35 = bf16[48,1920]{1,0:T(8,128)(2,1)S(1)} collective-permute-done((bf16[48,1920]{1,0:T(8,128)(2,1)S(1)}, bf16[48,1920]{1,0:T(8,128)(2,1)S(1)}, u32[]{:S(2)}, u32[]{:S(2)}) %collective-permute-start.35) | collective-permute-done | bytes 184352 | tf_op jit(solution)/shard_map/ppermute | solution.py:757
  224.0 1.7 collective-permute-start.34
  225.7 5.5 %collective-permute-done.36 = bf16[48,1920]{1,0:T(8,128)(2,1)S(1)} collective-permute-done((bf16[48,1920]{1,0:T(8,128)(2,1)S(1)}, bf16[48,1920]{1,0:T(8,128)(2,1)S(1)}, u32[]{:S(2)}, u32[]{:S(2)}) %collective-permute-start.36) | collective-permute-done | bytes 184352 | tf_op jit(solution)/shard_map/ppermute | solution.py:757
  232.2 10.4 %collective-permute-done.33 = bf16[4,48,1280]{2,1,0:T(8,128)(2,1)S(1)} collective-permute-done((bf16[4,48,1280]{2,1,0:T(8,128)(2,1)S(1)}, bf16[4,48,1280]{2,1,0:T(8,128)(2,1)S(1)}, u32[]{:S(2)}, u32[]{:S(2)}) %collective-permute-start.33) | collective-permute-done | bytes 491552 | tf_op jit(solution)/shard_map/ppermute | solution.py:757
  244.1 2.4 collective-permute-start.41
  246.5 1.5 collective-permute-start.42
  248.0 1.6 collective-permute-start.38
  249.6 5.2 %collective-permute-done.41 = bf16[48,1280]{1,0:T(8,128)(2,1)S(1)} collective-permute-done((bf16[48,1280]{1,0:T(8,128)(2,1)S(1)}, bf16[48,1280]{1,0:T(8,128)(2,1)S(1)}, u32[]{:S(2)}, u32[]{:S(2)}) %collective-permute-start.41) | collective-permute-done | bytes 122912 | tf_op jit(solution)/shard_map/ppermute | solution.py:757
  254.8 6.8 %collective-permute-done.38 = bf16[48,3456]{1,0:T(8,128)(2,1)S(1)} collective-permute-done((bf16[48,3456]{1,0:T(8,128)(2,1)S(1)}, bf16[48,3456]{1,0:T(8,128)(2,1)S(1)}, u32[]{:S(2)}, u32[]{:S(2)}) %collective-permute-start.38) | collective-permute-done | bytes 331808 | tf_op jit(solution)/shard_map/ppermute | solution.py:757
  264.3 2.3 maximum_select_fusion
  (188 shorter events, 23.6 us)
Async XLA Ops:
  7.2 94.8 %all-gather.2.cloned.1.call-start = ((), (), s32[]{:S(2)}) async-start(), calls=%async_computation | async-start | bytes 10027008 | tf_op jit(solution)/shard_map/all_gather | solution.py:747
  10.5 59.3 %copy-start.5 = (bf16[2,328,768]{2,1,0:T(8,128)(2,1)S(1)}, bf16[2,328,768]{2,1,0:T(8,128)(2,1)}, u32[]{:S(2)}) copy-start(bf16[2,328,768]{2,1,0:T(8,128)(2,1)} %param.31) | copy-start | bytes 3022852
  10.7 34.4 %collective-permute-start.3 = (bf16[344,768]{1,0:T(8,128)(2,1)S(1)}, bf16[344,768]{1,0:T(8,128)(2,1)S(1)}, u32[]{:S(2)}, u32[]{:S(2)}) collective-permute-start(bf16[344,768]{1,0:T(8,128)(2,1)S(1)} %get-tuple-element.271), channel_id=1, source_target_pairs={{0,1},{1,0},{2,3},{3,2},{4,5},{5,4},{6,7},{7,6},{8,9},{9,8},{10,11... | collective-permute-start | bytes 1585160 | tf_op jit(solution)/shard_map/ppermute | solution.py:757
  14.2 56.4 %copy-start.13 = (bf16[1,48,1664]{2,1,0:T(8,128)(2,1)}, bf16[1,48,1664]{2,1,0:T(8,128)(2,1)S(1)}, u32[]{:S(2)}) copy-start(bf16[1,48,1664]{2,1,0:T(8,128)(2,1)S(1)} %fusion.9.refs_0_) | copy-start | bytes 479236
  14.2 9.0 %collective-permute-start.2 = (bf16[1,48,1664]{2,1,0:T(8,128)(2,1)S(1)}, bf16[1,48,1664]{2,1,0:T(8,128)(2,1)S(1)}, u32[]{:S(2)}, u32[]{:S(2)}) collective-permute-start(bf16[1,48,1664]{2,1,0:T(8,128)(2,1)S(1)} %fusion.9.refs_0_), channel_id=1, source_target_pairs={{0,24},{1,25},{2,26},{3,27},{4,28},{5,29},{6,30},{7,31},{8,16},{9,... | collective-permute-start | bytes 479240 | tf_op jit(solution)/shard_map/ppermute | solution.py:757
  17.9 27.0 %collective-permute-start.1 = (bf16[1,48,1664]{2,1,0:T(8,128)(2,1)S(1)}, bf16[1,48,1664]{2,1,0:T(8,128)(2,1)S(1)}, u32[]{:S(2)}, u32[]{:S(2)}) collective-permute-start(bf16[1,48,1664]{2,1,0:T(8,128)(2,1)S(1)} %fusion.9.refs_0_), channel_id=1, source_target_pairs={{0,16},{1,17},{2,18},{3,19},{4,20},{5,21},{6,22},{7,23},{8,24},{9,... | collective-permute-start | bytes 479240 | tf_op jit(solution)/shard_map/ppermute | solution.py:757
  17.9 27.0 %collective-permute-start = (bf16[1,48,1664]{2,1,0:T(8,128)(2,1)S(1)}, bf16[1,48,1664]{2,1,0:T(8,128)(2,1)S(1)}, u32[]{:S(2)}, u32[]{:S(2)}) collective-permute-start(bf16[1,48,1664]{2,1,0:T(8,128)(2,1)S(1)} %fusion.9.refs_0_), channel_id=1, source_target_pairs={{0,8},{1,9},{2,10},{3,11},{4,12},{5,13},{6,14},{7,15},{8,0},{9,1},... | collective-permute-start | bytes 479240 | tf_op jit(solution)/shard_map/ppermute | solution.py:757
  18.7 26.3 %collective-permute-start.5 = (bf16[1,48,1664]{2,1,0:T(8,128)(2,1)S(1)}, bf16[1,48,1664]{2,1,0:T(8,128)(2,1)S(1)}, u32[]{:S(2)}, u32[]{:S(2)}) collective-permute-start(bf16[1,48,1664]{2,1,0:T(8,128)(2,1)S(1)} %fusion.9.refs_0_), channel_id=1, source_target_pairs={{0,1},{1,0},{2,3},{3,2},{4,5},{5,4},{6,7},{7,6},{8,9},{9,8},{10,11... | collective-permute-start | bytes 479240 | tf_op jit(solution)/shard_map/ppermute | solution.py:757
  23.2 21.9 %collective-permute-start.4 = (bf16[1,48,1664]{2,1,0:T(8,128)(2,1)S(1)}, bf16[1,48,1664]{2,1,0:T(8,128)(2,1)S(1)}, u32[]{:S(2)}, u32[]{:S(2)}) collective-permute-start(bf16[1,48,1664]{2,1,0:T(8,128)(2,1)S(1)} %fusion.9.refs_0_), channel_id=1, source_target_pairs={{0,4},{1,5},{2,6},{3,7},{4,0},{5,1},{6,2},{7,3},{8,12},{9,13},{10,... | collective-permute-start | bytes 479240 | tf_op jit(solution)/shard_map/ppermute | solution.py:757
  45.0 25.6 %copy-start.3 = (bf16[3,48,1664]{2,1,0:T(8,128)(2,1)}, bf16[3,48,1664]{2,1,0:T(8,128)(2,1)S(1)}, u32[]{:S(2)}) copy-start(bf16[3,48,1664]{2,1,0:T(8,128)(2,1)S(1)} %pad_maximum_fusion.6.refs_8_) | copy-start | bytes 1437700
  45.1 8.8 %collective-permute-start.14 = (bf16[3,48,1664]{2,1,0:T(8,128)(2,1)S(1)}, bf16[3,48,1664]{2,1,0:T(8,128)(2,1)S(1)}, u32[]{:S(2)}, u32[]{:S(2)}) collective-permute-start(bf16[3,48,1664]{2,1,0:T(8,128)(2,1)S(1)} %pad_maximum_fusion.6.refs_8_), channel_id=1, source_target_pairs={{0,4},{1,5},{2,6},{3,7},{4,0},{5,1},{6,2},{7,3},{8,12},{9,13},{10,... | collective-permute-start | bytes 1437704 | tf_op jit(solution)/shard_map/ppermute | solution.py:757
  46.7 22.5 %collective-permute-start.12 = (bf16[3,48,1664]{2,1,0:T(8,128)(2,1)S(1)}, bf16[3,48,1664]{2,1,0:T(8,128)(2,1)}, u32[]{:S(2)}, u32[]{:S(2)}) collective-permute-start(bf16[3,48,1664]{2,1,0:T(8,128)(2,1)S(1)} %pad_maximum_fusion.6.refs_8_), channel_id=1, source_target_pairs={{0,1},{1,0},{2,3},{3,2},{4,5},{5,4},{6,7},{7,6},{8,9},{9,8},{10,11... | collective-permute-start | bytes 1437704 | tf_op jit(solution)/shard_map/ppermute | solution.py:757
  53.9 15.8 %collective-permute-start.16 = (bf16[3,48,1664]{2,1,0:T(8,128)(2,1)S(1)}, bf16[3,48,1664]{2,1,0:T(8,128)(2,1)}, u32[]{:S(2)}, u32[]{:S(2)}) collective-permute-start(bf16[3,48,1664]{2,1,0:T(8,128)(2,1)S(1)} %collective-permute-done.14.refs_12_), channel_id=1, source_target_pairs={{0,1},{1,0},{2,3},{3,2},{4,5},{5,4},{6,7},{7,6},{8,9},{9,8},{10,11... | collective-permute-start | bytes 1437704 | tf_op jit(solution)/shard_map/ppermute | solution.py:757
  53.9 2.5 collective-permute-start.6
  53.9 2.6 collective-permute-start.7
  54.4 14.8 %collective-permute-start.9 = (bf16[1,48,1664]{2,1,0:T(8,128)(2,1)S(1)}, bf16[1,48,1664]{2,1,0:T(8,128)(2,1)}, u32[]{:S(2)}, u32[]{:S(2)}) collective-permute-start(bf16[1,48,1664]{2,1,0:T(8,128)(2,1)S(1)} %collective-permute-done.4.refs_4_), channel_id=1, source_target_pairs={{0,1},{1,0},{2,3},{3,2},{4,5},{5,4},{6,7},{7,6},{8,9},{9,8},{10,11... | collective-permute-start | bytes 479240 | tf_op jit(solution)/shard_map/ppermute | solution.py:757
  56.4 13.5 %collective-permute-start.8 = (bf16[1,48,1664]{2,1,0:T(8,128)(2,1)S(1)}, bf16[1,48,1664]{2,1,0:T(8,128)(2,1)S(1)}, u32[]{:S(2)}, u32[]{:S(2)}) collective-permute-start(bf16[1,48,1664]{2,1,0:T(8,128)(2,1)S(1)} %collective-permute-done.4.refs_4_), channel_id=1, source_target_pairs={{0,2},{1,3},{2,0},{3,1},{4,6},{5,7},{6,4},{7,5},{8,10},{9,11},{10,... | collective-permute-start | bytes 479240 | tf_op jit(solution)/shard_map/ppermute | solution.py:757
  56.5 16.6 %collective-permute-start.11 = (bf16[3,48,1664]{2,1,0:T(8,128)(2,1)S(1)}, bf16[3,48,1664]{2,1,0:T(8,128)(2,1)}, u32[]{:S(2)}, u32[]{:S(2)}) collective-permute-start(bf16[3,48,1664]{2,1,0:T(8,128)(2,1)S(1)} %pad_maximum_fusion.6.refs_8_), channel_id=1, source_target_pairs={{0,2},{1,3},{2,0},{3,1},{4,6},{5,7},{6,4},{7,5},{8,10},{9,11},{10,... | collective-permute-start | bytes 1437704 | tf_op jit(solution)/shard_map/ppermute | solution.py:757
  69.2 4.0 %collective-permute-start.15 = (bf16[3,48,1664]{2,1,0:T(8,128)(2,1)S(1)}, bf16[3,48,1664]{2,1,0:T(8,128)(2,1)}, u32[]{:S(2)}, u32[]{:S(2)}) collective-permute-start(bf16[3,48,1664]{2,1,0:T(8,128)(2,1)S(1)} %collective-permute-done.14.refs_12_), channel_id=1, source_target_pairs={{0,2},{1,3},{2,0},{3,1},{4,6},{5,7},{6,4},{7,5},{8,10},{9,11},{10,... | collective-permute-start | bytes 1437704 | tf_op jit(solution)/shard_map/ppermute | solution.py:757
  69.2 4.0 %collective-permute-start.13 = (bf16[3,48,1664]{2,1,0:T(8,128)(2,1)}, bf16[3,48,1664]{2,1,0:T(8,128)(2,1)}, u32[]{:S(2)}, u32[]{:S(2)}) collective-permute-start(bf16[3,48,1664]{2,1,0:T(8,128)(2,1)} %collective-permute-done.12.refs_10_), channel_id=1, source_target_pairs={{0,2},{1,3},{2,0},{3,1},{4,6},{5,7},{6,4},{7,5},{8,10},{9,11},{10,... | collective-permute-start | bytes 1437704 | tf_op jit(solution)/shard_map/ppermute | solution.py:757
  69.7 3.5 %collective-permute-start.17 = (bf16[3,48,1664]{2,1,0:T(8,128)(2,1)}, bf16[3,48,1664]{2,1,0:T(8,128)(2,1)}, u32[]{:S(2)}, u32[]{:S(2)}) collective-permute-start(bf16[3,48,1664]{2,1,0:T(8,128)(2,1)} %collective-permute-done.16.refs_14_), channel_id=1, source_target_pairs={{0,2},{1,3},{2,0},{3,1},{4,6},{5,7},{6,4},{7,5},{8,10},{9,11},{10,... | collective-permute-start | bytes 1437704 | tf_op jit(solution)/shard_map/ppermute | solution.py:757
  70.0 3.2 %collective-permute-start.10 = (bf16[1,48,1664]{2,1,0:T(8,128)(2,1)}, bf16[1,48,1664]{2,1,0:T(8,128)(2,1)}, u32[]{:S(2)}, u32[]{:S(2)}) collective-permute-start(bf16[1,48,1664]{2,1,0:T(8,128)(2,1)} %collective-permute-done.9.refs_6_), channel_id=1, source_target_pairs={{0,2},{1,3},{2,0},{3,1},{4,6},{5,7},{6,4},{7,5},{8,10},{9,11},{10,... | collective-permute-start | bytes 479240 | tf_op jit(solution)/shard_map/ppermute | solution.py:757
  78.5 22.5 %collective-permute-start.18 = (bf16[328,768]{1,0:T(8,128)(2,1)S(1)}, bf16[328,768]{1,0:T(8,128)(2,1)S(1)}, u32[]{:S(2)}, u32[]{:S(2)}) collective-permute-start(bf16[328,768]{1,0:T(8,128)(2,1)S(1)} %get-tuple-element.141), channel_id=1, source_target_pairs={{0,1},{1,0},{2,3},{3,2},{4,5},{5,4},{6,7},{7,6},{8,9},{9,8},{10,11... | collective-permute-start | bytes 1511432 | tf_op jit(solution)/shard_map/ppermute | solution.py:757
  124.2 15.7 %collective-permute-start.20 = (bf16[4,2,48,3072]{3,2,1,0:T(8,128)(2,1)}, bf16[4,2,48,3072]{3,2,1,0:T(8,128)(2,1)S(1)}, u32[]{:S(2)}, u32[]{:S(2)}) collective-permute-start(bf16[4,2,48,3072]{3,2,1,0:T(8,128)(2,1)} %get-tuple-element.151), channel_id=1, source_target_pairs={{0,2},{1,3},{2,0},{3,1},{4,6},{5,7},{6,4},{7,5},{8,10},{9,11},{10,... | collective-permute-start | bytes 7077896 | tf_op jit(solution)/shard_map/ppermute | solution.py:757
  124.4 15.5 %collective-permute-start.19 = (bf16[328,768]{1,0:T(8,128)(2,1)S(1)}, bf16[328,768]{1,0:T(8,128)(2,1)S(1)}, u32[]{:S(2)}, u32[]{:S(2)}) collective-permute-start(bf16[328,768]{1,0:T(8,128)(2,1)S(1)} %slice.134), channel_id=1, source_target_pairs={{0,1},{1,0},{2,3},{3,2},{4,5},{5,4},{6,7},{7,6},{8,9},{9,8},{10,11... | collective-permute-start | bytes 1511432 | tf_op jit(solution)/shard_map/ppermute | solution.py:757
  142.2 12.0 %collective-permute-start.21 = (bf16[4,2,48,3072]{3,2,1,0:T(8,128)(2,1)}, bf16[4,2,48,3072]{3,2,1,0:T(8,128)(2,1)S(1)}, u32[]{:S(2)}, u32[]{:S(2)}) collective-permute-start(bf16[4,2,48,3072]{3,2,1,0:T(8,128)(2,1)} %get-tuple-element.164), channel_id=1, source_target_pairs={{0,2},{1,3},{2,0},{3,1},{4,6},{5,7},{6,4},{7,5},{8,10},{9,11},{10,... | collective-permute-start | bytes 7077896 | tf_op jit(solution)/shard_map/ppermute | solution.py:757
  142.3 28.3 %collective-permute-start.23 = (bf16[4,48,1536]{2,1,0:T(8,128)(2,1)}, bf16[4,48,1536]{2,1,0:T(8,128)(2,1)}, u32[]{:S(2)}, u32[]{:S(2)}) collective-permute-start(bf16[4,48,1536]{2,1,0:T(8,128)(2,1)} %get-tuple-element.182), channel_id=1, source_target_pairs={{0,4},{1,5},{2,6},{3,7},{4,0},{5,1},{6,2},{7,3},{8,12},{9,13},{10,... | collective-permute-start | bytes 1769480 | tf_op jit(solution)/shard_map/ppermute | solution.py:757
  142.8 28.2 %collective-permute-start.24 = (bf16[4,48,1536]{2,1,0:T(8,128)(2,1)}, bf16[4,48,1536]{2,1,0:T(8,128)(2,1)}, u32[]{:S(2)}, u32[]{:S(2)}) collective-permute-start(bf16[4,48,1536]{2,1,0:T(8,128)(2,1)} %get-tuple-element.183), channel_id=1, source_target_pairs={{0,1},{1,0},{2,3},{3,2},{4,5},{5,4},{6,7},{7,6},{8,9},{9,8},{10,11... | collective-permute-start | bytes 1769480 | tf_op jit(solution)/shard_map/ppermute | solution.py:757
  143.1 28.0 %collective-permute-start.25 = (bf16[4,48,1536]{2,1,0:T(8,128)(2,1)}, bf16[4,48,1536]{2,1,0:T(8,128)(2,1)}, u32[]{:S(2)}, u32[]{:S(2)}) collective-permute-start(bf16[4,48,1536]{2,1,0:T(8,128)(2,1)} %get-tuple-element.184), channel_id=1, source_target_pairs={{0,5},{1,4},{2,7},{3,6},{4,1},{5,0},{6,3},{7,2},{8,13},{9,12},{10,... | collective-permute-start | bytes 1769480 | tf_op jit(solution)/shard_map/ppermute | solution.py:757
  154.1 14.2 %collective-permute-start.22 = (bf16[4,2,48,768]{3,2,1,0:T(8,128)(2,1)}, bf16[4,2,48,768]{3,2,1,0:T(8,128)(2,1)S(1)}, u32[]{:S(2)}, u32[]{:S(2)}) collective-permute-start(bf16[4,2,48,768]{3,2,1,0:T(8,128)(2,1)} %get-tuple-element.169), channel_id=1, source_target_pairs={{0,2},{1,3},{2,0},{3,1},{4,6},{5,7},{6,4},{7,5},{8,10},{9,11},{10,... | collective-permute-start | bytes 1769480 | tf_op jit(solution)/shard_map/ppermute | solution.py:757
  172.8 17.0 %collective-permute-start.26 = (bf16[2,48,1536]{2,1,0:T(8,128)(2,1)S(1)}, bf16[2,48,1536]{2,1,0:T(8,128)(2,1)S(1)}, u32[]{:S(2)}, u32[]{:S(2)}) collective-permute-start(bf16[2,48,1536]{2,1,0:T(8,128)(2,1)S(1)} %constant_dynamic-slice_fusion.1), channel_id=1, source_target_pairs={{0,16},{1,17},{2,18},{3,19},{4,20},{5,21},{6,22},{7,23},{8,24},{9,... | collective-permute-start | bytes 884744 | tf_op jit(solution)/shard_map/ppermute | solution.py:757
  173.0 31.3 %collective-permute-start.28 = (bf16[4,48,1920]{2,1,0:T(8,128)(2,1)}, bf16[4,48,1920]{2,1,0:T(8,128)(2,1)S(1)}, u32[]{:S(2)}, u32[]{:S(2)}) collective-permute-start(bf16[4,48,1920]{2,1,0:T(8,128)(2,1)} %pad_maximum_fusion.2), channel_id=1, source_target_pairs={{0,4},{1,5},{2,6},{3,7},{4,0},{5,1},{6,2},{7,3},{8,12},{9,13},{10,... | collective-permute-start | bytes 2211848 | tf_op jit(solution)/shard_map/ppermute | solution.py:757
  174.5 29.8 %collective-permute-start.29 = (bf16[4,48,1920]{2,1,0:T(8,128)(2,1)S(1)}, bf16[4,48,1920]{2,1,0:T(8,128)(2,1)S(1)}, u32[]{:S(2)}, u32[]{:S(2)}) collective-permute-start(bf16[4,48,1920]{2,1,0:T(8,128)(2,1)S(1)} %pad_maximum_fusion.3), channel_id=1, source_target_pairs={{0,1},{1,0},{2,3},{3,2},{4,5},{5,4},{6,7},{7,6},{8,9},{9,8},{10,11... | collective-permute-start | bytes 2211848 | tf_op jit(solution)/shard_map/ppermute | solution.py:757
  174.8 32.8 %collective-permute-start.30 = (bf16[4,48,1920]{2,1,0:T(8,128)(2,1)S(1)}, bf16[4,48,1920]{2,1,0:T(8,128)(2,1)S(1)}, u32[]{:S(2)}, u32[]{:S(2)}) collective-permute-start(bf16[4,48,1920]{2,1,0:T(8,128)(2,1)S(1)} %pad_maximum_fusion.4), channel_id=1, source_target_pairs={{0,5},{1,4},{2,7},{3,6},{4,1},{5,0},{6,3},{7,2},{8,13},{9,12},{10,... | collective-permute-start | bytes 2211848 | tf_op jit(solution)/shard_map/ppermute | solution.py:757
  190.0 14.3 %collective-permute-start.27 = (bf16[1,48,1536]{2,1,0:T(8,128)(2,1)S(1)}, bf16[1,48,1536]{2,1,0:T(8,128)(2,1)S(1)}, u32[]{:S(2)}, u32[]{:S(2)}) collective-permute-start(bf16[1,48,1536]{2,1,0:T(8,128)(2,1)S(1)} %constant_dynamic-slice_fusion), channel_id=1, source_target_pairs={{0,8},{1,9},{2,10},{3,11},{4,12},{5,13},{6,14},{7,15},{8,0},{9,1},... | collective-permute-start | bytes 442376 | tf_op jit(solution)/shard_map/ppermute | solution.py:757
  208.5 4.2 %collective-permute-start.31 = (bf16[4,2,48,2560]{3,2,1,0:T(8,128)(2,1)}, bf16[4,2,48,2560]{3,2,1,0:T(8,128)(2,1)S(1)}, u32[]{:S(2)}, u32[]{:S(2)}) collective-permute-start(bf16[4,2,48,2560]{3,2,1,0:T(8,128)(2,1)} %get-tuple-element.220), channel_id=1, source_target_pairs={{0,2},{1,3},{2,0},{3,1},{4,6},{5,7},{6,4},{7,5},{8,10},{9,11},{10,... | collective-permute-start | bytes 5898248 | tf_op jit(solution)/shard_map/ppermute | solution.py:757
  213.4 10.6 %collective-permute-start.35 = (bf16[48,1920]{1,0:T(8,128)(2,1)S(1)}, bf16[48,1920]{1,0:T(8,128)(2,1)S(1)}, u32[]{:S(2)}, u32[]{:S(2)}) collective-permute-start(bf16[48,1920]{1,0:T(8,128)(2,1)S(1)} %get-tuple-element.232), channel_id=1, source_target_pairs={{0,8},{1,9},{2,10},{3,11},{4,12},{5,13},{6,14},{7,15},{8,0},{9,1},... | collective-permute-start | bytes 552968 | tf_op jit(solution)/shard_map/ppermute | solution.py:757
  214.9 16.3 %collective-permute-start.36 = (bf16[48,1920]{1,0:T(8,128)(2,1)S(1)}, bf16[48,1920]{1,0:T(8,128)(2,1)S(1)}, u32[]{:S(2)}, u32[]{:S(2)}) collective-permute-start(bf16[48,1920]{1,0:T(8,128)(2,1)S(1)} %get-tuple-element.233), channel_id=1, source_target_pairs={{0,16},{1,17},{2,18},{3,19},{4,20},{5,21},{6,22},{7,23},{8,24},{9,... | collective-permute-start | bytes 552968 | tf_op jit(solution)/shard_map/ppermute | solution.py:757
  216.1 15.1 %collective-permute-start.37 = (bf16[48,1920]{1,0:T(8,128)(2,1)S(1)}, bf16[48,1920]{1,0:T(8,128)(2,1)S(1)}, u32[]{:S(2)}, u32[]{:S(2)}) collective-permute-start(bf16[48,1920]{1,0:T(8,128)(2,1)S(1)} %get-tuple-element.234), channel_id=1, source_target_pairs={{0,24},{1,25},{2,26},{3,27},{4,28},{5,29},{6,30},{7,31},{8,16},{9,... | collective-permute-start | bytes 552968 | tf_op jit(solution)/shard_map/ppermute | solution.py:757
  218.0 14.2 %collective-permute-start.32 = (bf16[4,48,1280]{2,1,0:T(8,128)(2,1)S(1)}, bf16[4,48,1280]{2,1,0:T(8,128)(2,1)S(1)}, u32[]{:S(2)}, u32[]{:S(2)}) collective-permute-start(bf16[4,48,1280]{2,1,0:T(8,128)(2,1)S(1)} %get-tuple-element.226), channel_id=1, source_target_pairs={{0,4},{1,5},{2,6},{3,7},{4,0},{5,1},{6,2},{7,3},{8,12},{9,13},{10,... | collective-permute-start | bytes 1474568 | tf_op jit(solution)/shard_map/ppermute | solution.py:757
  219.7 23.0 %collective-permute-start.33 = (bf16[4,48,1280]{2,1,0:T(8,128)(2,1)S(1)}, bf16[4,48,1280]{2,1,0:T(8,128)(2,1)S(1)}, u32[]{:S(2)}, u32[]{:S(2)}) collective-permute-start(bf16[4,48,1280]{2,1,0:T(8,128)(2,1)S(1)} %get-tuple-element.227), channel_id=1, source_target_pairs={{0,1},{1,0},{2,3},{3,2},{4,5},{5,4},{6,7},{7,6},{8,9},{9,8},{10,11... | collective-permute-start | bytes 1474568 | tf_op jit(solution)/shard_map/ppermute | solution.py:757
  224.0 18.6 %collective-permute-start.34 = (bf16[4,48,1280]{2,1,0:T(8,128)(2,1)S(1)}, bf16[4,48,1280]{2,1,0:T(8,128)(2,1)S(1)}, u32[]{:S(2)}, u32[]{:S(2)}) collective-permute-start(bf16[4,48,1280]{2,1,0:T(8,128)(2,1)S(1)} %get-tuple-element.228), channel_id=1, source_target_pairs={{0,5},{1,4},{2,7},{3,6},{4,1},{5,0},{6,3},{7,2},{8,13},{9,12},{10,... | collective-permute-start | bytes 1474568 | tf_op jit(solution)/shard_map/ppermute | solution.py:757
  243.0 18.7 %collective-permute-start.39 = (bf16[328,768]{1,0:T(8,128)(2,1)S(1)}, bf16[328,768]{1,0:T(8,128)(2,1)S(1)}, u32[]{:S(2)}, u32[]{:S(2)}) collective-permute-start(bf16[328,768]{1,0:T(8,128)(2,1)S(1)} %slice.133), channel_id=1, source_target_pairs={{0,1},{1,0},{2,3},{3,2},{4,5},{5,4},{6,7},{7,6},{8,9},{9,8},{10,11... | collective-permute-start | bytes 1511432 | tf_op jit(solution)/shard_map/ppermute | solution.py:757
  243.5 6.1 %collective-permute-start.40 = (bf16[48,1280]{1,0:T(8,128)(2,1)S(1)}, bf16[48,1280]{1,0:T(8,128)(2,1)S(1)}, u32[]{:S(2)}, u32[]{:S(2)}) collective-permute-start(bf16[48,1280]{1,0:T(8,128)(2,1)S(1)} %get-tuple-element.242), channel_id=1, source_target_pairs={{0,8},{1,9},{2,10},{3,11},{4,12},{5,13},{6,14},{7,15},{8,0},{9,1},... | collective-permute-start | bytes 368648 | tf_op jit(solution)/shard_map/ppermute | solution.py:757
  244.1 10.7 %collective-permute-start.41 = (bf16[48,1280]{1,0:T(8,128)(2,1)S(1)}, bf16[48,1280]{1,0:T(8,128)(2,1)S(1)}, u32[]{:S(2)}, u32[]{:S(2)}) collective-permute-start(bf16[48,1280]{1,0:T(8,128)(2,1)S(1)} %get-tuple-element.243), channel_id=1, source_target_pairs={{0,16},{1,17},{2,18},{3,19},{4,20},{5,21},{6,22},{7,23},{8,24},{9,... | collective-permute-start | bytes 368648 | tf_op jit(solution)/shard_map/ppermute | solution.py:757
  246.5 8.3 %collective-permute-start.42 = (bf16[48,1280]{1,0:T(8,128)(2,1)S(1)}, bf16[48,1280]{1,0:T(8,128)(2,1)S(1)}, u32[]{:S(2)}, u32[]{:S(2)}) collective-permute-start(bf16[48,1280]{1,0:T(8,128)(2,1)S(1)} %get-tuple-element.244), channel_id=1, source_target_pairs={{0,24},{1,25},{2,26},{3,27},{4,28},{5,29},{6,30},{7,31},{8,16},{9,... | collective-permute-start | bytes 368648 | tf_op jit(solution)/shard_map/ppermute | solution.py:757
  248.0 13.6 %collective-permute-start.38 = (bf16[48,3456]{1,0:T(8,128)(2,1)S(1)}, bf16[48,3456]{1,0:T(8,128)(2,1)S(1)}, u32[]{:S(2)}, u32[]{:S(2)}) collective-permute-start(bf16[48,3456]{1,0:T(8,128)(2,1)S(1)} %pad_maximum_fusion.7), channel_id=1, source_target_pairs={{0,1},{1,0},{2,3},{3,2},{4,5},{5,4},{6,7},{7,6},{8,9},{9,8},{10,11... | collective-permute-start | bytes 995336 | tf_op jit(solution)/shard_map/ppermute | solution.py:757
  261.8 5.7 %collective-permute-start.43 = (bf16[48,1280]{1,0:T(8,128)(2,1)S(1)}, bf16[48,1280]{1,0:T(8,128)(2,1)S(1)}, u32[]{:S(2)}, u32[]{:S(2)}) collective-permute-start(bf16[48,1280]{1,0:T(8,128)(2,1)S(1)} %add_convert_fusion.10), channel_id=1, source_target_pairs={{0,1},{1,0},{2,3},{3,2},{4,5},{5,4},{6,7},{7,6},{8,9},{9,8},{10,11... | collective-permute-start | bytes 368648 | tf_op jit(solution)/shard_map/ppermute | solution.py:757
  (31 other events, 207.6 us)
Sparse Core Ops, SparseCore 0:
  10.9 89.8 all-gather.1

commit v5 on v4

--- a/solution.py
+++ b/solution.py
@@ -487,7 +487,7 @@
 
 def mlp_first_kernel(
     shape, second_ref, dz_ref, up_ref, up_bias_ref, down_ref, middle_ref, small_ref,
-    out_ref, kept_ref, sent_ref, pre_grad_ref, up_bias_grad_ref, down_grad_ref,
+    out_ref, away_ref, kept_ref, sent_ref, pre_grad_ref, up_bias_grad_ref, down_grad_ref,
 ):
     step = pl.program_id(0)
     owners, pieces, dim = shape
@@ -529,6 +529,10 @@
     def _():
         out_ref[...] += out_part
 
+    @pl.when(step == pl.num_programs(0) - 1)
+    def _():
+        away_ref[...] = out_ref[away_ref.shape[0] :, :].astype(LOW)
+
 
 def mlp_first(second, dz, up_down, up_bias, middle, small, owners):
     rows, dim = second.shape
@@ -551,6 +555,7 @@
         ],
         out_specs=[
             whole,
+            pl.BlockSpec((rows // 2, dim), lambda j: (0, 0)),
             pl.BlockSpec((1, 2, shard, width), lambda j: (j, 0, 0, 0)),
             pl.BlockSpec((1, 2, shard, width), lambda j: (j, 0, 0, 0)),
             pl.BlockSpec((rows, dim), lambda j: (0, j)),
@@ -558,6 +563,7 @@
         ],
         out_shape=[
             jax.ShapeDtypeStruct((rows, dim), F32),
+            jax.ShapeDtypeStruct((rows // 2, dim), LOW),
             jax.ShapeDtypeStruct((4, 2, shard, width), LOW),
             jax.ShapeDtypeStruct((4, 2, shard, width), LOW),
             jax.ShapeDtypeStruct((rows, width), LOW),
@@ -687,7 +693,8 @@
 
 def last_kernel(
     inputs_ref, rows_ref, q_low, k_low, v_low, q_high, k_high, v_high, qkv_full_ref,
-    middle_grad_ref, small_ref, up_bias_ref, input_grad_ref, kept_ref, sent_ref, total_ref,
+    middle_grad_ref, small_ref, up_bias_ref,
+    input_grad_ref, away_ref, kept_ref, sent_ref, total_ref,
 ):
     unit, inverse = norm_parts(inputs_ref[...].astype(F32))
     gain = rows_ref[0:1]
@@ -696,7 +703,9 @@
     qkv_grad = jnp.concatenate(grads, axis=1)
     dim = unit.shape[1]
     normed_grad = dot_nt(qkv_grad, qkv_full_ref[...])
-    input_grad_ref[...] = middle_grad_ref[...] + norm_back(unit, inverse, gain, normed_grad)
+    input_grad = middle_grad_ref[...] + norm_back(unit, inverse, gain, normed_grad)
+    input_grad_ref[...] = input_grad
+    away_ref[...] = input_grad[away_ref.shape[0] :].astype(LOW)
     total_ref[:, : 3 * dim] = dot_tn(normed, qkv_grad).astype(LOW)
     bias_of = column_sums(qkv_grad.astype(F32))
     rows = [column_sums(normed_grad * unit), column_sums(normed_grad), bias_of[:, :dim], bias_of[:, 2 * dim :]]
@@ -722,8 +731,8 @@
         in_specs=[whole(rows, dim), whole(*small_rows.shape)]
         + [whole(*g.shape) for g in (*grads_low, *grads_high)]
         + [whole(dim, 3 * dim), whole(rows, dim), whole(*small.shape), whole(*up_bias.shape)],
-        out_specs=[whole(rows, dim), whole(*split.shape), whole(*split.shape)],
-        out_shape=[jax.ShapeDtypeStruct((rows, dim), F32), split, split],
+        out_specs=[whole(rows, dim), whole(rows // 2, dim), whole(*split.shape), whole(*split.shape)],
+        out_shape=[jax.ShapeDtypeStruct((rows, dim), F32), jax.ShapeDtypeStruct((rows // 2, dim), LOW), split, split],
         scratch_shapes=[pltpu.VMEM((dim, columns), LOW)],
         compiler_params=pltpu.CompilerParams(vmem_limit_bytes=VMEM),
         cost_estimate=cost(1),
@@ -876,10 +885,10 @@
     inputs_low = both[:, :shard_rows].reshape(2 * shard_rows, dim)
     mask_column = both[:, shard_rows, :shard_rows].astype(F32).reshape(2 * shard_rows, 1)
     merged, logs, *qkv, middle, second = attention_forward(inputs_low, small, first, mask_column)
-    output, down_kept, down_sent, pre_grad, grad_up_bias = mlp_first(
+    output, output_away, down_kept, down_sent, pre_grad, grad_up_bias = mlp_first(
         second, down_in, up_down, up_bias, middle, small, owners
     )
-    output_own, output_away = output[:shard_rows], output[shard_rows:].astype(LOW)
+    output_own = output[:shard_rows]
     pre_grad, output_away, down_sent = tie(pre_grad, output_away, down_sent)
     output_back, down_sent = swap(output_away, y=1), swap(down_sent, core=1)
     second_grad, up_kept, up_sent = mlp_second(second, pre_grad, up_down, owners)
@@ -914,13 +923,12 @@
     down_two = total([half_line(down_line, z // 2), down_away])
     grad_up_bias, down_away = tie(grad_up_bias, half_line(down_two, 1 - z % 2))
     down_away = swap(down_away, z=1)
-    input_grad, last_kept, last_sent = last_backward(
+    input_grad, input_away, last_kept, last_sent = last_backward(
         inputs_low, small, grads_low, grads_high, first, middle_grad, small_grads, grad_up_bias, owners
     )
-    tied = tie(input_grad, last_kept, last_sent, down_away, *up_pieces)
-    input_grad, last_kept, last_sent, down_away = tied[:4]
-    up_line = total(tied[4:])
-    input_away = input_grad[shard_rows:].astype(LOW)
+    tied = tie(input_grad, input_away, last_kept, last_sent, down_away, *up_pieces)
+    input_grad, input_away, last_kept, last_sent, down_away = tied[:5]
+    up_line = total(tied[5:])
     last_sent = swap(last_sent, core=1)
     last_pieces = plane_pieces(total([last_kept, last_sent]))
     tied = tie(*last_pieces, *line_pieces(up_line))

time: 281 us -> 280 us (level)
  transfers between devices with their start and end apart: 45 -> 45, of which waited for: 14 -> 14; matrix products, arithmetic and copies ran while one was open for 6% -> 6% of each run, Pallas kernels for 31% -> 32%
where the time goes in v5:
time: 280 us; the launch traced here: 276 us
  Pallas kernels  108 us (39%)
  waiting for transfers between devices  81.8 us (29%)
  starting transfers between devices  41.9 us (15%)
  other arithmetic  16.6 us (6%)
  between operations  15.4 us (6%)
  local copies, waits for them, and re-layouts  11.8 us (4%)
    ppermute x44, waiting for transfers between devices, swap(): lax.ppermute(block, ('img', 'seq'), [(i, i ^ bits) for i in range(32)])  81.8 us
    ppermute x44, starting transfers between devices, swap(): lax.ppermute(block, ('img', 'seq'), [(i, i ^ bits) for i in range(32)])  41.8 us
    pallas_call x2, Pallas kernels, attention_backward(): pl.pallas_call(functools.partial(attention_backward_kernel, size ** (-0.5...  26.4 us
    pallas_call x1, Pallas kernels, mlp_first(): pl.pallas_call(functools.partial(mlp_first_kernel, (some, pieces, dim)),...  21.1 us
    pallas_call x1, Pallas kernels, attention_forward(): pl.pallas_call(functools.partial(attention_forward_kernel, size ** (-0.5)...  21 us
    pallas_call x1, Pallas kernels, mlp_second(): pl.pallas_call(mlp_second_kernel, grid=(width // dim,), in_specs=[whole,...  13.5 us
    pallas_call x1, Pallas kernels, last_backward(): pl.pallas_call(last_kernel, grid=(1,), in_specs=[whole(rows, dim), whole(...  12.9 us
    pallas_call x1, Pallas kernels, middle_backward(): pl.pallas_call(middle_kernel, grid=(1,), in_specs=[whole, whole, whole, p...  8.29 us
  transfers between devices with their start and end apart: 45, of which 14 were waited for; matrix products, arithmetic and copies ran while one was open for 6% of the time, Pallas kernels for 32%

profile of v5, /device:TPU:0, one launch (start us, length us, event | category | flops | bytes accessed | tf_op | source)
XLA Modules:
  0.0 276.0 jit_solution(9158521730370613559)
XLA Ops:
  7.2 1.2 copy.47
  8.6 1.9 pad_maximum_fusion.5
  10.7 3.1 %collective-permute-start.3 = (bf16[344,768]{1,0:T(8,128)(2,1)S(1)}, bf16[344,768]{1,0:T(8,128)(2,1)S(1)}, u32[]{:S(2)}, u32[]{:S(2)}) collective-permute-start(bf16[344,768]{1,0:T(8,128)(2,1)S(1)} %get-tuple-element.277), channel_id=1, source_target_pairs={{0,1},{1,0},{2,3},{3,2},{4,5},{5,4},{6,7},{7,6},{8,9},{9,8},{10,11... | collective-permute-start | bytes 1585160 | tf_op jit(solution)/shard_map/ppermute | solution.py:766
  14.2 3.7 %collective-permute-start.2 = (bf16[1,48,1664]{2,1,0:T(8,128)(2,1)S(1)}, bf16[1,48,1664]{2,1,0:T(8,128)(2,1)S(1)}, u32[]{:S(2)}, u32[]{:S(2)}) collective-permute-start(bf16[1,48,1664]{2,1,0:T(8,128)(2,1)S(1)} %fusion.9.refs_0_), channel_id=1, source_target_pairs={{0,24},{1,25},{2,26},{3,27},{4,28},{5,29},{6,30},{7,31},{8,16},{9,... | collective-permute-start | bytes 479240 | tf_op jit(solution)/shard_map/ppermute | solution.py:766
  19.0 4.2 %collective-permute-done.2 = bf16[1,48,1664]{2,1,0:T(8,128)(2,1)S(1)} collective-permute-done((bf16[1,48,1664]{2,1,0:T(8,128)(2,1)S(1)}, bf16[1,48,1664]{2,1,0:T(8,128)(2,1)S(1)}, u32[]{:S(2)}, u32[]{:S(2)}) %collective-permute-start.2) | collective-permute-done | bytes 159776 | tf_op jit(solution)/shard_map/ppermute | solution.py:766
  23.2 1.5 collective-permute-start.4
  24.7 20.3 %collective-permute-done.1 = bf16[1,48,1664]{2,1,0:T(8,128)(2,1)S(1)} collective-permute-done((bf16[1,48,1664]{2,1,0:T(8,128)(2,1)S(1)}, bf16[1,48,1664]{2,1,0:T(8,128)(2,1)S(1)}, u32[]{:S(2)}, u32[]{:S(2)}) %collective-permute-start.1) | collective-permute-done | bytes 159776 | tf_op jit(solution)/shard_map/ppermute | solution.py:766
  45.1 1.6 collective-permute-start.14
  46.7 7.2 %collective-permute-done.14.refs_12_ = bf16[3,48,1664]{2,1,0:T(8,128)(2,1)S(1)} collective-permute-done((bf16[3,48,1664]{2,1,0:T(8,128)(2,1)S(1)}, bf16[3,48,1664]{2,1,0:T(8,128)(2,1)S(1)}, u32[]{:S(2)}, u32[]{:S(2)}) %collective-permute-start.14) | collective-permute-done | bytes 479264 | tf_op jit(solution)/shard_map/ppermute | solution.py:766
  54.4 2.0 collective-permute-start.9
  57.0 12.2 %collective-permute-done.9.refs_6_ = bf16[1,48,1664]{2,1,0:T(8,128)(2,1)} collective-permute-done((bf16[1,48,1664]{2,1,0:T(8,128)(2,1)S(1)}, bf16[1,48,1664]{2,1,0:T(8,128)(2,1)}, u32[]{:S(2)}, u32[]{:S(2)}) %collective-permute-start.9) | collective-permute-done | bytes 159776 | tf_op jit(solution)/shard_map/ppermute | solution.py:766
  70.7 0.9 reshape.101.mask_ref
  71.6 1.0 fusion
  73.2 5.3 %assemble.1 = (bf16[16,48,3328]{2,1,0:T(8,128)(2,1)}, f32[16,768]{1,0:T(8,128)}) custom-call(bf16[1,48,1664]{2,1,0:T(8,128)(2,1)} %copy-done.12, bf16[1,48,1664]{2,1,0:T(8,128)(2,1)} %copy-done.20, bf16[1,48,1664]{2,1,0:T(8,128)(2,1)} %copy-done.18, bf16[1,48,1664]{2,1,0:T(8,128)(2,1)} %copy-done.21, bf16[1,48,1664]{2,1,0:T(8,128)(2,1)} %copy-done.19, ...), custom_call_target="tpu_custom_call" | custom-call | tf_op jit(solution)/shard_map/assemble/pallas_call | solution.py:796
  78.5 21.0 %attention_forward.1 = (bf16[656,768]{1,0:T(8,128)(2,1)}, f32[6,2,656]{2,1,0:T(2,128)}, bf16[656,768]{1,0:T(8,128)(2,1)}, bf16[656,768]{1,0:T(8,128)(2,1)}, bf16...) custom-call(bf16[656,768]{1,0:T(8,128)(2,1)} %bitcast.108, ...), custom_call_target="tpu_custom_call" | custom-call | flops 20700000256 | bytes 1 | tf_op jit(solution)/shard_map/attention_forward/pallas_call | solution.py:391
  101.0 1.0 pad_maximum_fusion.dz_ref
  102.0 21.1 %mlp_first.1 = (f32[656,768]{1,0:T(8,128)}, bf16[328,768]{1,0:T(8,128)(2,1)}, bf16[4,2,48,3072]{3,2,1,0:T(8,128)(2,1)}, bf16[4,2,48,3072]{3,2,1,0:T(8,128)(2,1)}...) custom-call(bf16[656,768]{1,0:T(8,128)(2,1)} %get-tuple-element.143.second_ref, ...), custom_call_target="tpu_custom_call" | custom-call | flops 21849999360 | bytes 1 | tf_op jit(solution)/shard_map/mlp_first/pallas_call | solution.py:544
  123.3 1.9 collective-permute-start.19
  125.3 13.5 %mlp_second.1 = (f32[656,768]{1,0:T(8,128)}, bf16[4,2,48,3072]{3,2,1,0:T(8,128)(2,1)}, bf16[4,2,48,3072]{3,2,1,0:T(8,128)(2,1)}) custom-call(bf16[656,768]{1,0:T(8,128)(2,1)} %get-tuple-element.143.second_ref, bf16[656,3072]{1,0:T(8,128)(2,1)} %get-tuple-element.150.pre_grad_ref, bf16[768,6144]{1,0:T(8,128)(2,1)} %all-gather.2.cloned.1.call-done.up_ref), custom_call_target="tpu_custom_call" | custom-call | flops 1150000000 | bytes 1 | tf_op jit(solution)/shard_map/mlp_second/pallas_call | solution.py:601
  139.7 1.3 dynamic-slice_bitcast_fusion.4
  142.1 2.6 collective-permute-start.25
  144.7 8.3 %middle_backward.1 = (f32[656,768]{1,0:T(8,128)}, bf16[656,768]{1,0:T(8,128)(2,1)}, bf16[4,2,48,768]{3,2,1,0:T(8,128)(2,1)}, bf16[4,2,48,768]{3,2,1,0:T(8,128)(2,1)}, f32[4,768]{1,0:T(4,128)}) custom-call(f32[656,768]{1,0:T(8,128)} %get-tuple-element.145.middle_ref, f32[656,768]{1,0:T(8,128)} %get-tuple-element.161.grad_ref, ...), custom_call_target="tpu_custom_call" | custom-call | flops 1150000000 | bytes 1 | tf_op jit(solution)/shard_map/middle_backward/pallas_call | solution.py:662
  153.9 13.1 %attention_backward.2 = (bf16[656,384]{1,0:T(8,128)(2,1)}, bf16[656,384]{1,0:T(8,128)(2,1)}, bf16[656,384]{1,0:T(8,128)(2,1)}) custom-call(bf16[656,768]{1,0:T(8,128)(2,1)} %get-tuple-element.174.query_ref, bf16[656,768]{1,0:T(8,128)(2,1)} %get-tuple-element.175.key_ref, bf16[656,768]{1,0:T(8,128)(2,1)} %get-tuple-element.176.value_ref, ...), custom_call_target="tpu_custom_call" | custom-call | flops 1150000000 | bytes 1 | tf_op jit(solution)/shard_map/attention_backward/pallas_call | solution.py:460
  168.5 0.9 pad_maximum_fusion.2
  170.0 1.7 add_convert_fusion.4
  171.9 1.6 collective-permute-start.28
  173.9 1.5 collective-permute-start.30
  175.4 13.3 %attention_backward.3 = (bf16[656,384]{1,0:T(8,128)(2,1)}, bf16[656,384]{1,0:T(8,128)(2,1)}, bf16[656,384]{1,0:T(8,128)(2,1)}) custom-call(bf16[656,768]{1,0:T(8,128)(2,1)} %get-tuple-element.174.query_ref, bf16[656,768]{1,0:T(8,128)(2,1)} %get-tuple-element.175.key_ref, bf16[656,768]{1,0:T(8,128)(2,1)} %get-tuple-element.176.value_ref, ...), custom_call_target="tpu_custom_call" | custom-call | flops 1150000000 | bytes 1 | tf_op jit(solution)/shard_map/attention_backward/pallas_call | solution.py:460
  188.8 1.6 collective-permute-start.27
  190.5 12.9 %last_backward.1 = (f32[656,768]{1,0:T(8,128)}, bf16[328,768]{1,0:T(8,128)(2,1)}, bf16[4,2,48,2560]{3,2,1,0:T(8,128)(2,1)}, bf16[4,2,48,2560]{3,2,1,0:T(8,128)(2,1)}) custom-call(bf16[656,768]{1,0:T(8,128)(2,1)} %bitcast.109, f32[16,768]{1,0:T(8,128)} %get-tuple-element.140.small_ref.bias_ref.rows_ref, bf16[656,384]{1,0:T(8,128)(2,1)} %get-tuple-element.181.q_low, ...), custom_call_target="tpu_custom_call" | custom-call | flops 1150000000 | bytes 1 | tf_op jit(solution)/shard_map/last_backward/pallas_call | solution.py:728
  203.4 3.1 %collective-permute-done.30 = bf16[4,48,1920]{2,1,0:T(8,128)(2,1)S(1)} collective-permute-done((bf16[4,48,1920]{2,1,0:T(8,128)(2,1)S(1)}, bf16[4,48,1920]{2,1,0:T(8,128)(2,1)S(1)}, u32[]{:S(2)}, u32[]{:S(2)}) %collective-permute-start.30) | collective-permute-done | bytes 737312 | tf_op jit(solution)/shard_map/ppermute | solution.py:766
  207.4 1.4 slice_bitcast_fusion.1
  208.9 1.1 bitcast_convert_fusion.1
  210.5 1.1 collective-permute-done.31
  212.3 1.5 collective-permute-start.35
  213.8 1.2 collective-permute-start.36
  215.0 1.8 collective-permute-start.37
  216.8 1.7 collective-permute-start.32
  218.9 4.0 %collective-permute-done.35 = bf16[48,1920]{1,0:T(8,128)(2,1)S(1)} collective-permute-done((bf16[48,1920]{1,0:T(8,128)(2,1)S(1)}, bf16[48,1920]{1,0:T(8,128)(2,1)S(1)}, u32[]{:S(2)}, u32[]{:S(2)}) %collective-permute-start.35) | collective-permute-done | bytes 184352 | tf_op jit(solution)/shard_map/ppermute | solution.py:766
  222.9 1.7 collective-permute-start.34
  224.6 5.5 %collective-permute-done.36 = bf16[48,1920]{1,0:T(8,128)(2,1)S(1)} collective-permute-done((bf16[48,1920]{1,0:T(8,128)(2,1)S(1)}, bf16[48,1920]{1,0:T(8,128)(2,1)S(1)}, u32[]{:S(2)}, u32[]{:S(2)}) %collective-permute-start.36) | collective-permute-done | bytes 184352 | tf_op jit(solution)/shard_map/ppermute | solution.py:766
  231.0 10.4 %collective-permute-done.33 = bf16[4,48,1280]{2,1,0:T(8,128)(2,1)S(1)} collective-permute-done((bf16[4,48,1280]{2,1,0:T(8,128)(2,1)S(1)}, bf16[4,48,1280]{2,1,0:T(8,128)(2,1)S(1)}, u32[]{:S(2)}, u32[]{:S(2)}) %collective-permute-start.33) | collective-permute-done | bytes 491552 | tf_op jit(solution)/shard_map/ppermute | solution.py:766
  242.9 2.4 collective-permute-start.41
  245.3 1.5 collective-permute-start.42
  246.8 1.6 collective-permute-start.38
  248.4 5.2 %collective-permute-done.41 = bf16[48,1280]{1,0:T(8,128)(2,1)S(1)} collective-permute-done((bf16[48,1280]{1,0:T(8,128)(2,1)S(1)}, bf16[48,1280]{1,0:T(8,128)(2,1)S(1)}, u32[]{:S(2)}, u32[]{:S(2)}) %collective-permute-start.41) | collective-permute-done | bytes 122912 | tf_op jit(solution)/shard_map/ppermute | solution.py:766
  253.6 6.8 %collective-permute-done.38 = bf16[48,3456]{1,0:T(8,128)(2,1)S(1)} collective-permute-done((bf16[48,3456]{1,0:T(8,128)(2,1)S(1)}, bf16[48,3456]{1,0:T(8,128)(2,1)S(1)}, u32[]{:S(2)}, u32[]{:S(2)}) %collective-permute-start.38) | collective-permute-done | bytes 331808 | tf_op jit(solution)/shard_map/ppermute | solution.py:766
  263.1 2.3 maximum_select_fusion
  (188 shorter events, 22.8 us)
Async XLA Ops:
  7.2 94.8 %all-gather.2.cloned.1.call-start = ((), (), s32[]{:S(2)}) async-start(), calls=%async_computation | async-start | bytes 10027008 | tf_op jit(solution)/shard_map/all_gather | solution.py:756
  10.5 59.3 %copy-start.4 = (bf16[2,328,768]{2,1,0:T(8,128)(2,1)S(1)}, bf16[2,328,768]{2,1,0:T(8,128)(2,1)}, u32[]{:S(2)}) copy-start(bf16[2,328,768]{2,1,0:T(8,128)(2,1)} %param.31) | copy-start | bytes 3022852
  10.7 34.4 %collective-permute-start.3 = (bf16[344,768]{1,0:T(8,128)(2,1)S(1)}, bf16[344,768]{1,0:T(8,128)(2,1)S(1)}, u32[]{:S(2)}, u32[]{:S(2)}) collective-permute-start(bf16[344,768]{1,0:T(8,128)(2,1)S(1)} %get-tuple-element.277), channel_id=1, source_target_pairs={{0,1},{1,0},{2,3},{3,2},{4,5},{5,4},{6,7},{7,6},{8,9},{9,8},{10,11... | collective-permute-start | bytes 1585160 | tf_op jit(solution)/shard_map/ppermute | solution.py:766
  14.2 56.4 %copy-start.12 = (bf16[1,48,1664]{2,1,0:T(8,128)(2,1)}, bf16[1,48,1664]{2,1,0:T(8,128)(2,1)S(1)}, u32[]{:S(2)}) copy-start(bf16[1,48,1664]{2,1,0:T(8,128)(2,1)S(1)} %fusion.9.refs_0_) | copy-start | bytes 479236
  14.2 9.0 %collective-permute-start.2 = (bf16[1,48,1664]{2,1,0:T(8,128)(2,1)S(1)}, bf16[1,48,1664]{2,1,0:T(8,128)(2,1)S(1)}, u32[]{:S(2)}, u32[]{:S(2)}) collective-permute-start(bf16[1,48,1664]{2,1,0:T(8,128)(2,1)S(1)} %fusion.9.refs_0_), channel_id=1, source_target_pairs={{0,24},{1,25},{2,26},{3,27},{4,28},{5,29},{6,30},{7,31},{8,16},{9,... | collective-permute-start | bytes 479240 | tf_op jit(solution)/shard_map/ppermute | solution.py:766
  17.9 27.0 %collective-permute-start.1 = (bf16[1,48,1664]{2,1,0:T(8,128)(2,1)S(1)}, bf16[1,48,1664]{2,1,0:T(8,128)(2,1)S(1)}, u32[]{:S(2)}, u32[]{:S(2)}) collective-permute-start(bf16[1,48,1664]{2,1,0:T(8,128)(2,1)S(1)} %fusion.9.refs_0_), channel_id=1, source_target_pairs={{0,16},{1,17},{2,18},{3,19},{4,20},{5,21},{6,22},{7,23},{8,24},{9,... | collective-permute-start | bytes 479240 | tf_op jit(solution)/shard_map/ppermute | solution.py:766
  17.9 27.0 %collective-permute-start = (bf16[1,48,1664]{2,1,0:T(8,128)(2,1)S(1)}, bf16[1,48,1664]{2,1,0:T(8,128)(2,1)S(1)}, u32[]{:S(2)}, u32[]{:S(2)}) collective-permute-start(bf16[1,48,1664]{2,1,0:T(8,128)(2,1)S(1)} %fusion.9.refs_0_), channel_id=1, source_target_pairs={{0,8},{1,9},{2,10},{3,11},{4,12},{5,13},{6,14},{7,15},{8,0},{9,1},... | collective-permute-start | bytes 479240 | tf_op jit(solution)/shard_map/ppermute | solution.py:766
  18.7 26.3 %collective-permute-start.5 = (bf16[1,48,1664]{2,1,0:T(8,128)(2,1)S(1)}, bf16[1,48,1664]{2,1,0:T(8,128)(2,1)S(1)}, u32[]{:S(2)}, u32[]{:S(2)}) collective-permute-start(bf16[1,48,1664]{2,1,0:T(8,128)(2,1)S(1)} %fusion.9.refs_0_), channel_id=1, source_target_pairs={{0,1},{1,0},{2,3},{3,2},{4,5},{5,4},{6,7},{7,6},{8,9},{9,8},{10,11... | collective-permute-start | bytes 479240 | tf_op jit(solution)/shard_map/ppermute | solution.py:766
  23.2 21.9 %collective-permute-start.4 = (bf16[1,48,1664]{2,1,0:T(8,128)(2,1)S(1)}, bf16[1,48,1664]{2,1,0:T(8,128)(2,1)S(1)}, u32[]{:S(2)}, u32[]{:S(2)}) collective-permute-start(bf16[1,48,1664]{2,1,0:T(8,128)(2,1)S(1)} %fusion.9.refs_0_), channel_id=1, source_target_pairs={{0,4},{1,5},{2,6},{3,7},{4,0},{5,1},{6,2},{7,3},{8,12},{9,13},{10,... | collective-permute-start | bytes 479240 | tf_op jit(solution)/shard_map/ppermute | solution.py:766
  45.0 25.6 %copy-start.3 = (bf16[3,48,1664]{2,1,0:T(8,128)(2,1)}, bf16[3,48,1664]{2,1,0:T(8,128)(2,1)S(1)}, u32[]{:S(2)}) copy-start(bf16[3,48,1664]{2,1,0:T(8,128)(2,1)S(1)} %pad_maximum_fusion.6.refs_8_) | copy-start | bytes 1437700
  45.1 8.8 %collective-permute-start.14 = (bf16[3,48,1664]{2,1,0:T(8,128)(2,1)S(1)}, bf16[3,48,1664]{2,1,0:T(8,128)(2,1)S(1)}, u32[]{:S(2)}, u32[]{:S(2)}) collective-permute-start(bf16[3,48,1664]{2,1,0:T(8,128)(2,1)S(1)} %pad_maximum_fusion.6.refs_8_), channel_id=1, source_target_pairs={{0,4},{1,5},{2,6},{3,7},{4,0},{5,1},{6,2},{7,3},{8,12},{9,13},{10,... | collective-permute-start | bytes 1437704 | tf_op jit(solution)/shard_map/ppermute | solution.py:766
  46.7 22.5 %collective-permute-start.12 = (bf16[3,48,1664]{2,1,0:T(8,128)(2,1)S(1)}, bf16[3,48,1664]{2,1,0:T(8,128)(2,1)}, u32[]{:S(2)}, u32[]{:S(2)}) collective-permute-start(bf16[3,48,1664]{2,1,0:T(8,128)(2,1)S(1)} %pad_maximum_fusion.6.refs_8_), channel_id=1, source_target_pairs={{0,1},{1,0},{2,3},{3,2},{4,5},{5,4},{6,7},{7,6},{8,9},{9,8},{10,11... | collective-permute-start | bytes 1437704 | tf_op jit(solution)/shard_map/ppermute | solution.py:766
  53.9 15.8 %collective-permute-start.16 = (bf16[3,48,1664]{2,1,0:T(8,128)(2,1)S(1)}, bf16[3,48,1664]{2,1,0:T(8,128)(2,1)}, u32[]{:S(2)}, u32[]{:S(2)}) collective-permute-start(bf16[3,48,1664]{2,1,0:T(8,128)(2,1)S(1)} %collective-permute-done.14.refs_12_), channel_id=1, source_target_pairs={{0,1},{1,0},{2,3},{3,2},{4,5},{5,4},{6,7},{7,6},{8,9},{9,8},{10,11... | collective-permute-start | bytes 1437704 | tf_op jit(solution)/shard_map/ppermute | solution.py:766
  53.9 2.5 collective-permute-start.6
  53.9 2.6 collective-permute-start.7
  54.4 14.8 %collective-permute-start.9 = (bf16[1,48,1664]{2,1,0:T(8,128)(2,1)S(1)}, bf16[1,48,1664]{2,1,0:T(8,128)(2,1)}, u32[]{:S(2)}, u32[]{:S(2)}) collective-permute-start(bf16[1,48,1664]{2,1,0:T(8,128)(2,1)S(1)} %collective-permute-done.4.refs_4_), channel_id=1, source_target_pairs={{0,1},{1,0},{2,3},{3,2},{4,5},{5,4},{6,7},{7,6},{8,9},{9,8},{10,11... | collective-permute-start | bytes 479240 | tf_op jit(solution)/shard_map/ppermute | solution.py:766
  56.4 13.5 %collective-permute-start.8 = (bf16[1,48,1664]{2,1,0:T(8,128)(2,1)S(1)}, bf16[1,48,1664]{2,1,0:T(8,128)(2,1)S(1)}, u32[]{:S(2)}, u32[]{:S(2)}) collective-permute-start(bf16[1,48,1664]{2,1,0:T(8,128)(2,1)S(1)} %collective-permute-done.4.refs_4_), channel_id=1, source_target_pairs={{0,2},{1,3},{2,0},{3,1},{4,6},{5,7},{6,4},{7,5},{8,10},{9,11},{10,... | collective-permute-start | bytes 479240 | tf_op jit(solution)/shard_map/ppermute | solution.py:766
  56.5 16.6 %collective-permute-start.11 = (bf16[3,48,1664]{2,1,0:T(8,128)(2,1)S(1)}, bf16[3,48,1664]{2,1,0:T(8,128)(2,1)}, u32[]{:S(2)}, u32[]{:S(2)}) collective-permute-start(bf16[3,48,1664]{2,1,0:T(8,128)(2,1)S(1)} %pad_maximum_fusion.6.refs_8_), channel_id=1, source_target_pairs={{0,2},{1,3},{2,0},{3,1},{4,6},{5,7},{6,4},{7,5},{8,10},{9,11},{10,... | collective-permute-start | bytes 1437704 | tf_op jit(solution)/shard_map/ppermute | solution.py:766
  69.2 4.0 %collective-permute-start.15 = (bf16[3,48,1664]{2,1,0:T(8,128)(2,1)S(1)}, bf16[3,48,1664]{2,1,0:T(8,128)(2,1)}, u32[]{:S(2)}, u32[]{:S(2)}) collective-permute-start(bf16[3,48,1664]{2,1,0:T(8,128)(2,1)S(1)} %collective-permute-done.14.refs_12_), channel_id=1, source_target_pairs={{0,2},{1,3},{2,0},{3,1},{4,6},{5,7},{6,4},{7,5},{8,10},{9,11},{10,... | collective-permute-start | bytes 1437704 | tf_op jit(solution)/shard_map/ppermute | solution.py:766
  69.2 4.0 %collective-permute-start.13 = (bf16[3,48,1664]{2,1,0:T(8,128)(2,1)}, bf16[3,48,1664]{2,1,0:T(8,128)(2,1)}, u32[]{:S(2)}, u32[]{:S(2)}) collective-permute-start(bf16[3,48,1664]{2,1,0:T(8,128)(2,1)} %collective-permute-done.12.refs_10_), channel_id=1, source_target_pairs={{0,2},{1,3},{2,0},{3,1},{4,6},{5,7},{6,4},{7,5},{8,10},{9,11},{10,... | collective-permute-start | bytes 1437704 | tf_op jit(solution)/shard_map/ppermute | solution.py:766
  69.7 3.5 %collective-permute-start.17 = (bf16[3,48,1664]{2,1,0:T(8,128)(2,1)}, bf16[3,48,1664]{2,1,0:T(8,128)(2,1)}, u32[]{:S(2)}, u32[]{:S(2)}) collective-permute-start(bf16[3,48,1664]{2,1,0:T(8,128)(2,1)} %collective-permute-done.16.refs_14_), channel_id=1, source_target_pairs={{0,2},{1,3},{2,0},{3,1},{4,6},{5,7},{6,4},{7,5},{8,10},{9,11},{10,... | collective-permute-start | bytes 1437704 | tf_op jit(solution)/shard_map/ppermute | solution.py:766
  70.0 3.2 %collective-permute-start.10 = (bf16[1,48,1664]{2,1,0:T(8,128)(2,1)}, bf16[1,48,1664]{2,1,0:T(8,128)(2,1)}, u32[]{:S(2)}, u32[]{:S(2)}) collective-permute-start(bf16[1,48,1664]{2,1,0:T(8,128)(2,1)} %collective-permute-done.9.refs_6_), channel_id=1, source_target_pairs={{0,2},{1,3},{2,0},{3,1},{4,6},{5,7},{6,4},{7,5},{8,10},{9,11},{10,... | collective-permute-start | bytes 479240 | tf_op jit(solution)/shard_map/ppermute | solution.py:766
  78.5 22.5 %collective-permute-start.18 = (bf16[328,768]{1,0:T(8,128)(2,1)S(1)}, bf16[328,768]{1,0:T(8,128)(2,1)S(1)}, u32[]{:S(2)}, u32[]{:S(2)}) collective-permute-start(bf16[328,768]{1,0:T(8,128)(2,1)S(1)} %get-tuple-element.144), channel_id=1, source_target_pairs={{0,1},{1,0},{2,3},{3,2},{4,5},{5,4},{6,7},{7,6},{8,9},{9,8},{10,11... | collective-permute-start | bytes 1511432 | tf_op jit(solution)/shard_map/ppermute | solution.py:766
  123.1 15.7 %collective-permute-start.20 = (bf16[4,2,48,3072]{3,2,1,0:T(8,128)(2,1)}, bf16[4,2,48,3072]{3,2,1,0:T(8,128)(2,1)S(1)}, u32[]{:S(2)}, u32[]{:S(2)}) collective-permute-start(bf16[4,2,48,3072]{3,2,1,0:T(8,128)(2,1)} %get-tuple-element.155), channel_id=1, source_target_pairs={{0,2},{1,3},{2,0},{3,1},{4,6},{5,7},{6,4},{7,5},{8,10},{9,11},{10,... | collective-permute-start | bytes 7077896 | tf_op jit(solution)/shard_map/ppermute | solution.py:766
  123.3 15.5 %collective-permute-start.19 = (bf16[328,768]{1,0:T(8,128)(2,1)}, bf16[328,768]{1,0:T(8,128)(2,1)S(1)}, u32[]{:S(2)}, u32[]{:S(2)}) collective-permute-start(bf16[328,768]{1,0:T(8,128)(2,1)} %get-tuple-element.154), channel_id=1, source_target_pairs={{0,1},{1,0},{2,3},{3,2},{4,5},{5,4},{6,7},{7,6},{8,9},{9,8},{10,11... | collective-permute-start | bytes 1511432 | tf_op jit(solution)/shard_map/ppermute | solution.py:766
  141.0 12.0 %collective-permute-start.21 = (bf16[4,2,48,3072]{3,2,1,0:T(8,128)(2,1)}, bf16[4,2,48,3072]{3,2,1,0:T(8,128)(2,1)S(1)}, u32[]{:S(2)}, u32[]{:S(2)}) collective-permute-start(bf16[4,2,48,3072]{3,2,1,0:T(8,128)(2,1)} %get-tuple-element.168), channel_id=1, source_target_pairs={{0,2},{1,3},{2,0},{3,1},{4,6},{5,7},{6,4},{7,5},{8,10},{9,11},{10,... | collective-permute-start | bytes 7077896 | tf_op jit(solution)/shard_map/ppermute | solution.py:766
  141.2 28.3 %collective-permute-start.23 = (bf16[4,48,1536]{2,1,0:T(8,128)(2,1)}, bf16[4,48,1536]{2,1,0:T(8,128)(2,1)}, u32[]{:S(2)}, u32[]{:S(2)}) collective-permute-start(bf16[4,48,1536]{2,1,0:T(8,128)(2,1)} %get-tuple-element.186), channel_id=1, source_target_pairs={{0,4},{1,5},{2,6},{3,7},{4,0},{5,1},{6,2},{7,3},{8,12},{9,13},{10,... | collective-permute-start | bytes 1769480 | tf_op jit(solution)/shard_map/ppermute | solution.py:766
  141.7 28.2 %collective-permute-start.24 = (bf16[4,48,1536]{2,1,0:T(8,128)(2,1)}, bf16[4,48,1536]{2,1,0:T(8,128)(2,1)}, u32[]{:S(2)}, u32[]{:S(2)}) collective-permute-start(bf16[4,48,1536]{2,1,0:T(8,128)(2,1)} %get-tuple-element.187), channel_id=1, source_target_pairs={{0,1},{1,0},{2,3},{3,2},{4,5},{5,4},{6,7},{7,6},{8,9},{9,8},{10,11... | collective-permute-start | bytes 1769480 | tf_op jit(solution)/shard_map/ppermute | solution.py:766
  142.1 27.9 %collective-permute-start.25 = (bf16[4,48,1536]{2,1,0:T(8,128)(2,1)}, bf16[4,48,1536]{2,1,0:T(8,128)(2,1)}, u32[]{:S(2)}, u32[]{:S(2)}) collective-permute-start(bf16[4,48,1536]{2,1,0:T(8,128)(2,1)} %get-tuple-element.188), channel_id=1, source_target_pairs={{0,5},{1,4},{2,7},{3,6},{4,1},{5,0},{6,3},{7,2},{8,13},{9,12},{10,... | collective-permute-start | bytes 1769480 | tf_op jit(solution)/shard_map/ppermute | solution.py:766
  153.0 14.2 %collective-permute-start.22 = (bf16[4,2,48,768]{3,2,1,0:T(8,128)(2,1)}, bf16[4,2,48,768]{3,2,1,0:T(8,128)(2,1)S(1)}, u32[]{:S(2)}, u32[]{:S(2)}) collective-permute-start(bf16[4,2,48,768]{3,2,1,0:T(8,128)(2,1)} %get-tuple-element.173), channel_id=1, source_target_pairs={{0,2},{1,3},{2,0},{3,1},{4,6},{5,7},{6,4},{7,5},{8,10},{9,11},{10,... | collective-permute-start | bytes 1769480 | tf_op jit(solution)/shard_map/ppermute | solution.py:766
  171.7 17.0 %collective-permute-start.26 = (bf16[2,48,1536]{2,1,0:T(8,128)(2,1)S(1)}, bf16[2,48,1536]{2,1,0:T(8,128)(2,1)S(1)}, u32[]{:S(2)}, u32[]{:S(2)}) collective-permute-start(bf16[2,48,1536]{2,1,0:T(8,128)(2,1)S(1)} %constant_dynamic-slice_fusion.1), channel_id=1, source_target_pairs={{0,16},{1,17},{2,18},{3,19},{4,20},{5,21},{6,22},{7,23},{8,24},{9,... | collective-permute-start | bytes 884744 | tf_op jit(solution)/shard_map/ppermute | solution.py:766
  171.9 31.5 %collective-permute-start.28 = (bf16[4,48,1920]{2,1,0:T(8,128)(2,1)}, bf16[4,48,1920]{2,1,0:T(8,128)(2,1)S(1)}, u32[]{:S(2)}, u32[]{:S(2)}) collective-permute-start(bf16[4,48,1920]{2,1,0:T(8,128)(2,1)} %pad_maximum_fusion.2), channel_id=1, source_target_pairs={{0,4},{1,5},{2,6},{3,7},{4,0},{5,1},{6,2},{7,3},{8,12},{9,13},{10,... | collective-permute-start | bytes 2211848 | tf_op jit(solution)/shard_map/ppermute | solution.py:766
  173.4 30.0 %collective-permute-start.29 = (bf16[4,48,1920]{2,1,0:T(8,128)(2,1)S(1)}, bf16[4,48,1920]{2,1,0:T(8,128)(2,1)S(1)}, u32[]{:S(2)}, u32[]{:S(2)}) collective-permute-start(bf16[4,48,1920]{2,1,0:T(8,128)(2,1)S(1)} %pad_maximum_fusion.3), channel_id=1, source_target_pairs={{0,1},{1,0},{2,3},{3,2},{4,5},{5,4},{6,7},{7,6},{8,9},{9,8},{10,11... | collective-permute-start | bytes 2211848 | tf_op jit(solution)/shard_map/ppermute | solution.py:766
  173.9 32.6 %collective-permute-start.30 = (bf16[4,48,1920]{2,1,0:T(8,128)(2,1)S(1)}, bf16[4,48,1920]{2,1,0:T(8,128)(2,1)S(1)}, u32[]{:S(2)}, u32[]{:S(2)}) collective-permute-start(bf16[4,48,1920]{2,1,0:T(8,128)(2,1)S(1)} %pad_maximum_fusion.4), channel_id=1, source_target_pairs={{0,5},{1,4},{2,7},{3,6},{4,1},{5,0},{6,3},{7,2},{8,13},{9,12},{10,... | collective-permute-start | bytes 2211848 | tf_op jit(solution)/shard_map/ppermute | solution.py:766
  188.8 14.5 %collective-permute-start.27 = (bf16[1,48,1536]{2,1,0:T(8,128)(2,1)S(1)}, bf16[1,48,1536]{2,1,0:T(8,128)(2,1)S(1)}, u32[]{:S(2)}, u32[]{:S(2)}) collective-permute-start(bf16[1,48,1536]{2,1,0:T(8,128)(2,1)S(1)} %constant_dynamic-slice_fusion), channel_id=1, source_target_pairs={{0,8},{1,9},{2,10},{3,11},{4,12},{5,13},{6,14},{7,15},{8,0},{9,1},... | collective-permute-start | bytes 442376 | tf_op jit(solution)/shard_map/ppermute | solution.py:766
  207.4 4.2 %collective-permute-start.31 = (bf16[4,2,48,2560]{3,2,1,0:T(8,128)(2,1)}, bf16[4,2,48,2560]{3,2,1,0:T(8,128)(2,1)S(1)}, u32[]{:S(2)}, u32[]{:S(2)}) collective-permute-start(bf16[4,2,48,2560]{3,2,1,0:T(8,128)(2,1)} %get-tuple-element.226), channel_id=1, source_target_pairs={{0,2},{1,3},{2,0},{3,1},{4,6},{5,7},{6,4},{7,5},{8,10},{9,11},{10,... | collective-permute-start | bytes 5898248 | tf_op jit(solution)/shard_map/ppermute | solution.py:766
  212.3 10.6 %collective-permute-start.35 = (bf16[48,1920]{1,0:T(8,128)(2,1)S(1)}, bf16[48,1920]{1,0:T(8,128)(2,1)S(1)}, u32[]{:S(2)}, u32[]{:S(2)}) collective-permute-start(bf16[48,1920]{1,0:T(8,128)(2,1)S(1)} %get-tuple-element.238), channel_id=1, source_target_pairs={{0,8},{1,9},{2,10},{3,11},{4,12},{5,13},{6,14},{7,15},{8,0},{9,1},... | collective-permute-start | bytes 552968 | tf_op jit(solution)/shard_map/ppermute | solution.py:766
  213.8 16.3 %collective-permute-start.36 = (bf16[48,1920]{1,0:T(8,128)(2,1)S(1)}, bf16[48,1920]{1,0:T(8,128)(2,1)S(1)}, u32[]{:S(2)}, u32[]{:S(2)}) collective-permute-start(bf16[48,1920]{1,0:T(8,128)(2,1)S(1)} %get-tuple-element.239), channel_id=1, source_target_pairs={{0,16},{1,17},{2,18},{3,19},{4,20},{5,21},{6,22},{7,23},{8,24},{9,... | collective-permute-start | bytes 552968 | tf_op jit(solution)/shard_map/ppermute | solution.py:766
  215.0 15.1 %collective-permute-start.37 = (bf16[48,1920]{1,0:T(8,128)(2,1)S(1)}, bf16[48,1920]{1,0:T(8,128)(2,1)S(1)}, u32[]{:S(2)}, u32[]{:S(2)}) collective-permute-start(bf16[48,1920]{1,0:T(8,128)(2,1)S(1)} %get-tuple-element.240), channel_id=1, source_target_pairs={{0,24},{1,25},{2,26},{3,27},{4,28},{5,29},{6,30},{7,31},{8,16},{9,... | collective-permute-start | bytes 552968 | tf_op jit(solution)/shard_map/ppermute | solution.py:766
  216.8 14.2 %collective-permute-start.32 = (bf16[4,48,1280]{2,1,0:T(8,128)(2,1)S(1)}, bf16[4,48,1280]{2,1,0:T(8,128)(2,1)S(1)}, u32[]{:S(2)}, u32[]{:S(2)}) collective-permute-start(bf16[4,48,1280]{2,1,0:T(8,128)(2,1)S(1)} %get-tuple-element.232), channel_id=1, source_target_pairs={{0,4},{1,5},{2,6},{3,7},{4,0},{5,1},{6,2},{7,3},{8,12},{9,13},{10,... | collective-permute-start | bytes 1474568 | tf_op jit(solution)/shard_map/ppermute | solution.py:766
  218.5 23.0 %collective-permute-start.33 = (bf16[4,48,1280]{2,1,0:T(8,128)(2,1)S(1)}, bf16[4,48,1280]{2,1,0:T(8,128)(2,1)S(1)}, u32[]{:S(2)}, u32[]{:S(2)}) collective-permute-start(bf16[4,48,1280]{2,1,0:T(8,128)(2,1)S(1)} %get-tuple-element.233), channel_id=1, source_target_pairs={{0,1},{1,0},{2,3},{3,2},{4,5},{5,4},{6,7},{7,6},{8,9},{9,8},{10,11... | collective-permute-start | bytes 1474568 | tf_op jit(solution)/shard_map/ppermute | solution.py:766
  222.9 18.5 %collective-permute-start.34 = (bf16[4,48,1280]{2,1,0:T(8,128)(2,1)S(1)}, bf16[4,48,1280]{2,1,0:T(8,128)(2,1)S(1)}, u32[]{:S(2)}, u32[]{:S(2)}) collective-permute-start(bf16[4,48,1280]{2,1,0:T(8,128)(2,1)S(1)} %get-tuple-element.234), channel_id=1, source_target_pairs={{0,5},{1,4},{2,7},{3,6},{4,1},{5,0},{6,3},{7,2},{8,13},{9,12},{10,... | collective-permute-start | bytes 1474568 | tf_op jit(solution)/shard_map/ppermute | solution.py:766
  241.8 18.7 %collective-permute-start.39 = (bf16[328,768]{1,0:T(8,128)(2,1)S(1)}, bf16[328,768]{1,0:T(8,128)(2,1)S(1)}, u32[]{:S(2)}, u32[]{:S(2)}) collective-permute-start(bf16[328,768]{1,0:T(8,128)(2,1)S(1)} %copy-done.33), channel_id=1, source_target_pairs={{0,1},{1,0},{2,3},{3,2},{4,5},{5,4},{6,7},{7,6},{8,9},{9,8},{10,11... | collective-permute-start | bytes 1511432 | tf_op jit(solution)/shard_map/ppermute | solution.py:766
  242.3 6.1 %collective-permute-start.40 = (bf16[48,1280]{1,0:T(8,128)(2,1)S(1)}, bf16[48,1280]{1,0:T(8,128)(2,1)S(1)}, u32[]{:S(2)}, u32[]{:S(2)}) collective-permute-start(bf16[48,1280]{1,0:T(8,128)(2,1)S(1)} %get-tuple-element.248), channel_id=1, source_target_pairs={{0,8},{1,9},{2,10},{3,11},{4,12},{5,13},{6,14},{7,15},{8,0},{9,1},... | collective-permute-start | bytes 368648 | tf_op jit(solution)/shard_map/ppermute | solution.py:766
  242.9 10.7 %collective-permute-start.41 = (bf16[48,1280]{1,0:T(8,128)(2,1)S(1)}, bf16[48,1280]{1,0:T(8,128)(2,1)S(1)}, u32[]{:S(2)}, u32[]{:S(2)}) collective-permute-start(bf16[48,1280]{1,0:T(8,128)(2,1)S(1)} %get-tuple-element.249), channel_id=1, source_target_pairs={{0,16},{1,17},{2,18},{3,19},{4,20},{5,21},{6,22},{7,23},{8,24},{9,... | collective-permute-start | bytes 368648 | tf_op jit(solution)/shard_map/ppermute | solution.py:766
  245.3 8.3 %collective-permute-start.42 = (bf16[48,1280]{1,0:T(8,128)(2,1)S(1)}, bf16[48,1280]{1,0:T(8,128)(2,1)S(1)}, u32[]{:S(2)}, u32[]{:S(2)}) collective-permute-start(bf16[48,1280]{1,0:T(8,128)(2,1)S(1)} %get-tuple-element.250), channel_id=1, source_target_pairs={{0,24},{1,25},{2,26},{3,27},{4,28},{5,29},{6,30},{7,31},{8,16},{9,... | collective-permute-start | bytes 368648 | tf_op jit(solution)/shard_map/ppermute | solution.py:766
  246.8 13.6 %collective-permute-start.38 = (bf16[48,3456]{1,0:T(8,128)(2,1)S(1)}, bf16[48,3456]{1,0:T(8,128)(2,1)S(1)}, u32[]{:S(2)}, u32[]{:S(2)}) collective-permute-start(bf16[48,3456]{1,0:T(8,128)(2,1)S(1)} %pad_maximum_fusion.7), channel_id=1, source_target_pairs={{0,1},{1,0},{2,3},{3,2},{4,5},{5,4},{6,7},{7,6},{8,9},{9,8},{10,11... | collective-permute-start | bytes 995336 | tf_op jit(solution)/shard_map/ppermute | solution.py:766
  260.6 5.7 %collective-permute-start.43 = (bf16[48,1280]{1,0:T(8,128)(2,1)S(1)}, bf16[48,1280]{1,0:T(8,128)(2,1)S(1)}, u32[]{:S(2)}, u32[]{:S(2)}) collective-permute-start(bf16[48,1280]{1,0:T(8,128)(2,1)S(1)} %add_convert_fusion.10), channel_id=1, source_target_pairs={{0,1},{1,0},{2,3},{3,2},{4,5},{5,4},{6,7},{7,6},{8,9},{9,8},{10,11... | collective-permute-start | bytes 368648 | tf_op jit(solution)/shard_map/ppermute | solution.py:766
  (32 other events, 226.2 us)
Sparse Core Ops, SparseCore 0:
  10.9 89.8 all-gather.1
